TPU v7x, 32 devices: a whole 2x2x4 slice. The times are simulated.
32 devices in a mesh: members: 2 (over x), tiles: 16 (over z, y, core).
Axes of the slice: x: 2, y: 2, z: 4, core: 2. Of those that a mesh axis runs over, the one named last changes fastest.
Arguments:
- atm_state: float32 [256, 3072], P(('members', 'tiles')), parts along dimension 0, may hold values from -6 to 6
- atm_kappa: float32 [3072], replicated, may hold values from 0.05 to 0.2
- forcing: bfloat16 [8, 256, 3072], P(None, ('members', 'tiles')), parts along dimension 1, may hold values from -6 to 6
- flux_gain: float32 [8], replicated, may hold values from 0.5 to 1.5
- remap_weight: bfloat16 [4096, 128, 128], P('tiles'), may hold values from -0.5 to 0.5
- remap_source: int32 [4096], P('tiles'), may hold values from 0 to 191
- remap_owner: int32 [4096, 1], P('tiles'), may hold values from 0 to 15; in each aligned block of 256 rows (0 to 255, 256 to 511, ...) at most 32 rows name the same one
- remap_dest: int32 [4096], P('tiles'), may hold values from 0 to 447
- ocean_state: float32 [512, 3584], P(('members', 'tiles')), parts along dimension 0, may hold values from -6 to 6
- ocean_nu: float32 [3584], replicated, may hold values from 0.05 to 0.2
- flux_coef: float32 [8], replicated, may hold values from 0.05 to 0.3
Outputs:
- atm_next: float32 [256, 3072], P(('members', 'tiles')), parts along dimension 0
- ocean_next: float32 [512, 3584], P(('members', 'tiles')), parts along dimension 0
- atm_feedback: float32 [256, 3072], P(('members', 'tiles')), parts along dimension 0
There are 2 independent parts, one for each index of `members`. A program takes and returns all parts, laid end to end along the dimension named above; an argument that names none is the same for every part. Nothing has to cross between parts.
Inputs may be any that keep to these rules, and one draw needn't show every extreme that they name: `remap_owner`: among the 256 blocks of one device no owner is named more than 32 times, a bound that some block reaches.
All inputs are finite; a program needn't handle non-finite values.
Results may differ from a plain program's by a relative error of at most 0.0085.
Values may be sent and summed in bfloat16 or wider, within the bound.
No kernel may reach another device: no remote copies, remote signals or barrier semaphores. Data moves between devices by JAX's collectives and lax.ppermute only.
A program may use at most 64 MiB of HBM per device.

v0:
```python
import jax
import jax.numpy as jnp
from jax import lax
from jax.sharding import PartitionSpec as P

NFLUX = 8
TILE = 128


def with_halo(x, sides, width, wrap):
    for axis, dim in sides:
        devices, length = (lax.axis_size(axis), x.shape[dim])
        up = [(i, (i + 1) % devices) for i in range(devices if wrap else devices - 1)]
        down = [(j, i) for i, j in up]
        last = lax.slice_in_dim(x, length - width, length, axis=dim)
        first = lax.slice_in_dim(x, 0, width, axis=dim)
        before = lax.ppermute(last, axis, up)
        after = lax.ppermute(first, axis, down)
        x = jnp.concatenate([before, x, after], axis=dim)
    return x


def atm_update(padded, kappa_row):
    center = padded[1:-1]
    laplace = (
        padded[:-2] + padded[2:] + jnp.roll(center, 1, 1) + jnp.roll(center, -1, 1) - 4.0 * center
    )
    return center + kappa_row * laplace


def per_device(
    atm_state,
    atm_kappa,
    forcing,
    flux_gain,
    remap_weight,
    remap_source,
    remap_owner,
    remap_dest,
    ocean_state,
    ocean_nu,
    flux_coef,
):
    ntiles = lax.axis_size("tiles")
    blocks = remap_source.shape[0]
    capacity = max(2, 2 * blocks // ntiles)
    n_slots = ntiles * capacity
    kappa_row = atm_kappa[None, :]
    atm_rows, atm_cols = atm_state.shape
    ocean_rows, ocean_cols = ocean_state.shape
    atm_tiles = atm_rows * atm_cols // TILE
    ocean_tiles = ocean_rows * ocean_cols // TILE
    atmos = atm_state
    for section in range(2):
        atmos = atm_update(with_halo(atmos, (("tiles", 0),), 1, True), kappa_row)
    fluxes = (forcing.astype(jnp.float32) + flux_gain[:, None, None] * atmos[None]).astype(
        jnp.bfloat16
    )
    flux_tiles = fluxes.reshape(NFLUX, atm_tiles, TILE)
    pieces = jnp.take(flux_tiles, remap_source, axis=1)
    owners = remap_owner[:, 0]
    matches = (owners[:, None] == jnp.arange(ntiles, dtype=jnp.int32)[None, :]).astype(jnp.int32)
    before = jnp.cumsum(matches, axis=0) - matches
    ranks = jnp.sum(before * matches, axis=1)
    slot_of = owners * capacity + ranks
    dest_slots = jnp.full((n_slots,), -1, jnp.int32).at[slot_of].set(remap_dest)
    contribution = jnp.einsum(
        "kbi,bij->bkj", pieces, remap_weight, preferred_element_type=jnp.float32
    )
    outgoing = jnp.zeros((n_slots, NFLUX, TILE), jnp.float32).at[slot_of].set(contribution)
    arrived, in_dest = (
        lax.all_to_all(outgoing, "tiles", split_axis=0, concat_axis=0, tiled=True),
        lax.all_to_all(dest_slots, "tiles", split_axis=0, concat_axis=0, tiled=True),
    )
    select = (in_dest[None, :] == jnp.arange(ocean_tiles, dtype=jnp.int32)[:, None]).astype(
        jnp.float32
    )
    summed = jnp.dot(
        select, arrived.reshape(n_slots, NFLUX * TILE), precision=lax.Precision.HIGHEST
    )
    flux_field = (
        summed.reshape(ocean_tiles, NFLUX, TILE)
        .transpose(1, 0, 2)
        .reshape(NFLUX, ocean_rows, ocean_cols)
    )
    drive_sum = jnp.tensordot(flux_coef, flux_field, axes=1)
    at_top = lax.axis_index("tiles") == ntiles - 1
    nu_row = ocean_nu[None, :]
    ocean = ocean_state
    for section in range(2):
        padded = with_halo(ocean, (("tiles", 0),), 1, False)
        ghost_row = jnp.where(at_top, ocean[-1, ::-1], padded[-1])
        upper = jnp.concatenate([padded[2:-1], ghost_row[None, :]], 0)
        lower = padded[:-2]
        laplace = lower + upper + jnp.roll(ocean, 1, 1) + jnp.roll(ocean, -1, 1) - 4.0 * ocean
        ocean = ocean + nu_row * laplace + drive_sum
    returned = jnp.dot(
        select.T, ocean.reshape(ocean_tiles, TILE), precision=lax.Precision.HIGHEST
    ).astype(jnp.bfloat16)
    came_back = lax.all_to_all(returned, "tiles", split_axis=0, concat_axis=0, tiled=True)
    own_rows = jnp.take(came_back, slot_of, axis=0)
    back_values = jnp.einsum(
        "bij,bj->bi", remap_weight, own_rows, preferred_element_type=jnp.float32
    )
    source_select = (
        remap_source[None, :] == jnp.arange(atm_tiles, dtype=jnp.int32)[:, None]
    ).astype(jnp.float32)
    feedback = jnp.dot(source_select, back_values, precision=lax.Precision.HIGHEST).reshape(
        atm_rows, atm_cols
    )
    return (atmos, ocean, feedback)


def solution(mesh):
    return jax.shard_map(
        per_device,
        mesh=mesh,
        in_specs=(
            P(("members", "tiles"), None),
            P(),
            P(None, ("members", "tiles"), None),
            P(),
            P("tiles", None, None),
            P("tiles"),
            P("tiles", None),
            P("tiles"),
            P(("members", "tiles"), None),
            P(),
            P(),
        ),
        out_specs=(
            P(("members", "tiles"), None),
            P(("members", "tiles"), None),
            P(("members", "tiles"), None),
        ),
        check_vma=False,
    )
```

profile of v0, /device:TPU:0, one launch (start us, length us, event | category | flops | bytes accessed | tf_op | source)
XLA Modules:
  0.0 153.3 jit_solution(17070424844199859272)
XLA Ops:
  0.6 0.0 copy-start
  0.7 1.0 fusion.66
  1.7 0.5 collective-permute-start
  2.2 5.1 %collective-permute-start.1 = (f32[1,3072]{1,0:T(1,128)S(1)}, f32[1,3072]{1,0:T(1,128)S(1)}, u32[]{:S(2)}, u32[]{:S(2)}) collective-permute-start(f32[1,3072]{1,0:T(1,128)S(1)} %get-tuple-element.28), channel_id=1, source_target_pairs={{1,0},{2,1},{3,2},{4,3},{5,4},{6,5},{7,6},{8,7},{9,8},{10,9},{11,1... | collective-permute-start | bytes 36872 | tf_op jit(solution)/shard_map/ppermute | solution.py:18
  7.2 0.7 fusion.49
  7.9 0.6 reduce-window.6
  8.5 0.2 slice_reduce_fusion
  8.7 0.8 fusion.48
  9.5 0.7 and_reduce_fusion
  10.2 1.6 %scatter_custom_fusion = s32[512]{0:T(512)S(1)} fusion(s32[256]{0:T(256)S(1)} %bitcast.69, s32[256]{0:T(256)} %param.18, s32[]{:T(128)} %constant.26.clone.1), kind=kCustom, calls=%fused_computation.75 | custom fusion | bytes 2560 | tf_op jit(solution)/shard_map/scatter | solution.py:66
  11.7 0.7 all_to_all.17
  12.4 3.6 %all-to-all-start = ((s32[16,32,1]{1,2,0:T(1,128)}), s32[16,32,1]{1,2,0:T(1,128)S(1)}, u32[]{:S(2)}, u32[]{:S(2)}) async-start(s32[16,32,1]{1,2,0:T(1,128)} %bitcast.5), calls=%async_computation | async-start | bytes 16384 | tf_op jit(solution)/shard_map/all_to_all | solution.py:73
  16.1 1.1 fusion.64
  17.1 0.8 fusion.65
  17.9 0.7 compare_select_fusion.1
  18.6 0.7 compare_and_fusion
  19.3 1.2 fusion.44
  20.4 0.1 fusion.61
  20.6 0.5 collective-permute-start.2
  21.0 4.0 %collective-permute-start.3 = (f32[1,3072]{1,0:T(1,128)S(1)}, f32[1,3072]{1,0:T(1,128)S(1)}, u32[]{:S(2)}, u32[]{:S(2)}) collective-permute-start(f32[1,3072]{1,0:T(1,128)S(1)} %get-tuple-element.22), channel_id=1, source_target_pairs={{1,0},{2,1},{3,2},{4,3},{5,4},{6,5},{7,6},{8,7},{9,8},{10,9},{11,1... | collective-permute-start | bytes 36872 | tf_op jit(solution)/shard_map/ppermute | solution.py:18
  25.1 0.1 fusion.62
  25.1 1.3 collective-permute-done.2
  26.4 0.0 collective-permute-done.3
  26.5 0.8 fusion.38
  27.3 0.0 copy-start.4
  27.3 0.8 add_convert_fusion
  28.1 0.2 reshape.62
  28.3 0.3 copy.21
  28.6 0.8 gather_fusion
  29.4 4.7 %fusion.9 = f32[256,8,128]{2,1,0:T(8,128)S(1)} fusion(bf16[256,128,128]{2,1,0:T(8,128)(2,1)} %param.15, bf16[256,8,128]{2,1,0:T(8,128)(2,1)S(1)} %gather_fusion, pred[256]{0:T(512)(128)(4,1)S(1)} %compare_and_fusion), kind=kOutput, calls=%fused_computation.13 | convolution fusion | flops 67371008 | bytes 9961728 | tf_op jit(solution)/shard_map/kbi,bij->bkj/dot_general | solution.py:67
  34.2 1.5 broadcast_in_dim.42
  35.6 23.9 %scatter_fusion = f32[512,8,128]{2,1,0:T(8,128)} fusion(f32[512,8,128]{2,1,0:T(8,128)} %broadcast_in_dim.42, s32[256]{0:T(256)S(1)} %bitcast.70, f32[256,8,128]{2,1,0:T(8,128)S(1)} %fusion.9), kind=kCustom, calls=%fused_computation.3 | custom fusion | bytes 3146752 | tf_op jit(solution)/shard_map/scatter | solution.py:70
  59.6 5.9 %all-to-all-start.1 = ((f32[512,8,128]{2,1,0:T(8,128)}), f32[512,8,128]{2,1,0:T(8,128)S(1)}, u32[]{:S(2)}, u32[]{:S(2)}) async-start(f32[512,8,128]{2,1,0:T(8,128)} %scatter_fusion), calls=%async_computation.1 | async-start | bytes 4194304 | tf_op jit(solution)/shard_map/all_to_all | solution.py:72
  65.5 1.3 collective-permute-start.5
  66.8 3.0 %collective-permute-start.4 = (f32[1,3584]{1,0:T(1,128)S(1)}, f32[1,3584]{1,0:T(1,128)S(1)}, u32[]{:S(2)}, u32[]{:S(2)}) collective-permute-start(f32[1,3584]{1,0:T(1,128)S(1)} %get-tuple-element.16), channel_id=1, source_target_pairs={{0,1},{1,2},{2,3},{3,4},{4,5},{5,6},{6,7},{7,8},{8,9},{9,10},{10,1... | collective-permute-start | bytes 43016 | tf_op jit(solution)/shard_map/ppermute | solution.py:17
  69.9 0.1 fusion.58
  70.0 0.1 fusion.59
  70.1 2.4 %rev.6 = f32[1,3584]{1,0:T(1,128)S(1)} reverse(f32[1,3584]{1,0:T(1,128)S(1)} %get-tuple-element.16), dimensions={1} | reverse | bytes 28672 | tf_op jit(solution)/shard_map/rev | solution.py:92
  72.6 0.5 broadcast.92
  73.1 0.7 reduce.7
  73.8 0.1 eq.65
  73.9 32.8 %all-to-all-done.1 = f32[512,8,128]{2,1,0:T(8,128)S(1)} async-done(((f32[512,8,128]{2,1,0:T(8,128)}), f32[512,8,128]{2,1,0:T(8,128)S(1)}, u32[]{:S(2)}, u32[]{:S(2)}) %all-to-all-start.1) | async-done | bytes 2097184 | tf_op jit(solution)/shard_map/all_to_all | solution.py:72
  106.6 1.9 %copy.27 = f32[512,8,128]{0,2,1:T(8,128)} copy(f32[512,8,128]{2,1,0:T(8,128)S(1)} %all-to-all-done.1) | data formatting | bytes 4194304 | tf_op jit(solution)/shard_map/reshape | solution.py:79
  108.5 3.4 %fusion.4 = bf16[8,448,128]{2,1,0:T(8,128)(2,1)S(1)} fusion(f32[512,8,128]{0,2,1:T(8,128)} %copy.27, s32[512]{0:T(512)S(1)} %eq.65), kind=kOutput, calls=%fused_computation.8 | convolution fusion | flops 2818801664 | bytes 3016704 | tf_op jit(solution)/shard_map/dot_general | solution.py:78
  111.9 0.0 copy-start.5
  111.9 1.0 reshape.64
  112.9 0.7 fusion.2
  113.6 0.1 fusion.29
  113.8 0.1 fusion.55
  113.9 1.3 collective-permute-start.7
  115.2 0.1 fusion.56
  115.3 3.3 %collective-permute-start.6 = (f32[1,3584]{1,0:T(1,128)S(1)}, f32[1,3584]{1,0:T(1,128)S(1)}, u32[]{:S(2)}, u32[]{:S(2)}) collective-permute-start(f32[1,3584]{1,0:T(1,128)S(1)} %get-tuple-element.10), channel_id=1, source_target_pairs={{0,1},{1,2},{2,3},{3,4},{4,5},{5,6},{6,7},{7,8},{8,9},{9,10},{10,1... | collective-permute-start | bytes 43016 | tf_op jit(solution)/shard_map/ppermute | solution.py:17
  118.6 2.5 %rev.7 = f32[1,3584]{1,0:T(1,128)S(1)} reverse(f32[1,3584]{1,0:T(1,128)S(1)} %get-tuple-element.10), dimensions={1} | reverse | bytes 28672 | tf_op jit(solution)/shard_map/rev | solution.py:92
  121.1 0.1 fusion.22
  121.3 0.0 copy-start.2
  121.3 1.7 %convolution_convert_fusion = bf16[512,128]{1,0:T(8,128)(2,1)} fusion(f32[448,128]{1,0:T(8,128)S(1)} %reshape.65, s32[512]{0:T(512)S(1)} %eq.65), kind=kOutput, calls=%fused_computation.9 | convolution fusion | flops 352616448 | bytes 362496 | tf_op jit(solution)/shard_map/dot_general | solution.py:97
  123.0 12.6 %all-to-all-start.2 = ((bf16[16,32,128]{2,1,0:T(8,128)(2,1)}), bf16[16,32,128]{2,1,0:T(8,128)(2,1)S(1)}, u32[]{:S(2)}, u32[]{:S(2)}) async-start(bf16[16,32,128]{2,1,0:T(8,128)(2,1)} %bitcast.14), calls=%async_computation.2 | async-start | bytes 262144 | tf_op jit(solution)/shard_map/all_to_all | solution.py:100
  135.6 7.9 %all-to-all-done.2 = bf16[16,32,128]{2,1,0:T(8,128)(2,1)S(1)} async-done(((bf16[16,32,128]{2,1,0:T(8,128)(2,1)}), bf16[16,32,128]{2,1,0:T(8,128)(2,1)S(1)}, u32[]{:S(2)}, u32[]{:S(2)}) %all-to-all-start.2) | async-done | bytes 131104 | tf_op jit(solution)/shard_map/all_to_all | solution.py:100
  143.6 0.9 gather_fusion.1
  144.4 0.1 select_bitcast_fusion
  144.5 0.0 copy-start.6
  144.5 7.8 %fusion.31 = f32[256,1,128]{2,1,0:T(1,128)S(1)} fusion(bf16[256,128,128]{2,1,0:T(8,128)(2,1)} %param.15, bf16[256,128,1]{1,0,2:T(8,128)(2,1)S(1)} %select_bitcast_fusion), kind=kOutput, calls=%fused_computation.38 | convolution fusion | flops 8388608 | bytes 8585216 | tf_op jit(solution)/shard_map/bij,bj->bi/dot_general | solution.py:102
  152.3 0.3 fusion.30
  152.6 0.7 reshape.66
  (28 shorter events, 0.2 us)
Async XLA Ops:
  0.6 112.3 %copy-start = (f32[8]{0:T(128)S(1)}, f32[8]{0:T(128)}, u32[]{:S(2)}) copy-start(f32[8]{0:T(128)} %param.21) | copy-start | bytes 100
  0.6 26.6 %copy-start.3 = (bf16[8,8,3072]{2,1,0:T(8,128)(2,1)S(1)}, bf16[8,8,3072]{2,1,0:T(8,128)(2,1)}, u32[]{:S(2)}) copy-start(bf16[8,8,3072]{2,1,0:T(8,128)(2,1)} %param.13) | copy-start | bytes 1179652
  1.7 17.6 %collective-permute-start = (f32[1,3072]{1,0:T(1,128)S(1)}, f32[1,3072]{1,0:T(1,128)S(1)}, u32[]{:S(2)}, u32[]{:S(2)}) collective-permute-start(f32[1,3072]{1,0:T(1,128)S(1)} %get-tuple-element.27), channel_id=1, source_target_pairs={{0,1},{1,2},{2,3},{3,4},{4,5},{5,6},{6,7},{7,8},{8,9},{9,10},{10,1... | collective-permute-start | bytes 36872 | tf_op jit(solution)/shard_map/ppermute | solution.py:17
  2.2 17.1 %collective-permute-start.1 = (f32[1,3072]{1,0:T(1,128)S(1)}, f32[1,3072]{1,0:T(1,128)S(1)}, u32[]{:S(2)}, u32[]{:S(2)}) collective-permute-start(f32[1,3072]{1,0:T(1,128)S(1)} %get-tuple-element.28), channel_id=1, source_target_pairs={{1,0},{2,1},{3,2},{4,3},{5,4},{6,5},{7,6},{8,7},{9,8},{10,9},{11,1... | collective-permute-start | bytes 36872 | tf_op jit(solution)/shard_map/ppermute | solution.py:18
  12.4 47.1 %all-to-all-start = ((s32[16,32,1]{1,2,0:T(1,128)}), s32[16,32,1]{1,2,0:T(1,128)S(1)}, u32[]{:S(2)}, u32[]{:S(2)}) async-start(s32[16,32,1]{1,2,0:T(1,128)} %bitcast.5), calls=%async_computation | async-start | bytes 16384 | tf_op jit(solution)/shard_map/all_to_all | solution.py:73
  20.6 5.9 %collective-permute-start.2 = (f32[1,3072]{1,0:T(1,128)S(1)}, f32[1,3072]{1,0:T(1,128)S(1)}, u32[]{:S(2)}, u32[]{:S(2)}) collective-permute-start(f32[1,3072]{1,0:T(1,128)S(1)} %get-tuple-element.21), channel_id=1, source_target_pairs={{0,1},{1,2},{2,3},{3,4},{4,5},{5,6},{6,7},{7,8},{8,9},{9,10},{10,1... | collective-permute-start | bytes 36872 | tf_op jit(solution)/shard_map/ppermute | solution.py:17
  21.0 5.4 %collective-permute-start.3 = (f32[1,3072]{1,0:T(1,128)S(1)}, f32[1,3072]{1,0:T(1,128)S(1)}, u32[]{:S(2)}, u32[]{:S(2)}) collective-permute-start(f32[1,3072]{1,0:T(1,128)S(1)} %get-tuple-element.22), channel_id=1, source_target_pairs={{1,0},{2,1},{3,2},{4,3},{5,4},{6,5},{7,6},{8,7},{9,8},{10,9},{11,1... | collective-permute-start | bytes 36872 | tf_op jit(solution)/shard_map/ppermute | solution.py:18
  27.3 6.9 %copy-start.4 = (f32[8,3072]{1,0:T(8,128)}, f32[8,3072]{1,0:T(8,128)S(1)}, u32[]{:S(2)}) copy-start(f32[8,3072]{1,0:T(8,128)S(1)} %fusion.38) | copy-start | bytes 294916
  59.5 6.0 %copy-start.1 = (f32[16,3584]{1,0:T(8,128)S(1)}, f32[16,3584]{1,0:T(8,128)}, u32[]{:S(2)}) copy-start(f32[16,3584]{1,0:T(8,128)} %param.19) | copy-start | bytes 688132
  59.6 47.1 %all-to-all-start.1 = ((f32[512,8,128]{2,1,0:T(8,128)}), f32[512,8,128]{2,1,0:T(8,128)S(1)}, u32[]{:S(2)}, u32[]{:S(2)}) async-start(f32[512,8,128]{2,1,0:T(8,128)} %scatter_fusion), calls=%async_computation.1 | async-start | bytes 4194304 | tf_op jit(solution)/shard_map/all_to_all | solution.py:72
  65.5 8.3 %collective-permute-start.5 = (f32[1,3584]{1,0:T(1,128)S(1)}, f32[1,3584]{1,0:T(1,128)S(1)}, u32[]{:S(2)}, u32[]{:S(2)}) collective-permute-start(f32[1,3584]{1,0:T(1,128)S(1)} %get-tuple-element.15), channel_id=1, source_target_pairs={{1,0},{2,1},{3,2},{4,3},{5,4},{6,5},{7,6},{8,7},{9,8},{10,9},{11,1... | collective-permute-start | bytes 43016 | tf_op jit(solution)/shard_map/ppermute | solution.py:18
  66.8 46.7 %collective-permute-start.4 = (f32[1,3584]{1,0:T(1,128)S(1)}, f32[1,3584]{1,0:T(1,128)S(1)}, u32[]{:S(2)}, u32[]{:S(2)}) collective-permute-start(f32[1,3584]{1,0:T(1,128)S(1)} %get-tuple-element.16), channel_id=1, source_target_pairs={{0,1},{1,2},{2,3},{3,4},{4,5},{5,6},{6,7},{7,8},{8,9},{9,10},{10,1... | collective-permute-start | bytes 43016 | tf_op jit(solution)/shard_map/ppermute | solution.py:17
  111.9 1.7 %copy-start.5 = (f32[3584]{0:T(1024)S(1)}, f32[3584]{0:T(1024)}, u32[]{:S(2)}) copy-start(f32[3584]{0:T(1024)} %param.20) | copy-start | bytes 43012
  113.9 7.2 %collective-permute-start.7 = (f32[1,3584]{1,0:T(1,128)S(1)}, f32[1,3584]{1,0:T(1,128)S(1)}, u32[]{:S(2)}, u32[]{:S(2)}) collective-permute-start(f32[1,3584]{1,0:T(1,128)S(1)} %get-tuple-element.9), channel_id=1, source_target_pairs={{1,0},{2,1},{3,2},{4,3},{5,4},{6,5},{7,6},{8,7},{9,8},{10,9},{11,1... | collective-permute-start | bytes 43016 | tf_op jit(solution)/shard_map/ppermute | solution.py:18
  115.3 5.8 %collective-permute-start.6 = (f32[1,3584]{1,0:T(1,128)S(1)}, f32[1,3584]{1,0:T(1,128)S(1)}, u32[]{:S(2)}, u32[]{:S(2)}) collective-permute-start(f32[1,3584]{1,0:T(1,128)S(1)} %get-tuple-element.10), channel_id=1, source_target_pairs={{0,1},{1,2},{2,3},{3,4},{4,5},{5,6},{6,7},{7,8},{8,9},{9,10},{10,1... | collective-permute-start | bytes 43016 | tf_op jit(solution)/shard_map/ppermute | solution.py:17
  121.3 31.1 %copy-start.2 = (f32[16,3584]{1,0:T(8,128)}, f32[16,3584]{1,0:T(8,128)S(1)}, u32[]{:S(2)}) copy-start(f32[16,3584]{1,0:T(8,128)S(1)} %fusion.22) | copy-start | bytes 688132
  123.0 20.5 %all-to-all-start.2 = ((bf16[16,32,128]{2,1,0:T(8,128)(2,1)}), bf16[16,32,128]{2,1,0:T(8,128)(2,1)S(1)}, u32[]{:S(2)}, u32[]{:S(2)}) async-start(bf16[16,32,128]{2,1,0:T(8,128)(2,1)} %bitcast.14), calls=%async_computation.2 | async-start | bytes 262144 | tf_op jit(solution)/shard_map/all_to_all | solution.py:100
  144.5 7.8 %copy-start.6 = (s32[256]{0:T(256)S(1)}, s32[256]{0:T(256)}, u32[]{:S(2)}) copy-start(s32[256]{0:T(256)} %param.16) | copy-start | bytes 3076
where the time goes:
time: 155 us; the launch traced here: 153 us
  local copies, waits for them, and re-layouts  42.5 us (27%)
  waiting for transfers between devices  42 us (27%)
  starting transfers between devices  41.1 us (27%)
  matrix products  18.5 us (12%)
  other arithmetic  8.04 us (5%)
    all_to_all x1, waiting for transfers between devices, per_device(): lax.all_to_all(outgoing, 'tiles', split_axis=0, concat_axis=0, tiled=True)  32.8 us
    scatter x1, local copies, waits for them, and re-layouts, per_device(): jnp.zeros((n_slots, NFLUX, TILE), jnp.float32).at[slot_of].set(contribution)  23.9 us
    all_to_all x1, starting transfers between devices, per_device(): lax.all_to_all(returned, 'tiles', split_axis=0, concat_axis=0, tiled=True)  12.6 us
    ppermute x4, starting transfers between devices, with_halo(): after = lax.ppermute(first, axis, down)  11.7 us
    all_to_all x1, waiting for transfers between devices, per_device(): lax.all_to_all(returned, 'tiles', split_axis=0, concat_axis=0, tiled=True)  7.92 us
    dot_general x1, matrix products, per_device(): jnp.einsum('bij,bj->bi', remap_weight, own_rows, preferred_element_type=j...  7.78 us
    ppermute x4, starting transfers between devices, with_halo(): before = lax.ppermute(last, axis, up)  7.29 us
    all_to_all x1, starting transfers between devices, per_device(): lax.all_to_all(outgoing, 'tiles', split_axis=0, concat_axis=0, tiled=True)  5.95 us
  transfers between devices with their start and end apart: 11, of which 3 were waited for; matrix products, arithmetic and copies ran while one was open for 36% of the time, Pallas kernels for 0%

commit v1 on v0

v1 whole, which is shorter than its diff:
```python
import functools

import jax
import jax.numpy as jnp
from jax import lax
from jax.experimental import pallas as pl
from jax.experimental.pallas import tpu as pltpu
from jax.sharding import PartitionSpec as P

LANE = 128
EDGE = 32
CHUNK = 8
F32 = jnp.float32
BF16 = jnp.bfloat16
VMEM = pl.BlockSpec(memory_space=pltpu.VMEM)
SMEM = pl.BlockSpec(memory_space=pltpu.SMEM)


def iota(shape, dim):
    return lax.broadcasted_iota(jnp.int32, shape, dim)


def dot(a, b):
    return lax.dot_general(a, b, (((1,), (0,)), ((), ())), preferred_element_type=F32)


def dot_nt(a, b):
    return lax.dot_general(a, b, (((1,), (1,)), ((), ())), preferred_element_type=F32)


def onehot(mask):
    return jnp.where(mask, 1.0, 0.0).astype(BF16)


def routing_kernel(
    ntiles, main, ocean_rows, row_tiles, me_ref, src_col, src_row, own_col, own_row, dst_row,
    pick_ref, back_ref, slots_ref, sort_ref, ids_ref,
):
    blocks = own_row.shape[1]
    rows = main + 2 * EDGE
    per_lane = LANE // main
    owner = own_row[...]
    row_of, col_of = dst_row[...] // row_tiles, dst_row[...] % row_tiles
    owner_c = own_col[...]
    match_c = owner_c == iota((blocks, LANE), 1)
    below = onehot(iota((blocks, blocks), 1) < iota((blocks, blocks), 0))
    rank_c = jnp.sum(
        jnp.where(match_c, dot(below, onehot(match_c)), 0.0), axis=1, keepdims=True
    ).astype(jnp.int32)
    match_r = owner == iota((ntiles, blocks), 0)
    above = onehot(iota((blocks, blocks), 0) < iota((blocks, blocks), 1))
    rank_r = jnp.sum(
        jnp.where(match_r, dot(onehot(match_r), above), 0.0), axis=0, keepdims=True
    ).astype(jnp.int32)
    pick_ref[...] = onehot(src_col[...] == iota(pick_ref.shape, 1))
    back_ref[...] = onehot(src_row[...] == iota(back_ref.shape, 0))
    sort_ref[...] = onehot(owner_c * main + rank_c == iota(sort_ref.shape, 1))
    own_slot = owner * rows + rank_r
    low = (row_of == ocean_rows - 1) & (owner < ntiles - 1)
    low_slot = jnp.where(low, (owner + 1) * rows + main + col_of, -1)
    high = (row_of == 0) & (owner > 0)
    high_slot = jnp.where(high, (owner - 1) * rows + main + EDGE + col_of, -1)
    for t in range(ntiles):
        slot = iota((rows, blocks), 0) + t * rows
        slots_ref[pl.ds(t * rows, rows), :] = onehot(
            (slot == own_slot) | (slot == low_slot) | (slot == high_slot)
        )
    lane_of = rank_c + (me_ref[0] % per_lane) * main
    place = onehot(lane_of == iota((blocks, LANE), 1))
    ids_ref[0] = dot(jnp.where(match_r, (col_of + 1).astype(F32), 0.0).astype(BF16), place)
    ids_ref[1] = dot(jnp.where(match_r, row_of.astype(F32), 0.0).astype(BF16), place)


def forward_kernel(
    ntiles, main, me_ref, gain_ref, coef_ref, atm_ref, kappa_ref, even_ref, odd_ref, forcing_ref,
    pick_ref, slots_ref, ids_ref, weight_ref, next_ref, out_ref, work,
):
    atm_rows, cols = atm_ref.shape
    rows = main + 2 * EDGE
    even = me_ref[0] % 2 == 0
    ev, od = even_ref[:, :cols], odd_ref[:, :cols]
    size = 2 * atm_rows
    work[0:atm_rows] = atm_ref[...]
    work[atm_rows : 2 * atm_rows] = jnp.zeros((atm_rows, cols), F32)
    work[size - 2 : size] = jnp.where(even, od, ev)
    work[atm_rows : atm_rows + 2] = jnp.where(even, ev, od)
    x = work[...]
    kappa = kappa_ref[...]
    for _ in range(2):
        near = (
            pltpu.roll(x, 1, 0) + pltpu.roll(x, size - 1, 0)
            + pltpu.roll(x, 1, 1) + pltpu.roll(x, cols - 1, 1)
        )
        x = x + kappa * (near - 4.0 * x)
    atm = x[:atm_rows]
    next_ref[...] = atm
    nflux = forcing_ref.shape[0]
    scale = coef_ref[0] * gain_ref[0]
    for k in range(1, nflux):
        scale = scale + coef_ref[k] * gain_ref[k]
    field = scale * atm
    for k in range(nflux):
        field = field + coef_ref[k] * forcing_ref[k].astype(F32)
    tiles = jnp.concatenate(
        [field[:, c * LANE : (c + 1) * LANE] for c in range(cols // LANE)], axis=0
    ).astype(BF16)
    pieces = dot(pick_ref[...], tiles)
    blocks = pieces.shape[0]
    row = iota((CHUNK, LANE), 0)
    parts = []
    for n in range(blocks // CHUNK):
        piece = pieces[n * CHUNK : (n + 1) * CHUNK]
        spread = jnp.concatenate(
            [jnp.where(row == q, piece, 0.0) for q in range(CHUNK)], axis=1
        ).astype(BF16)
        weight = weight_ref[pl.ds(n * CHUNK, CHUNK)].reshape(CHUNK * LANE, LANE)
        parts.append(dot(spread, weight))
    contribution = jnp.concatenate(parts, axis=0).astype(BF16)
    at = iota((EDGE, LANE), 0)
    for t in range(ntiles):
        sent = dot(slots_ref[pl.ds(t * rows, rows), :], contribution)
        low = sent[main : main + EDGE]
        low = jnp.where(at == EDGE - 4, ids_ref[0, t : t + 1, :], low)
        low = jnp.where(at == EDGE - 3, ids_ref[1, t : t + 1, :], low)
        out_ref[pl.ds(t * rows, main), :] = sent[:main].astype(BF16)
        out_ref[pl.ds(t * rows + main, EDGE), :] = low.astype(BF16)
        out_ref[pl.ds(t * rows + main + EDGE, EDGE), :] = sent[main + EDGE :].astype(BF16)


def reverse_lanes(x):
    tiles = x.shape[1] // LANE
    back = LANE - 1 - iota((x.shape[0], LANE), 1)
    parts = [
        jnp.take_along_axis(x[:, c * LANE : (c + 1) * LANE], back, axis=1) for c in range(tiles)
    ]
    return jnp.concatenate(parts[::-1], axis=1)


def free_ocean_kernel(ntiles, offset, me_ref, ocean_ref, nu_ref, even_ref, odd_ref, out_ref, work):
    rows, cols = ocean_ref.shape
    me = me_ref[0]
    even, bottom, top = me % 2 == 0, me == 0, me == ntiles - 1
    ev, od = even_ref[:, offset:], odd_ref[:, offset:]
    size = rows + 8
    work[0:rows] = ocean_ref[...]
    work[rows:size] = jnp.zeros((8, cols), F32)
    work[size - 2 : size] = jnp.where(bottom, 0.0, jnp.where(even, od, ev))
    work[rows : rows + 2] = jnp.where(even, ev, od)
    nu = nu_ref[...]
    x = work[...]
    at = iota((size, cols), 0)
    for _ in range(2):
        folded = pltpu.roll(reverse_lanes(x[rows - 8 : rows]), 1, 0)
        tail = jnp.where(top & (iota((8, cols), 0) == 0), folded, x[rows:])
        x = jnp.concatenate([x[:rows], tail], axis=0)
        near = (
            pltpu.roll(x, 1, 0) + pltpu.roll(x, size - 1, 0)
            + pltpu.roll(x, 1, 1) + pltpu.roll(x, cols - 1, 1)
        )
        x = x + nu * (near - 4.0 * x)
        x = jnp.where(bottom & (at >= rows + 4), 0.0, x)
    out_ref[...] = x[:rows]


def ocean_kernel(ntiles, main, me_ref, arrived_ref, free_ref, nu_ref, next_ref, return_ref):
    rows, cols = free_ref.shape
    row_tiles = cols // LANE
    per_lane = LANE // main
    step = main + 2 * EDGE
    total = rows * row_tiles
    top = me_ref[0] == ntiles - 1
    groups = ntiles // per_lane
    drive = jnp.zeros((total, LANE), F32)
    low = jnp.zeros((EDGE, LANE), F32)
    high = jnp.zeros((EDGE, LANE), F32)
    keys = []
    for g in range(groups):
        edge = jnp.zeros((EDGE, LANE), F32)
        values = []
        for s in range(g * per_lane, (g + 1) * per_lane):
            values.append(arrived_ref[pl.ds(s * step, main), :])
            edge = edge + arrived_ref[pl.ds(s * step + main, EDGE), :].astype(F32)
            high = high + arrived_ref[pl.ds(s * step + main + EDGE, EDGE), :].astype(F32)
        low = low + edge
        key = (edge[EDGE - 4 : EDGE - 3] - 1.0) * rows + edge[EDGE - 3 : EDGE - 2]
        key = key.astype(jnp.int32)
        keys.append(key)
        drive = drive + dot(
            onehot(key == iota((total, LANE), 0)), jnp.concatenate(values, axis=0)
        )
    tile = lambda c: drive[c * rows : (c + 1) * rows]
    spun = [pltpu.roll(tile(c), 1, 1) for c in range(row_tiles)]
    back = [pltpu.roll(tile(c), LANE - 1, 1) for c in range(row_tiles)]
    lane, at = iota((rows, LANE), 1), iota((rows, LANE), 0)
    turned = LANE - 1 - iota((8, LANE), 1)
    results = []
    for c in range(row_tiles):
        d = tile(c)
        left = jnp.where(lane == 0, spun[c - 1], spun[c])
        right = jnp.where(lane == LANE - 1, back[(c + 1) % row_tiles], back[c])
        under = jnp.where(at == 0, low[c : c + 1], pltpu.roll(d, 1, 0))
        fold = jnp.take_along_axis(tile(row_tiles - 1 - c)[rows - 8 :], turned, axis=1)[7:8]
        over_row = jnp.where(top, fold, high[c : c + 1])
        over = jnp.where(at == rows - 1, over_row, pltpu.roll(d, rows - 1, 0))
        span = slice(c * LANE, (c + 1) * LANE)
        near = under + over + left + right
        value = free_ref[:, span] + (2.0 * d + nu_ref[:, span] * (near - 4.0 * d))
        next_ref[:, span] = value
        results.append(value.astype(BF16))
    cells = jnp.concatenate(results, axis=0)
    for g in range(groups):
        column = jnp.transpose(jnp.broadcast_to(keys[g], (LANE, LANE)))
        wide = jnp.concatenate([column] * -(-total // LANE), axis=1)[:, :total]
        picked = dot(onehot(wide == iota((LANE, total), 1)), cells)
        return_ref[pl.ds(g * LANE, LANE), :] = picked.astype(BF16)


def backward_kernel(came_ref, sort_ref, back_ref, weight_ref, out_ref):
    values = dot(sort_ref[...], came_ref[...])
    blocks = values.shape[0]
    row = iota((CHUNK, LANE), 0)
    parts = []
    for n in range(blocks // CHUNK):
        value = values[n * CHUNK : (n + 1) * CHUNK].astype(BF16)
        weight = weight_ref[pl.ds(n * CHUNK, CHUNK)].reshape(CHUNK * LANE, LANE)
        full = dot_nt(value, weight)
        part = full[:, :LANE]
        for q in range(1, CHUNK):
            part = jnp.where(row == q, full[:, q * LANE : (q + 1) * LANE], part)
        parts.append(part)
    result = jnp.concatenate(parts, axis=0)
    coarse = result.astype(BF16)
    fine = (result - coarse.astype(F32)).astype(BF16)
    tiles = dot(back_ref[...], coarse) + dot(back_ref[...], fine)
    rows = out_ref.shape[0]
    for c in range(out_ref.shape[1] // LANE):
        out_ref[:, c * LANE : (c + 1) * LANE] = tiles[c * rows : (c + 1) * rows]


def call(kernel, outs, specs, cost, scratch=(), limit=24 << 20):
    return pl.pallas_call(
        kernel,
        out_shape=outs,
        in_specs=specs,
        out_specs=jax.tree.map(lambda _: VMEM, outs),
        scratch_shapes=scratch,
        compiler_params=pltpu.CompilerParams(vmem_limit_bytes=limit),
        cost_estimate=pl.CostEstimate(flops=cost, bytes_accessed=cost // 64, transcendentals=0),
    )


def per_device(
    atm_state,
    atm_kappa,
    forcing,
    flux_gain,
    remap_weight,
    remap_source,
    remap_owner,
    remap_dest,
    ocean_state,
    ocean_nu,
    flux_coef,
):
    ntiles = lax.axis_size("tiles")
    me = lax.axis_index("tiles")
    blocks = remap_source.shape[0]
    capacity = max(2, 2 * blocks // ntiles)
    main = -(-capacity // 16) * 16
    rows = main + 2 * EDGE
    atm_rows, atm_cols = atm_state.shape
    ocean_rows, ocean_cols = ocean_state.shape
    atm_tiles = atm_rows * atm_cols // LANE
    row_tiles = ocean_cols // LANE
    shape = jax.ShapeDtypeStruct
    even = me % 2 == 0
    first = jnp.concatenate([atm_state[:2], ocean_state[:2]], axis=1)
    last = jnp.concatenate([atm_state[-2:], ocean_state[-2:]], axis=1)
    pairs = [(2 * k + 1, (2 * k + 2) % ntiles) for k in range(ntiles // 2)]
    from_odd = lax.ppermute(
        jnp.where(even, first, last), "tiles", pairs + [(j, i) for i, j in pairs]
    )
    from_even = lax.ppermute(
        jnp.where(even, last, first), "tiles", [(i, i ^ 1) for i in range(ntiles)]
    )
    me_arr = me.astype(jnp.int32).reshape(1)
    atm_cols_tiles = atm_cols // LANE
    source = (remap_source % atm_cols_tiles) * atm_rows + remap_source // atm_cols_tiles
    pick, back, slots, sort, ids = call(
        functools.partial(routing_kernel, ntiles, main, ocean_rows, row_tiles),
        (
            shape((blocks, atm_tiles), BF16),
            shape((atm_tiles, blocks), BF16),
            shape((ntiles * rows, blocks), BF16),
            shape((blocks, ntiles * main), BF16),
            shape((2, ntiles, LANE), F32),
        ),
        [SMEM, VMEM, VMEM, VMEM, VMEM, VMEM],
        1 << 27,
    )(
        me_arr,
        source[:, None],
        source[None, :],
        remap_owner,
        remap_owner.reshape(1, blocks),
        remap_dest[None, :],
    )
    atm_next, outgoing = call(
        functools.partial(forward_kernel, ntiles, main),
        (shape(atm_state.shape, F32), shape((ntiles * rows, LANE), BF16)),
        [SMEM, SMEM, SMEM] + [VMEM] * 9,
        1 << 28,
        [pltpu.VMEM((2 * atm_rows, atm_cols), F32)],
    )(
        me_arr,
        flux_gain,
        flux_coef,
        atm_state,
        atm_kappa[None, :],
        from_even,
        from_odd,
        forcing,
        pick,
        slots,
        ids,
        remap_weight,
    )
    arrived = lax.all_to_all(outgoing, "tiles", split_axis=0, concat_axis=0, tiled=True)
    free = call(
        functools.partial(free_ocean_kernel, ntiles, atm_cols),
        shape(ocean_state.shape, F32),
        [SMEM] + [VMEM] * 4,
        1 << 27,
        [pltpu.VMEM((ocean_rows + 8, ocean_cols), F32)],
    )(me_arr, ocean_state, ocean_nu[None, :], from_even, from_odd)
    ocean_next, returned = call(
        functools.partial(ocean_kernel, ntiles, main),
        (shape(ocean_state.shape, F32), shape((ntiles * main, LANE), BF16)),
        [SMEM] + [VMEM] * 3,
        1 << 27,
    )(me_arr, arrived, free, ocean_nu[None, :])
    came_back = lax.all_to_all(returned, "tiles", split_axis=0, concat_axis=0, tiled=True)
    feedback = call(
        backward_kernel,
        shape(atm_state.shape, F32),
        [VMEM] * 4,
        1 << 28,
    )(came_back, sort, back, remap_weight)
    return (atm_next, ocean_next, feedback)


def solution(mesh):
    return jax.shard_map(
        per_device,
        mesh=mesh,
        in_specs=(
            P(("members", "tiles"), None),
            P(),
            P(None, ("members", "tiles"), None),
            P(),
            P("tiles", None, None),
            P("tiles"),
            P("tiles", None),
            P("tiles"),
            P(("members", "tiles"), None),
            P(),
            P(),
        ),
        out_specs=(
            P(("members", "tiles"), None),
            P(("members", "tiles"), None),
            P(("members", "tiles"), None),
        ),
        check_vma=False,
    )
```

time: 155 us -> 59 us (0.38)
  starting transfers between devices: 41.1 us -> 9.89 us
  waiting for transfers between devices: 42 us -> 11.6 us
  local copies, waits for them, and re-layouts: 42.5 us -> 15 us
  matrix products: 18.5 us -> 0 us
  blocking collectives: 0 us -> 11.2 us
  Pallas kernels: 0 us -> 9.22 us
  other arithmetic: 8.04 us -> 0.74 us
    scatter x2 -> x0, local copies, waits for them, and re-layouts: 25.5 us -> none  [the longest x1 23.9 us: per_device(): jnp.zeros((n_slots, NFLUX, TILE), jnp.float32).at[slot_of].set(contribution)]
    all_to_all x1, waiting for transfers between devices: 32.8 us -> 11.6 us  [per_device(): lax.all_to_all(outgoing, 'tiles', split_axis=0, concat_axis=0, tiled=True)]
    dot_general x6 -> x0, matrix products: 18.5 us -> none  [the longest x1 7.78 us: per_device(): jnp.einsum('bij,bj->bi', remap_weight, own_rows, preferred_element_type=j...]
    all_to_all x2 -> x0, starting transfers between devices: 16.2 us -> none  [the longest x1 12.6 us: per_device(): lax.all_to_all(returned, 'tiles', split_axis=0, concat_axis=0, tiled=True)]
    unnamed x14 -> x23, local copies, waits for them, and re-layouts: 0.04 us -> 12.8 us
    ppermute x8 -> x2, starting transfers between devices: 19 us -> 6.18 us  [the longest x1 5.67 us: per_device(): lax.ppermute(jnp.where(even, first, last), 'tiles', pairs + [(j, i) for i...]
    all_to_all x0 -> x1, blocking collectives: none -> 11.2 us  [per_device(): lax.all_to_all(returned, 'tiles', split_axis=0, concat_axis=0, tiled=True)]
    pallas_call x0 -> x5, Pallas kernels: none -> 9.22 us  [the longest x1 3.28 us: per_device(): call(functools.partial(forward_kernel, ntiles, main), (shape(atm_state.sh...]
  transfers between devices with their start and end apart: 11 -> 3, of which waited for: 3 -> 1; matrix products, arithmetic and copies ran while one was open for 36% -> 3% of each run, Pallas kernels for 0% -> 2%
where the time goes in v1:
time: 59 us; the launch traced here: 58.5 us
  local copies, waits for them, and re-layouts  15 us (25%)
  waiting for transfers between devices  11.6 us (20%)
  blocking collectives  11.2 us (19%)
  starting transfers between devices  9.89 us (17%)
  Pallas kernels  9.22 us (16%)
  between operations  0.78 us (1%)
  other arithmetic  0.74 us (1%)
    unnamed x23, local copies, waits for them, and re-layouts  12.8 us
    all_to_all x1, waiting for transfers between devices, per_device(): lax.all_to_all(outgoing, 'tiles', split_axis=0, concat_axis=0, tiled=True)  11.6 us
    all_to_all x1, blocking collectives, per_device(): lax.all_to_all(returned, 'tiles', split_axis=0, concat_axis=0, tiled=True)  11.2 us
    ppermute x1, starting transfers between devices, per_device(): lax.ppermute(jnp.where(even, first, last), 'tiles', pairs + [(j, i) for i...  5.67 us
    all_to_all x1, starting transfers between devices, per_device(): lax.all_to_all(outgoing, 'tiles', split_axis=0, concat_axis=0, tiled=True)  3.7 us
    pallas_call x1, Pallas kernels, per_device(): call(functools.partial(forward_kernel, ntiles, main), (shape(atm_state.sh...  3.28 us
    pallas_call x1, Pallas kernels, per_device(): call(backward_kernel, shape(atm_state.shape, F32), [VMEM] * 4, 1 << 28)  3.24 us
    slice x2, local copies, waits for them, and re-layouts, per_device(): last = jnp.concatenate([atm_state[-2:], ocean_state[-2:]], axis=1)  2 us
  transfers between devices with their start and end apart: 3, of which 1 were waited for; matrix products, arithmetic and copies ran while one was open for 3% of the time, Pallas kernels for 2%

profile of v1, /device:TPU:0, one launch (start us, length us, event | category | flops | bytes accessed | tf_op | source)
XLA Modules:
  0.0 58.5 jit_solution(5962037791639476340)
XLA Ops:
  0.6 0.0 copy-start.3
  0.6 0.0 copy-start.10
  0.7 1.0 %fusion.2 = (f32[2,3584]{1,0:T(2,128)S(1)}, f32[2,3584]{1,0:T(2,128)S(1)}) fusion(f32[16,3584]{1,0:T(8,128)} %ocean_ref.1), kind=kLoop, calls=%fused_computation.8 | loop fusion | bytes 114688 | tf_op jit(solution)/shard_map/slice | solution.py:278
  1.7 1.0 %fusion.3 = (f32[2,3072]{1,0:T(2,128)S(1)}, f32[2,3072]{1,0:T(2,128)S(1)}) fusion(f32[8,3072]{1,0:T(8,128)} %atm_ref.1), kind=kLoop, calls=%fused_computation.9 | loop fusion | bytes 98304 | tf_op jit(solution)/shard_map/slice | solution.py:278
  2.7 0.1 broadcast_select_fusion
  2.7 0.5 collective-permute-start
  3.2 5.7 %collective-permute-start.1 = (f32[2,6656]{1,0:T(2,128)S(1)}, f32[2,6656]{1,0:T(2,128)S(1)}, u32[]{:S(2)}, u32[]{:S(2)}) collective-permute-start(f32[2,6656]{1,0:T(2,128)S(1)} %get-tuple-element.23), channel_id=1, source_target_pairs={{1,2},{3,4},{5,6},{7,8},{9,10},{11,12},{13,14},{15,0},{2,1},{4,3},... | collective-permute-start | bytes 159752 | tf_op jit(solution)/shard_map/ppermute | solution.py:280
  8.9 0.7 %fusion.1 = s32[256]{0:T(256)S(1)} fusion(s32[256]{0:T(256)} %param.16), kind=kLoop, calls=%fused_computation.7 | loop fusion | flops 3584 | bytes 2048 | tf_op jit(solution)/shard_map/add | solution.py:288
  9.6 0.1 copy.15.src_col
  9.8 0.8 %copy.16.own_col = s32[256,1]{1,0:T(8,128)S(1)} copy(s32[256,1]{0,1:T(1,128)} %param.17) | data formatting | bytes 2048 | tf_op args[6]
  10.6 0.0 copy-start.6
  10.6 0.7 %copy-done.6 = s32[256,1]{0,1:T(1,128)S(1)} copy-done((s32[256,1]{0,1:T(1,128)S(1)}, s32[256,1]{0,1:T(1,128)}, u32[]{:S(2)}) %copy-start.6) | copy-done | bytes 1048
  11.3 0.0 copy-start.9
  11.3 0.7 %copy-done.9 = s32[256]{0:T(256)S(1)} copy-done((s32[256]{0:T(256)S(1)}, s32[256]{0:T(256)}, u32[]{:S(2)}) %copy-start.9) | copy-done | bytes 1048
  11.9 0.9 %shard_map.130 = (bf16[256,192]{1,0:T(8,128)(2,1)S(1)}, bf16[192,256]{1,0:T(8,128)(2,1)S(1)}, bf16[1536,256]{1,0:T(8,128)(2,1)S(1)}, bf16[256,512]{1,0:T(8,128)(2,1)S(1)}, f32[2,16,128]{2,1,0:T(8,128)S(1)}) custom-call(s32[1]{0:T(128)} %bitcast.me_ref, s32[256,1]{1,0:T(8,128)S(1)} %copy.15.src_col, s32[1,256]{1,0:T(1,128)S(1)} %bitcast.15, ...), custom_call_target="tpu_custom_call" | custom-call | flops 134217728 | bytes 2097152 | tf_op jit(solution)/shard_map/pallas_call | solution.py:289
  12.8 0.0 collective-permute-done.even_ref
  12.8 0.0 collective-permute-done.1.odd_ref
  12.8 0.0 copy-start
  12.9 3.4 %copy-done = bf16[256,128,128]{2,1,0:T(8,128)(2,1)S(1)} copy-done((bf16[256,128,128]{2,1,0:T(8,128)(2,1)S(1)}, bf16[256,128,128]{2,1,0:T(8,128)(2,1)}, u32[]{:S(2)}) %copy-start) | copy-done | bytes 8388632
  16.2 0.0 copy-start.2
  16.2 1.0 %copy-done.2 = bf16[8,8,3072]{2,1,0:T(8,128)(2,1)S(1)} copy-done((bf16[8,8,3072]{2,1,0:T(8,128)(2,1)S(1)}, bf16[8,8,3072]{2,1,0:T(8,128)(2,1)}, u32[]{:S(2)}) %copy-start.2) | copy-done | bytes 393240
  17.2 0.0 copy-start.4
  17.2 0.9 %copy-done.4 = f32[8,3072]{1,0:T(8,128)S(1)} copy-done((f32[8,3072]{1,0:T(8,128)S(1)}, f32[8,3072]{1,0:T(8,128)}, u32[]{:S(2)}) %copy-start.4) | copy-done | bytes 98328
  18.1 0.0 copy-start.5
  18.1 0.7 %copy-done.5 = f32[3072]{0:T(1024)S(1)} copy-done((f32[3072]{0:T(1024)S(1)}, f32[3072]{0:T(1024)}, u32[]{:S(2)}) %copy-start.5) | copy-done | bytes 12312
  18.8 0.0 copy-start.7
  18.8 0.7 %copy-done.7 = f32[8]{0:T(128)S(1)} copy-done((f32[8]{0:T(128)S(1)}, f32[8]{0:T(128)}, u32[]{:S(2)}) %copy-start.7) | copy-done | bytes 56
  19.5 0.0 copy-start.8
  19.5 0.7 %copy-done.8 = f32[8]{0:T(128)S(1)} copy-done((f32[8]{0:T(128)S(1)}, f32[8]{0:T(128)}, u32[]{:S(2)}) %copy-start.8) | copy-done | bytes 56
  20.1 3.3 %shard_map.131 = (f32[8,3072]{1,0:T(8,128)}, bf16[1536,128]{1,0:T(8,128)(2,1)}) custom-call(s32[1]{0:T(128)} %bitcast.me_ref, f32[8]{0:T(128)S(1)} %copy-done.7, f32[8]{0:T(128)S(1)} %copy-done.8, f32[8,3072]{1,0:T(8,128)S(1)} %copy-done.4, f32[1,3072]{1,0:T(1,128)S(1)} %bitcast.13, f32[2,6656]{1,0:T(2,128)S(1)} %collective-permute-done.even_ref, ...), custom_call_target="tpu_custom_call" | custom-call | flops 268435456 | bytes 4194304 | tf_op jit(solution)/shard_map/pallas_call | solution.py:308
  23.4 3.7 %all-to-all-start = ((bf16[16,96,128]{2,1,0:T(8,128)(2,1)}), bf16[16,96,128]{2,1,0:T(8,128)(2,1)S(1)}, u32[]{:S(2)}, u32[]{:S(2)}) async-start(bf16[16,96,128]{2,1,0:T(8,128)(2,1)} %bitcast.6), calls=%async_computation | async-start | bytes 786432 | tf_op jit(solution)/shard_map/all_to_all | solution.py:328
  27.1 0.0 copy-done.10
  27.2 0.0 copy-done.3
  27.2 0.6 shard_map.132.free_ref
  27.7 11.6 %all-to-all-done = bf16[16,96,128]{2,1,0:T(8,128)(2,1)S(1)} async-done(((bf16[16,96,128]{2,1,0:T(8,128)(2,1)}), bf16[16,96,128]{2,1,0:T(8,128)(2,1)S(1)}, u32[]{:S(2)}, u32[]{:S(2)}) %all-to-all-start) | async-done | bytes 393248 | tf_op jit(solution)/shard_map/all_to_all | solution.py:328
  39.3 1.3 %shard_map.133 = (f32[16,3584]{1,0:T(8,128)}, bf16[512,128]{1,0:T(8,128)(2,1)S(1)}) custom-call(s32[1]{0:T(128)} %bitcast.me_ref, bf16[1536,128]{1,0:T(8,128)(2,1)S(1)} %bitcast.10, f32[16,3584]{1,0:T(8,128)S(1)} %shard_map.132.free_ref, f32[1,3584]{1,0:T(1,128)S(1)} %broadcast_in_dim.20.nu_ref), custom_call_target="tpu_custom_call" | custom-call | flops 134217728 | bytes 2097152 | tf_op jit(solution)/shard_map/pallas_call | solution.py:336
  40.6 11.2 %all_to_all.22 = bf16[16,32,128]{2,1,0:T(8,128)(2,1)S(1)} all-to-all(bf16[16,32,128]{2,1,0:T(8,128)(2,1)S(1)} %bitcast.12), channel_id=1, replica_groups=mesh['members'=2,'tiles'=16] {'tiles'}, dimensions={0} | all-to-all | bytes 262144 | tf_op jit(solution)/shard_map/all_to_all | solution.py:342
  51.8 0.0 copy-start.1
  51.8 3.4 %copy-done.1 = bf16[256,128,128]{2,1,0:T(8,128)(2,1)S(1)} copy-done((bf16[256,128,128]{2,1,0:T(8,128)(2,1)S(1)}, bf16[256,128,128]{2,1,0:T(8,128)(2,1)}, u32[]{:S(2)}) %copy-start.1) | copy-done | bytes 8388632
  55.2 3.2 %shard_map.134 = f32[8,3072]{1,0:T(8,128)} custom-call(bf16[512,128]{1,0:T(8,128)(2,1)S(1)} %bitcast.11, bf16[256,512]{1,0:T(8,128)(2,1)S(1)} %get-tuple-element.19.sort_ref, bf16[192,256]{1,0:T(8,128)(2,1)S(1)} %get-tuple-element.20.back_ref, bf16[256,128,128]{2,1,0:T(8,128)(2,1)S(1)} %copy-done.1), custom_call_target="tpu_custom_call" | custom-call | flops 268435456 | bytes 4194304 | tf_op jit(solution)/shard_map/pallas_call | solution.py:343
  (1 shorter events, 0.0 us)
Async XLA Ops:
  0.6 26.5 %copy-start.3 = (f32[16,3584]{1,0:T(8,128)S(1)}, f32[16,3584]{1,0:T(8,128)}, u32[]{:S(2)}) copy-start(f32[16,3584]{1,0:T(8,128)} %ocean_ref.1) | copy-start | bytes 688132
  0.6 26.5 %copy-start.10 = (f32[3584]{0:T(1024)S(1)}, f32[3584]{0:T(1024)}, u32[]{:S(2)}) copy-start(f32[3584]{0:T(1024)} %param.20) | copy-start | bytes 43012
  2.7 10.1 %collective-permute-start = (f32[2,6656]{1,0:T(2,128)S(1)}, f32[2,6656]{1,0:T(2,128)S(1)}, u32[]{:S(2)}, u32[]{:S(2)}) collective-permute-start(f32[2,6656]{1,0:T(2,128)S(1)} %get-tuple-element.24), channel_id=1, source_target_pairs={{0,1},{1,0},{2,3},{3,2},{4,5},{5,4},{6,7},{7,6},{8,9},{9,8},{10,11... | collective-permute-start | bytes 159752 | tf_op jit(solution)/shard_map/ppermute | solution.py:283
  3.2 9.6 %collective-permute-start.1 = (f32[2,6656]{1,0:T(2,128)S(1)}, f32[2,6656]{1,0:T(2,128)S(1)}, u32[]{:S(2)}, u32[]{:S(2)}) collective-permute-start(f32[2,6656]{1,0:T(2,128)S(1)} %get-tuple-element.23), channel_id=1, source_target_pairs={{1,2},{3,4},{5,6},{7,8},{9,10},{11,12},{13,14},{15,0},{2,1},{4,3},... | collective-permute-start | bytes 159752 | tf_op jit(solution)/shard_map/ppermute | solution.py:280
  10.6 0.7 %copy-start.6 = (s32[256,1]{0,1:T(1,128)S(1)}, s32[256,1]{0,1:T(1,128)}, u32[]{:S(2)}) copy-start(s32[256,1]{0,1:T(1,128)} %param.17) | copy-start | bytes 3076
  11.3 0.7 %copy-start.9 = (s32[256]{0:T(256)S(1)}, s32[256]{0:T(256)}, u32[]{:S(2)}) copy-start(s32[256]{0:T(256)} %param.18) | copy-start | bytes 3076
  12.8 3.4 %copy-start = (bf16[256,128,128]{2,1,0:T(8,128)(2,1)S(1)}, bf16[256,128,128]{2,1,0:T(8,128)(2,1)}, u32[]{:S(2)}) copy-start(bf16[256,128,128]{2,1,0:T(8,128)(2,1)} %weight_ref.3) | copy-start | bytes 25165828
  16.2 1.0 %copy-start.2 = (bf16[8,8,3072]{2,1,0:T(8,128)(2,1)S(1)}, bf16[8,8,3072]{2,1,0:T(8,128)(2,1)}, u32[]{:S(2)}) copy-start(bf16[8,8,3072]{2,1,0:T(8,128)(2,1)} %forcing_ref.1) | copy-start | bytes 1179652
  17.2 0.9 %copy-start.4 = (f32[8,3072]{1,0:T(8,128)S(1)}, f32[8,3072]{1,0:T(8,128)}, u32[]{:S(2)}) copy-start(f32[8,3072]{1,0:T(8,128)} %atm_ref.1) | copy-start | bytes 294916
  18.1 0.7 %copy-start.5 = (f32[3072]{0:T(1024)S(1)}, f32[3072]{0:T(1024)}, u32[]{:S(2)}) copy-start(f32[3072]{0:T(1024)} %param.12) | copy-start | bytes 36868
  18.8 0.7 %copy-start.7 = (f32[8]{0:T(128)S(1)}, f32[8]{0:T(128)}, u32[]{:S(2)}) copy-start(f32[8]{0:T(128)} %gain_ref.1) | copy-start | bytes 100
  19.5 0.7 %copy-start.8 = (f32[8]{0:T(128)S(1)}, f32[8]{0:T(128)}, u32[]{:S(2)}) copy-start(f32[8]{0:T(128)} %coef_ref.1) | copy-start | bytes 100
  23.4 15.9 %all-to-all-start = ((bf16[16,96,128]{2,1,0:T(8,128)(2,1)}), bf16[16,96,128]{2,1,0:T(8,128)(2,1)S(1)}, u32[]{:S(2)}, u32[]{:S(2)}) async-start(bf16[16,96,128]{2,1,0:T(8,128)(2,1)} %bitcast.6), calls=%async_computation | async-start | bytes 786432 | tf_op jit(solution)/shard_map/all_to_all | solution.py:328
  51.8 3.4 %copy-start.1 = (bf16[256,128,128]{2,1,0:T(8,128)(2,1)S(1)}, bf16[256,128,128]{2,1,0:T(8,128)(2,1)}, u32[]{:S(2)}) copy-start(bf16[256,128,128]{2,1,0:T(8,128)(2,1)} %weight_ref.3) | copy-start | bytes 25165828

commit v2 on v1

--- a/solution.py
+++ b/solution.py
@@ -10,10 +10,12 @@
 LANE = 128
 EDGE = 32
 CHUNK = 8
+PIECES = 8
 F32 = jnp.float32
 BF16 = jnp.bfloat16
 VMEM = pl.BlockSpec(memory_space=pltpu.VMEM)
 SMEM = pl.BlockSpec(memory_space=pltpu.SMEM)
+HBM = pl.BlockSpec(memory_space=pltpu.HBM)
 
 
 def iota(shape, dim):
@@ -32,30 +34,81 @@
     return jnp.where(mask, 1.0, 0.0).astype(BF16)
 
 
-def routing_kernel(
-    ntiles, main, ocean_rows, row_tiles, me_ref, src_col, src_row, own_col, own_row, dst_row,
-    pick_ref, back_ref, slots_ref, sort_ref, ids_ref,
+def as_column(row):
+    parts = [
+        jnp.transpose(jnp.broadcast_to(row[:, k : k + LANE], (LANE, LANE)))
+        for k in range(0, row.shape[1], LANE)
+    ]
+    return jnp.concatenate(parts, axis=0)
+
+
+def matches_lane(column, width):
+    parts = [
+        onehot(column == iota(column.shape, 1) + k)[:, : min(LANE, width - k)]
+        for k in range(0, width, LANE)
+    ]
+    return jnp.concatenate(parts, axis=1)
+
+
+def send_kernel(me_ref, atm_hbm, ocean_hbm, atm_ref, ocean_ref, even_ref, odd_ref, sems):
+    copies = [
+        pltpu.make_async_copy(atm_hbm, atm_ref, sems.at[0]),
+        pltpu.make_async_copy(ocean_hbm, ocean_ref, sems.at[1]),
+    ]
+    for copy in copies:
+        copy.start()
+    even = me_ref[0] % 2 == 0
+    start = 0
+    for copy, ref in zip(copies, (atm_ref, ocean_ref)):
+        copy.wait()
+        rows, cols = ref.shape
+        first, last = ref[0:2], ref[rows - 2 : rows]
+        even_ref[:, start : start + cols] = jnp.where(even, last, first)
+        odd_ref[:, start : start + cols] = jnp.where(even, first, last)
+        start += cols
+
+
+def stage_kernel(
+    ntiles, main, atm_rows, atm_row_tiles, ocean_rows, row_tiles,
+    me_ref, src_hbm, own_hbm, dst_hbm, gain_hbm, coef_hbm, kappa_hbm, nu_hbm, forcing_hbm,
+    weight_hbm,
+    pick_ref, back_ref, slots_ref, sort_ref, ids_ref, field_ref, scale_ref, kappa_ref, nu_ref,
+    weight_ref,
+    ints, gains, forcing_ref, sems,
 ):
-    blocks = own_row.shape[1]
+    small = [
+        (src_hbm, ints.at[0]), (own_hbm, ints.at[1]), (dst_hbm, ints.at[2]),
+        (gain_hbm, gains.at[0]), (coef_hbm, gains.at[1]), (forcing_hbm, forcing_ref),
+        (kappa_hbm, kappa_ref), (nu_hbm, nu_ref),
+    ]
+    copies = [pltpu.make_async_copy(a, b, sems.at[k]) for k, (a, b) in enumerate(small)]
+    share = weight_hbm.shape[0] // PIECES
+    for n in range(PIECES):
+        span = pl.ds(n * share, share)
+        copies.append(
+            pltpu.make_async_copy(
+                weight_hbm.at[span], weight_ref.at[span], sems.at[len(small) + n]
+            )
+        )
+    for copy in copies:
+        copy.start()
+    for copy in copies[:3]:
+        copy.wait()
     rows = main + 2 * EDGE
     per_lane = LANE // main
-    owner = own_row[...]
-    row_of, col_of = dst_row[...] // row_tiles, dst_row[...] % row_tiles
-    owner_c = own_col[...]
-    match_c = owner_c == iota((blocks, LANE), 1)
-    below = onehot(iota((blocks, blocks), 1) < iota((blocks, blocks), 0))
-    rank_c = jnp.sum(
-        jnp.where(match_c, dot(below, onehot(match_c)), 0.0), axis=1, keepdims=True
+    source, owner, dest = ints[0], ints[1], ints[2]
+    blocks = owner.shape[1]
+    source = (source % atm_row_tiles) * atm_rows + source // atm_row_tiles
+    row_of, col_of = dest // row_tiles, dest % row_tiles
+    match = owner == iota((ntiles, blocks), 0)
+    above = onehot(iota((blocks, blocks), 0) < iota((blocks, blocks), 1))
+    rank = jnp.sum(
+        jnp.where(match, dot(onehot(match), above), 0.0), axis=0, keepdims=True
     ).astype(jnp.int32)
-    match_r = owner == iota((ntiles, blocks), 0)
-    above = onehot(iota((blocks, blocks), 0) < iota((blocks, blocks), 1))
-    rank_r = jnp.sum(
-        jnp.where(match_r, dot(onehot(match_r), above), 0.0), axis=0, keepdims=True
-    ).astype(jnp.int32)
-    pick_ref[...] = onehot(src_col[...] == iota(pick_ref.shape, 1))
-    back_ref[...] = onehot(src_row[...] == iota(back_ref.shape, 0))
-    sort_ref[...] = onehot(owner_c * main + rank_c == iota(sort_ref.shape, 1))
-    own_slot = owner * rows + rank_r
+    pick_ref[...] = matches_lane(as_column(source), pick_ref.shape[1])
+    back_ref[...] = onehot(source == iota(back_ref.shape, 0))
+    sort_ref[...] = matches_lane(as_column(owner * main + rank), sort_ref.shape[1])
+    own_slot = owner * rows + rank
     low = (row_of == ocean_rows - 1) & (owner < ntiles - 1)
     low_slot = jnp.where(low, (owner + 1) * rows + main + col_of, -1)
     high = (row_of == 0) & (owner > 0)
@@ -65,14 +118,26 @@
         slots_ref[pl.ds(t * rows, rows), :] = onehot(
             (slot == own_slot) | (slot == low_slot) | (slot == high_slot)
         )
-    lane_of = rank_c + (me_ref[0] % per_lane) * main
-    place = onehot(lane_of == iota((blocks, LANE), 1))
-    ids_ref[0] = dot(jnp.where(match_r, (col_of + 1).astype(F32), 0.0).astype(BF16), place)
-    ids_ref[1] = dot(jnp.where(match_r, row_of.astype(F32), 0.0).astype(BF16), place)
+    lane_of = rank + (me_ref[0] % per_lane) * main
+    place = onehot(lane_of == iota((LANE, blocks), 0))
+    ids_ref[0] = dot_nt(jnp.where(match, (col_of + 1).astype(F32), 0.0).astype(BF16), place)
+    ids_ref[1] = dot_nt(jnp.where(match, row_of.astype(F32), 0.0).astype(BF16), place)
+    for copy in copies[3 : len(small)]:
+        copy.wait()
+    coef = gains[1]
+    scale_ref[...] = jnp.broadcast_to(
+        jnp.sum(gains[0] * coef, axis=1, keepdims=True), scale_ref.shape
+    )
+    field = jnp.zeros(field_ref.shape, F32)
+    for k in range(forcing_ref.shape[0]):
+        field = field + coef[:, k : k + 1] * forcing_ref[k].astype(F32)
+    field_ref[...] = field
+    for copy in copies[len(small) :]:
+        copy.wait()
 
 
 def forward_kernel(
-    ntiles, main, me_ref, gain_ref, coef_ref, atm_ref, kappa_ref, even_ref, odd_ref, forcing_ref,
+    ntiles, main, me_ref, atm_ref, kappa_ref, even_ref, odd_ref, field_ref, scale_ref,
     pick_ref, slots_ref, ids_ref, weight_ref, next_ref, out_ref, work,
 ):
     atm_rows, cols = atm_ref.shape
@@ -94,13 +159,7 @@
         x = x + kappa * (near - 4.0 * x)
     atm = x[:atm_rows]
     next_ref[...] = atm
-    nflux = forcing_ref.shape[0]
-    scale = coef_ref[0] * gain_ref[0]
-    for k in range(1, nflux):
-        scale = scale + coef_ref[k] * gain_ref[k]
-    field = scale * atm
-    for k in range(nflux):
-        field = field + coef_ref[k] * forcing_ref[k].astype(F32)
+    field = field_ref[...] + scale_ref[:, 0:1] * atm
     tiles = jnp.concatenate(
         [field[:, c * LANE : (c + 1) * LANE] for c in range(cols // LANE)], axis=0
     ).astype(BF16)
@@ -146,7 +205,7 @@
     work[rows:size] = jnp.zeros((8, cols), F32)
     work[size - 2 : size] = jnp.where(bottom, 0.0, jnp.where(even, od, ev))
     work[rows : rows + 2] = jnp.where(even, ev, od)
-    nu = nu_ref[...]
+    nu = jnp.concatenate([nu_ref[c : c + 1] for c in range(cols // LANE)], axis=1)
     x = work[...]
     at = iota((size, cols), 0)
     for _ in range(2):
@@ -204,7 +263,7 @@
         over = jnp.where(at == rows - 1, over_row, pltpu.roll(d, rows - 1, 0))
         span = slice(c * LANE, (c + 1) * LANE)
         near = under + over + left + right
-        value = free_ref[:, span] + (2.0 * d + nu_ref[:, span] * (near - 4.0 * d))
+        value = free_ref[:, span] + (2.0 * d + nu_ref[c : c + 1] * (near - 4.0 * d))
         next_ref[:, span] = value
         results.append(value.astype(BF16))
     cells = jnp.concatenate(results, axis=0)
@@ -238,7 +297,7 @@
 
 
 def call(kernel, outs, specs, cost, scratch=(), limit=24 << 20):
-    return pl.pallas_call(
+    run = pl.pallas_call(
         kernel,
         out_shape=outs,
         in_specs=specs,
@@ -247,6 +306,16 @@
         compiler_params=pltpu.CompilerParams(vmem_limit_bytes=limit),
         cost_estimate=pl.CostEstimate(flops=cost, bytes_accessed=cost // 64, transcendentals=0),
     )
+
+    def placed(*args):
+        return run(
+            *[
+                pltpu.with_memory_space_constraint(x, pltpu.HBM) if spec is HBM else x
+                for x, spec in zip(args, specs)
+            ]
+        )
+
+    return placed
 
 
 def per_device(
@@ -273,58 +342,63 @@
     atm_tiles = atm_rows * atm_cols // LANE
     row_tiles = ocean_cols // LANE
     shape = jax.ShapeDtypeStruct
-    even = me % 2 == 0
-    first = jnp.concatenate([atm_state[:2], ocean_state[:2]], axis=1)
-    last = jnp.concatenate([atm_state[-2:], ocean_state[-2:]], axis=1)
+    me_arr = me.astype(jnp.int32).reshape(1)
+    edges = shape((2, atm_cols + ocean_cols), F32)
+    atm, ocean, to_even, to_odd = call(
+        send_kernel,
+        (shape(atm_state.shape, F32), shape(ocean_state.shape, F32), edges, edges),
+        [SMEM, HBM, HBM],
+        1 << 20,
+        [pltpu.SemaphoreType.DMA((2,))],
+    )(me_arr, atm_state, ocean_state)
     pairs = [(2 * k + 1, (2 * k + 2) % ntiles) for k in range(ntiles // 2)]
-    from_odd = lax.ppermute(
-        jnp.where(even, first, last), "tiles", pairs + [(j, i) for i, j in pairs]
-    )
-    from_even = lax.ppermute(
-        jnp.where(even, last, first), "tiles", [(i, i ^ 1) for i in range(ntiles)]
-    )
-    me_arr = me.astype(jnp.int32).reshape(1)
-    atm_cols_tiles = atm_cols // LANE
-    source = (remap_source % atm_cols_tiles) * atm_rows + remap_source // atm_cols_tiles
-    pick, back, slots, sort, ids = call(
-        functools.partial(routing_kernel, ntiles, main, ocean_rows, row_tiles),
+    from_odd = lax.ppermute(to_odd, "tiles", pairs + [(j, i) for i, j in pairs])
+    from_even = lax.ppermute(to_even, "tiles", [(i, i ^ 1) for i in range(ntiles)])
+    atm_row_tiles = atm_cols // LANE
+    nflux = forcing.shape[0]
+    pick, back, slots, sort, ids, field, scale, kappa, nu, weight = call(
+        functools.partial(
+            stage_kernel, ntiles, main, atm_rows, atm_row_tiles, ocean_rows, row_tiles
+        ),
         (
             shape((blocks, atm_tiles), BF16),
             shape((atm_tiles, blocks), BF16),
             shape((ntiles * rows, blocks), BF16),
             shape((blocks, ntiles * main), BF16),
             shape((2, ntiles, LANE), F32),
+            shape(atm_state.shape, F32),
+            shape((1, LANE), F32),
+            shape((1, atm_cols), F32),
+            shape((row_tiles, LANE), F32),
+            shape(remap_weight.shape, BF16),
         ),
-        [SMEM, VMEM, VMEM, VMEM, VMEM, VMEM],
-        1 << 27,
+        [SMEM] + [HBM] * 9,
+        1 << 31,
+        [
+            pltpu.VMEM((3, 1, blocks), jnp.int32),
+            pltpu.VMEM((2, 1, nflux), F32),
+            pltpu.VMEM(forcing.shape, BF16),
+            pltpu.SemaphoreType.DMA((8 + PIECES,)),
+        ],
     )(
         me_arr,
-        source[:, None],
-        source[None, :],
-        remap_owner,
+        remap_source.reshape(1, blocks),
         remap_owner.reshape(1, blocks),
-        remap_dest[None, :],
+        remap_dest.reshape(1, blocks),
+        flux_gain.reshape(1, nflux),
+        flux_coef.reshape(1, nflux),
+        atm_kappa.reshape(1, atm_cols),
+        ocean_nu.reshape(row_tiles, LANE),
+        forcing,
+        remap_weight,
     )
     atm_next, outgoing = call(
         functools.partial(forward_kernel, ntiles, main),
         (shape(atm_state.shape, F32), shape((ntiles * rows, LANE), BF16)),
-        [SMEM, SMEM, SMEM] + [VMEM] * 9,
+        [SMEM] + [VMEM] * 10,
         1 << 28,
         [pltpu.VMEM((2 * atm_rows, atm_cols), F32)],
-    )(
-        me_arr,
-        flux_gain,
-        flux_coef,
-        atm_state,
-        atm_kappa[None, :],
-        from_even,
-        from_odd,
-        forcing,
-        pick,
-        slots,
-        ids,
-        remap_weight,
-    )
+    )(me_arr, atm, kappa, from_even, from_odd, field, scale, pick, slots, ids, weight)
     arrived = lax.all_to_all(outgoing, "tiles", split_axis=0, concat_axis=0, tiled=True)
     free = call(
         functools.partial(free_ocean_kernel, ntiles, atm_cols),
@@ -332,20 +406,20 @@
         [SMEM] + [VMEM] * 4,
         1 << 27,
         [pltpu.VMEM((ocean_rows + 8, ocean_cols), F32)],
-    )(me_arr, ocean_state, ocean_nu[None, :], from_even, from_odd)
+    )(me_arr, ocean, nu, from_even, from_odd)
     ocean_next, returned = call(
         functools.partial(ocean_kernel, ntiles, main),
         (shape(ocean_state.shape, F32), shape((ntiles * main, LANE), BF16)),
         [SMEM] + [VMEM] * 3,
         1 << 27,
-    )(me_arr, arrived, free, ocean_nu[None, :])
+    )(me_arr, arrived, free, nu)
     came_back = lax.all_to_all(returned, "tiles", split_axis=0, concat_axis=0, tiled=True)
     feedback = call(
         backward_kernel,
         shape(atm_state.shape, F32),
         [VMEM] * 4,
         1 << 28,
-    )(came_back, sort, back, remap_weight)
+    )(came_back, sort, back, weight)
     return (atm_next, ocean_next, feedback)
 
 

time: 59 us -> 53.1 us (0.900)
  local copies, waits for them, and re-layouts: 15 us -> 6.61 us
  Pallas kernels: 9.22 us -> 12.6 us
  other arithmetic: 0.74 us -> 0 us
    unnamed x23 -> x4, local copies, waits for them, and re-layouts: 12.8 us -> 6.61 us
    pallas_call x5 -> x6, Pallas kernels: 9.22 us -> 12.6 us  [placed(): run(*[pltpu.with_memory_space_constraint(x, pltpu.HBM) if spec is HBM els...]
    slice x2 -> x0, local copies, waits for them, and re-layouts: 2 us -> none  [per_device(): last = jnp.concatenate([atm_state[-2:], ocean_state[-2:]], axis=1)]
    add x1 -> x0, other arithmetic: 0.69 us -> none  [per_device(): remap_source % atm_cols_tiles * atm_rows + remap_source // atm_cols_tiles]
  transfers between devices with their start and end apart: 3 -> 3, of which waited for: 1 -> 1; matrix products, arithmetic and copies ran while one was open for 3% -> 0% of each run, Pallas kernels for 2% -> 8%
where the time goes in v2:
time: 53.1 us; the launch traced here: 52.8 us
  Pallas kernels  12.6 us (24%)
  waiting for transfers between devices  11.6 us (22%)
  blocking collectives  11.2 us (21%)
  starting transfers between devices  10 us (19%)
  local copies, waits for them, and re-layouts  6.61 us (12%)
  between operations  0.69 us (1%)
    pallas_call x6, Pallas kernels, placed(): run(*[pltpu.with_memory_space_constraint(x, pltpu.HBM) if spec is HBM els...  12.6 us
    all_to_all x1, waiting for transfers between devices, per_device(): lax.all_to_all(outgoing, 'tiles', split_axis=0, concat_axis=0, tiled=True)  11.6 us
    all_to_all x1, blocking collectives, per_device(): lax.all_to_all(returned, 'tiles', split_axis=0, concat_axis=0, tiled=True)  11.2 us
    unnamed x4, local copies, waits for them, and re-layouts  6.61 us
    ppermute x1, starting transfers between devices, per_device(): from_odd = lax.ppermute(to_odd, 'tiles', pairs + [(j, i) for i, j in pairs])  5.67 us
    all_to_all x1, starting transfers between devices, per_device(): lax.all_to_all(outgoing, 'tiles', split_axis=0, concat_axis=0, tiled=True)  3.84 us
  transfers between devices with their start and end apart: 3, of which 1 were waited for; matrix products, arithmetic and copies ran while one was open for 0% of the time, Pallas kernels for 8%

profile of v2, /device:TPU:0, one launch (start us, length us, event | category | flops | bytes accessed | tf_op | source)
XLA Modules:
  0.0 52.8 jit_solution(4894242888731316105)
XLA Ops:
  0.6 1.0 %shard_map.130 = (f32[8,3072]{1,0:T(8,128)S(1)}, f32[16,3584]{1,0:T(8,128)S(1)}, f32[2,6656]{1,0:T(2,128)S(1)}, f32[2,6656]{1,0:T(2,128)S(1)}) custom-call(s32[1]{0:T(128)} %bitcast.me_ref, f32[8,3072]{1,0:T(8,128)} %atm_hbm.1, f32[16,3584]{1,0:T(8,128)} %ocean_hbm.1), custom_call_target="tpu_custom_call" | custom-call | flops 1048576 | bytes 16384 | tf_op jit(solution)/shard_map/pallas_call | solution.py:311
  1.7 0.5 collective-permute-start
  2.2 5.7 %collective-permute-start.1 = (f32[2,6656]{1,0:T(2,128)S(1)}, f32[2,6656]{1,0:T(2,128)S(1)}, u32[]{:S(2)}, u32[]{:S(2)}) collective-permute-start(f32[2,6656]{1,0:T(2,128)S(1)} %get-tuple-element.24), channel_id=1, source_target_pairs={{1,2},{3,4},{5,6},{7,8},{9,10},{11,12},{13,14},{15,0},{2,1},{4,3},... | collective-permute-start | bytes 159752 | tf_op jit(solution)/shard_map/ppermute | solution.py:355
  7.9 3.8 %shard_map.131 = (bf16[256,192]{1,0:T(8,128)(2,1)S(1)}, bf16[192,256]{1,0:T(8,128)(2,1)S(1)}, bf16[1536,256]{1,0:T(8,128)(2,1)S(1)}, bf16[256,512]{1,0:T(8,128)(...) custom-call(s32[1]{0:T(128)} %bitcast.me_ref, ...), custom_call_target="tpu_custom_call" | custom-call | flops 2147483648 | bytes 33554432 | tf_op jit(solution)/shard_map/pallas_call | solution.py:311
  11.6 0.0 collective-permute-done.even_ref
  11.6 0.0 collective-permute-done.1.odd_ref
  11.7 2.7 %shard_map.132 = (f32[8,3072]{1,0:T(8,128)}, bf16[1536,128]{1,0:T(8,128)(2,1)}) custom-call(s32[1]{0:T(128)} %bitcast.me_ref, f32[8,3072]{1,0:T(8,128)S(1)} %get-tuple-element.21.atm_ref, f32[1,3072]{1,0:T(1,128)S(1)} %get-tuple-element.22.kappa_ref, f32[2,6656]{1,0:T(2,128)S(1)} %collective-permute-done.even_ref, ...), custom_call_target="tpu_custom_call" | custom-call | flops 268435456 | bytes 4194304 | tf_op jit(solution)/shard_map/pallas_call | solution.py:311
  14.4 0.0 copy-start
  14.4 3.2 %copy-done = bf16[256,128,128]{2,1,0:T(8,128)(2,1)} copy-done((bf16[256,128,128]{2,1,0:T(8,128)(2,1)}, bf16[256,128,128]{2,1,0:T(8,128)(2,1)S(1)}, u32[]{:S(2)}) %copy-start) | copy-done | bytes 8388632
  17.6 3.8 %all-to-all-start = ((bf16[16,96,128]{2,1,0:T(8,128)(2,1)}), bf16[16,96,128]{2,1,0:T(8,128)(2,1)S(1)}, u32[]{:S(2)}, u32[]{:S(2)}) async-start(bf16[16,96,128]{2,1,0:T(8,128)(2,1)} %bitcast.8), calls=%async_computation | async-start | bytes 786432 | tf_op jit(solution)/shard_map/all_to_all | solution.py:402
  21.5 0.6 %shard_map.133.free_ref = f32[16,3584]{1,0:T(8,128)S(1)} custom-call(s32[1]{0:T(128)} %bitcast.me_ref, f32[16,3584]{1,0:T(8,128)S(1)} %get-tuple-element.33.ocean_ref, f32[28,128]{1,0:T(8,128)S(1)} %get-tuple-element.34.nu_ref, f32[2,6656]{1,0:T(2,128)S(1)} %collective-permute-done.even_ref, f32[2,6656]{1,0:T(2,128)S(1)} %collective-permute-done.1.odd_ref), custom_call_target="tpu_custom_call" | custom-call | flops 134217728 | bytes 2097152 | tf_op jit(solution)/shard_map/pallas_call | solution.py:311
  22.0 11.6 %all-to-all-done = bf16[16,96,128]{2,1,0:T(8,128)(2,1)S(1)} async-done(((bf16[16,96,128]{2,1,0:T(8,128)(2,1)}), bf16[16,96,128]{2,1,0:T(8,128)(2,1)S(1)}, u32[]{:S(2)}, u32[]{:S(2)}) %all-to-all-start) | async-done | bytes 393248 | tf_op jit(solution)/shard_map/all_to_all | solution.py:402
  33.7 1.3 %shard_map.134 = (f32[16,3584]{1,0:T(8,128)}, bf16[512,128]{1,0:T(8,128)(2,1)S(1)}) custom-call(s32[1]{0:T(128)} %bitcast.me_ref, bf16[1536,128]{1,0:T(8,128)(2,1)S(1)} %bitcast.12, f32[16,3584]{1,0:T(8,128)S(1)} %shard_map.133.free_ref, f32[28,128]{1,0:T(8,128)S(1)} %get-tuple-element.34.nu_ref), custom_call_target="tpu_custom_call" | custom-call | flops 134217728 | bytes 2097152 | tf_op jit(solution)/shard_map/pallas_call | solution.py:311
  34.9 11.2 %all_to_all.22 = bf16[16,32,128]{2,1,0:T(8,128)(2,1)S(1)} all-to-all(bf16[16,32,128]{2,1,0:T(8,128)(2,1)S(1)} %bitcast.14), channel_id=1, replica_groups=mesh['members'=2,'tiles'=16] {'tiles'}, dimensions={0} | all-to-all | bytes 262144 | tf_op jit(solution)/shard_map/all_to_all | solution.py:416
  46.2 0.0 copy-start.1
  46.2 3.4 %copy-done.1 = bf16[256,128,128]{2,1,0:T(8,128)(2,1)S(1)} copy-done((bf16[256,128,128]{2,1,0:T(8,128)(2,1)S(1)}, bf16[256,128,128]{2,1,0:T(8,128)(2,1)}, u32[]{:S(2)}) %copy-start.1) | copy-done | bytes 8388632
  49.6 3.2 %shard_map.135 = f32[8,3072]{1,0:T(8,128)} custom-call(bf16[512,128]{1,0:T(8,128)(2,1)S(1)} %bitcast.13, bf16[256,512]{1,0:T(8,128)(2,1)S(1)} %get-tuple-element.37.sort_ref, bf16[192,256]{1,0:T(8,128)(2,1)S(1)} %get-tuple-element.38.back_ref, bf16[256,128,128]{2,1,0:T(8,128)(2,1)S(1)} %copy-done.1), custom_call_target="tpu_custom_call" | custom-call | flops 268435456 | bytes 4194304 | tf_op jit(solution)/shard_map/pallas_call | solution.py:311
Async XLA Ops:
  1.7 10.0 %collective-permute-start = (f32[2,6656]{1,0:T(2,128)S(1)}, f32[2,6656]{1,0:T(2,128)S(1)}, u32[]{:S(2)}, u32[]{:S(2)}) collective-permute-start(f32[2,6656]{1,0:T(2,128)S(1)} %get-tuple-element.23), channel_id=1, source_target_pairs={{0,1},{1,0},{2,3},{3,2},{4,5},{5,4},{6,7},{7,6},{8,9},{9,8},{10,11... | collective-permute-start | bytes 159752 | tf_op jit(solution)/shard_map/ppermute | solution.py:356
  2.2 9.4 %collective-permute-start.1 = (f32[2,6656]{1,0:T(2,128)S(1)}, f32[2,6656]{1,0:T(2,128)S(1)}, u32[]{:S(2)}, u32[]{:S(2)}) collective-permute-start(f32[2,6656]{1,0:T(2,128)S(1)} %get-tuple-element.24), channel_id=1, source_target_pairs={{1,2},{3,4},{5,6},{7,8},{9,10},{11,12},{13,14},{15,0},{2,1},{4,3},... | collective-permute-start | bytes 159752 | tf_op jit(solution)/shard_map/ppermute | solution.py:355
  14.4 3.2 %copy-start = (bf16[256,128,128]{2,1,0:T(8,128)(2,1)}, bf16[256,128,128]{2,1,0:T(8,128)(2,1)S(1)}, u32[]{:S(2)}) copy-start(bf16[256,128,128]{2,1,0:T(8,128)(2,1)S(1)} %get-tuple-element.30.weight_ref) | copy-start | bytes 25165828
  17.6 16.0 %all-to-all-start = ((bf16[16,96,128]{2,1,0:T(8,128)(2,1)}), bf16[16,96,128]{2,1,0:T(8,128)(2,1)S(1)}, u32[]{:S(2)}, u32[]{:S(2)}) async-start(bf16[16,96,128]{2,1,0:T(8,128)(2,1)} %bitcast.8), calls=%async_computation | async-start | bytes 786432 | tf_op jit(solution)/shard_map/all_to_all | solution.py:402
  46.2 3.4 %copy-start.1 = (bf16[256,128,128]{2,1,0:T(8,128)(2,1)S(1)}, bf16[256,128,128]{2,1,0:T(8,128)(2,1)}, u32[]{:S(2)}) copy-start(bf16[256,128,128]{2,1,0:T(8,128)(2,1)} %copy-done) | copy-start | bytes 25165828

commit v3 on v2

--- a/solution.py
+++ b/solution.py
@@ -10,7 +10,8 @@
 LANE = 128
 EDGE = 32
 CHUNK = 8
-PIECES = 8
+PIECE = 32
+EARLY = 64
 F32 = jnp.float32
 BF16 = jnp.bfloat16
 VMEM = pl.BlockSpec(memory_space=pltpu.VMEM)
@@ -48,6 +49,19 @@
         for k in range(0, width, LANE)
     ]
     return jnp.concatenate(parts, axis=1)
+
+
+def fetches(weight_hbm, first, held, sems):
+    copies = []
+    for n in range(held.shape[0] // PIECE):
+        copies.append(
+            pltpu.make_async_copy(
+                weight_hbm.at[pl.ds(first + n * PIECE, PIECE)],
+                held.at[pl.ds(n * PIECE, PIECE)],
+                sems.at[n],
+            )
+        )
+    return copies
 
 
 def send_kernel(me_ref, atm_hbm, ocean_hbm, atm_ref, ocean_ref, even_ref, odd_ref, sems):
@@ -74,7 +88,7 @@
     weight_hbm,
     pick_ref, back_ref, slots_ref, sort_ref, ids_ref, field_ref, scale_ref, kappa_ref, nu_ref,
     weight_ref,
-    ints, gains, forcing_ref, sems,
+    ints, gains, forcing_ref, sems, weight_sems,
 ):
     small = [
         (src_hbm, ints.at[0]), (own_hbm, ints.at[1]), (dst_hbm, ints.at[2]),
@@ -82,14 +96,7 @@
         (kappa_hbm, kappa_ref), (nu_hbm, nu_ref),
     ]
     copies = [pltpu.make_async_copy(a, b, sems.at[k]) for k, (a, b) in enumerate(small)]
-    share = weight_hbm.shape[0] // PIECES
-    for n in range(PIECES):
-        span = pl.ds(n * share, share)
-        copies.append(
-            pltpu.make_async_copy(
-                weight_hbm.at[span], weight_ref.at[span], sems.at[len(small) + n]
-            )
-        )
+    copies += fetches(weight_hbm, 0, weight_ref, weight_sems)
     for copy in copies:
         copy.start()
     for copy in copies[:3]:
@@ -274,14 +281,32 @@
         return_ref[pl.ds(g * LANE, LANE), :] = picked.astype(BF16)
 
 
-def backward_kernel(came_ref, sort_ref, back_ref, weight_ref, out_ref):
+def fetch_kernel(after_hbm, weight_hbm, weight_ref, sems):
+    copies = fetches(weight_hbm, 0, weight_ref, sems)
+    for copy in copies:
+        copy.start()
+    for copy in copies:
+        copy.wait()
+
+
+def backward_kernel(
+    came_ref, sort_ref, back_ref, early_ref, weight_hbm, out_ref, late_ref, sems
+):
+    early = early_ref.shape[0]
+    copies = fetches(weight_hbm, early, late_ref, sems)
+    for copy in copies:
+        copy.start()
     values = dot(sort_ref[...], came_ref[...])
     blocks = values.shape[0]
     row = iota((CHUNK, LANE), 0)
     parts = []
     for n in range(blocks // CHUNK):
         value = values[n * CHUNK : (n + 1) * CHUNK].astype(BF16)
-        weight = weight_ref[pl.ds(n * CHUNK, CHUNK)].reshape(CHUNK * LANE, LANE)
+        at = n * CHUNK - early
+        if at >= 0 and at % PIECE == 0:
+            copies[at // PIECE].wait()
+        held = early_ref[pl.ds(n * CHUNK, CHUNK)] if at < 0 else late_ref[pl.ds(at, CHUNK)]
+        weight = held.reshape(CHUNK * LANE, LANE)
         full = dot_nt(value, weight)
         part = full[:, :LANE]
         for q in range(1, CHUNK):
@@ -355,6 +380,8 @@
     from_odd = lax.ppermute(to_odd, "tiles", pairs + [(j, i) for i, j in pairs])
     from_even = lax.ppermute(to_even, "tiles", [(i, i ^ 1) for i in range(ntiles)])
     atm_row_tiles = atm_cols // LANE
+    early = min(EARLY, blocks)
+    whole = blocks // PIECE
     nflux = forcing.shape[0]
     pick, back, slots, sort, ids, field, scale, kappa, nu, weight = call(
         functools.partial(
@@ -378,7 +405,8 @@
             pltpu.VMEM((3, 1, blocks), jnp.int32),
             pltpu.VMEM((2, 1, nflux), F32),
             pltpu.VMEM(forcing.shape, BF16),
-            pltpu.SemaphoreType.DMA((8 + PIECES,)),
+            pltpu.SemaphoreType.DMA((8,)),
+            pltpu.SemaphoreType.DMA((whole,)),
         ],
     )(
         me_arr,
@@ -414,12 +442,23 @@
         1 << 27,
     )(me_arr, arrived, free, nu)
     came_back = lax.all_to_all(returned, "tiles", split_axis=0, concat_axis=0, tiled=True)
+    again = call(
+        fetch_kernel,
+        shape((early, LANE, LANE), BF16),
+        [HBM, HBM],
+        1 << 31,
+        [pltpu.SemaphoreType.DMA((early // PIECE,))],
+    )(ocean_next, remap_weight)
     feedback = call(
         backward_kernel,
         shape(atm_state.shape, F32),
-        [VMEM] * 4,
+        [VMEM] * 4 + [HBM],
         1 << 28,
-    )(came_back, sort, back, weight)
+        [
+            pltpu.VMEM((blocks - early, LANE, LANE), BF16),
+            pltpu.SemaphoreType.DMA(((blocks - early) // PIECE,)),
+        ],
+    )(came_back, sort, back, again, remap_weight)
     return (atm_next, ocean_next, feedback)
 
 

time: 53.1 us -> 48.5 us (0.913)
  blocking collectives: 11.2 us -> 0 us
  local copies, waits for them, and re-layouts: 6.61 us -> 0 us
  waiting for transfers between devices: 11.6 us -> 18 us
  starting transfers between devices: 10 us -> 13.6 us
  Pallas kernels: 12.6 us -> 15.8 us
    all_to_all x1 -> x0, blocking collectives: 11.2 us -> none  [per_device(): lax.all_to_all(returned, 'tiles', split_axis=0, concat_axis=0, tiled=True)]
    unnamed x4 -> x0, local copies, waits for them, and re-layouts: 6.61 us -> none
    all_to_all x0 -> x1, waiting for transfers between devices: none -> 6.36 us  [per_device(): lax.all_to_all(returned, 'tiles', split_axis=0, concat_axis=0, tiled=True)]
    all_to_all x0 -> x1, starting transfers between devices: none -> 3.52 us  [per_device(): lax.all_to_all(returned, 'tiles', split_axis=0, concat_axis=0, tiled=True)]
    pallas_call x6 -> x7, Pallas kernels: 12.6 us -> 15.8 us  [placed(): run(*[pltpu.with_memory_space_constraint(x, pltpu.HBM) if spec is HBM els...]
  transfers between devices with their start and end apart: 3 -> 4, of which waited for: 1 -> 2; matrix products, arithmetic and copies ran while one was open for 0% -> 0% of each run, Pallas kernels for 8% -> 12%
where the time goes in v3:
time: 48.5 us; the launch traced here: 48.1 us
  waiting for transfers between devices  18 us (37%)
  Pallas kernels  15.8 us (33%)
  starting transfers between devices  13.6 us (28%)
  between operations  0.7 us (1%)
    pallas_call x7, Pallas kernels, placed(): run(*[pltpu.with_memory_space_constraint(x, pltpu.HBM) if spec is HBM els...  15.8 us
    all_to_all x1, waiting for transfers between devices, per_device(): lax.all_to_all(outgoing, 'tiles', split_axis=0, concat_axis=0, tiled=True)  11.6 us
    all_to_all x1, waiting for transfers between devices, per_device(): lax.all_to_all(returned, 'tiles', split_axis=0, concat_axis=0, tiled=True)  6.36 us
    ppermute x1, starting transfers between devices, per_device(): from_odd = lax.ppermute(to_odd, 'tiles', pairs + [(j, i) for i, j in pairs])  5.67 us
    all_to_all x1, starting transfers between devices, per_device(): lax.all_to_all(outgoing, 'tiles', split_axis=0, concat_axis=0, tiled=True)  3.87 us
    all_to_all x1, starting transfers between devices, per_device(): lax.all_to_all(returned, 'tiles', split_axis=0, concat_axis=0, tiled=True)  3.52 us
  transfers between devices with their start and end apart: 4, of which 2 were waited for; matrix products, arithmetic and copies ran while one was open for 0% of the time, Pallas kernels for 12%

profile of v3, /device:TPU:0, one launch (start us, length us, event | category | flops | bytes accessed | tf_op | source)
XLA Modules:
  0.0 48.1 jit_solution(479837175386262258)
XLA Ops:
  0.6 1.0 %shard_map.130 = (f32[8,3072]{1,0:T(8,128)S(1)}, f32[16,3584]{1,0:T(8,128)S(1)}, f32[2,6656]{1,0:T(2,128)S(1)}, f32[2,6656]{1,0:T(2,128)S(1)}) custom-call(s32[1]{0:T(128)} %bitcast.me_ref, f32[8,3072]{1,0:T(8,128)} %atm_hbm.1, f32[16,3584]{1,0:T(8,128)} %ocean_hbm.1), custom_call_target="tpu_custom_call" | custom-call | flops 1048576 | bytes 16384 | tf_op jit(solution)/shard_map/pallas_call | solution.py:336
  1.7 0.5 %collective-permute-start = (f32[2,6656]{1,0:T(2,128)S(1)}, f32[2,6656]{1,0:T(2,128)S(1)}, u32[]{:S(2)}, u32[]{:S(2)}) collective-permute-start(f32[2,6656]{1,0:T(2,128)S(1)} %get-tuple-element.23), channel_id=1, source_target_pairs={{0,1},{1,0},{2,3},{3,2},{4,5},{5,4},{6,7},{7,6},{8,9},{9,8},{10,11... | collective-permute-start | bytes 159752 | tf_op jit(solution)/shard_map/ppermute | solution.py:381
  2.2 5.7 %collective-permute-start.1 = (f32[2,6656]{1,0:T(2,128)S(1)}, f32[2,6656]{1,0:T(2,128)S(1)}, u32[]{:S(2)}, u32[]{:S(2)}) collective-permute-start(f32[2,6656]{1,0:T(2,128)S(1)} %get-tuple-element.24), channel_id=1, source_target_pairs={{1,2},{3,4},{5,6},{7,8},{9,10},{11,12},{13,14},{15,0},{2,1},{4,3},... | collective-permute-start | bytes 159752 | tf_op jit(solution)/shard_map/ppermute | solution.py:380
  7.9 3.7 %shard_map.131 = (bf16[256,192]{1,0:T(8,128)(2,1)S(1)}, bf16[192,256]{1,0:T(8,128)(2,1)S(1)}, bf16[1536,256]{1,0:T(8,128)(2,1)S(1)}, bf16[256,512]{1,0:T(8,128)(...) custom-call(s32[1]{0:T(128)} %bitcast.me_ref, ...), custom_call_target="tpu_custom_call" | custom-call | flops 2147483648 | bytes 33554432 | tf_op jit(solution)/shard_map/pallas_call | solution.py:336
  11.6 0.0 collective-permute-done.even_ref
  11.6 0.0 collective-permute-done.1.odd_ref
  11.6 2.7 %shard_map.132 = (f32[8,3072]{1,0:T(8,128)}, bf16[1536,128]{1,0:T(8,128)(2,1)}) custom-call(s32[1]{0:T(128)} %bitcast.me_ref, f32[8,3072]{1,0:T(8,128)S(1)} %get-tuple-element.21.atm_ref, f32[1,3072]{1,0:T(1,128)S(1)} %get-tuple-element.22.kappa_ref, f32[2,6656]{1,0:T(2,128)S(1)} %collective-permute-done.even_ref, ...), custom_call_target="tpu_custom_call" | custom-call | flops 268435456 | bytes 4194304 | tf_op jit(solution)/shard_map/pallas_call | solution.py:336
  14.3 3.9 %all-to-all-start = ((bf16[16,96,128]{2,1,0:T(8,128)(2,1)}), bf16[16,96,128]{2,1,0:T(8,128)(2,1)S(1)}, u32[]{:S(2)}, u32[]{:S(2)}) async-start(bf16[16,96,128]{2,1,0:T(8,128)(2,1)} %bitcast.8), calls=%async_computation | async-start | bytes 786432 | tf_op jit(solution)/shard_map/all_to_all | solution.py:430
  18.2 0.6 %shard_map.133.free_ref = f32[16,3584]{1,0:T(8,128)S(1)} custom-call(s32[1]{0:T(128)} %bitcast.me_ref, f32[16,3584]{1,0:T(8,128)S(1)} %get-tuple-element.33.ocean_ref, f32[28,128]{1,0:T(8,128)S(1)} %get-tuple-element.34.nu_ref, f32[2,6656]{1,0:T(2,128)S(1)} %collective-permute-done.even_ref, f32[2,6656]{1,0:T(2,128)S(1)} %collective-permute-done.1.odd_ref), custom_call_target="tpu_custom_call" | custom-call | flops 134217728 | bytes 2097152 | tf_op jit(solution)/shard_map/pallas_call | solution.py:336
  18.7 11.6 %all-to-all-done = bf16[16,96,128]{2,1,0:T(8,128)(2,1)S(1)} async-done(((bf16[16,96,128]{2,1,0:T(8,128)(2,1)}), bf16[16,96,128]{2,1,0:T(8,128)(2,1)S(1)}, u32[]{:S(2)}, u32[]{:S(2)}) %all-to-all-start) | async-done | bytes 393248 | tf_op jit(solution)/shard_map/all_to_all | solution.py:430
  30.4 1.5 %shard_map.134 = (f32[16,3584]{1,0:T(8,128)}, bf16[512,128]{1,0:T(8,128)(2,1)}) custom-call(s32[1]{0:T(128)} %bitcast.me_ref, bf16[1536,128]{1,0:T(8,128)(2,1)S(1)} %bitcast.12, f32[16,3584]{1,0:T(8,128)S(1)} %shard_map.133.free_ref, f32[28,128]{1,0:T(8,128)S(1)} %get-tuple-element.34.nu_ref), custom_call_target="tpu_custom_call" | custom-call | flops 134217728 | bytes 2097152 | tf_op jit(solution)/shard_map/pallas_call | solution.py:336
  31.9 3.5 %all-to-all-start.1 = ((bf16[16,32,128]{2,1,0:T(8,128)(2,1)}), bf16[16,32,128]{2,1,0:T(8,128)(2,1)S(1)}, u32[]{:S(2)}, u32[]{:S(2)}) async-start(bf16[16,32,128]{2,1,0:T(8,128)(2,1)} %bitcast.10), calls=%async_computation.1 | async-start | bytes 262144 | tf_op jit(solution)/shard_map/all_to_all | solution.py:444
  35.5 1.6 %shard_map.135.early_ref = bf16[64,128,128]{2,1,0:T(8,128)(2,1)S(1)} custom-call(f32[16,3584]{1,0:T(8,128)} %get-tuple-element.19.after_hbm, bf16[256,128,128]{2,1,0:T(8,128)(2,1)} %weight_hbm.5), custom_call_target="tpu_custom_call" | custom-call | flops 2147483648 | bytes 33554432 | tf_op jit(solution)/shard_map/pallas_call | solution.py:336
  37.0 6.4 %all-to-all-done.1 = bf16[16,32,128]{2,1,0:T(8,128)(2,1)S(1)} async-done(((bf16[16,32,128]{2,1,0:T(8,128)(2,1)}), bf16[16,32,128]{2,1,0:T(8,128)(2,1)S(1)}, u32[]{:S(2)}, u32[]{:S(2)}) %all-to-all-start.1) | async-done | bytes 131104 | tf_op jit(solution)/shard_map/all_to_all | solution.py:444
  43.4 4.7 %shard_map.136 = f32[8,3072]{1,0:T(8,128)} custom-call(bf16[512,128]{1,0:T(8,128)(2,1)S(1)} %bitcast.13, bf16[256,512]{1,0:T(8,128)(2,1)S(1)} %get-tuple-element.37.sort_ref, bf16[192,256]{1,0:T(8,128)(2,1)S(1)} %get-tuple-element.38.back_ref, bf16[64,128,128]{2,1,0:T(8,128)(2,1)S(1)} %shard_map.135.early_ref, bf16[256,128,128]{2,1,0:T(8,128)(2,1)} %weight_hbm.5), custom_call_target="tpu_custom_call" | custom-call | flops 268435456 | bytes 4194304 | tf_op jit(solution)/shard_map/pallas_call | solution.py:336
Async XLA Ops:
  1.7 9.9 %collective-permute-start = (f32[2,6656]{1,0:T(2,128)S(1)}, f32[2,6656]{1,0:T(2,128)S(1)}, u32[]{:S(2)}, u32[]{:S(2)}) collective-permute-start(f32[2,6656]{1,0:T(2,128)S(1)} %get-tuple-element.23), channel_id=1, source_target_pairs={{0,1},{1,0},{2,3},{3,2},{4,5},{5,4},{6,7},{7,6},{8,9},{9,8},{10,11... | collective-permute-start | bytes 159752 | tf_op jit(solution)/shard_map/ppermute | solution.py:381
  2.2 9.4 %collective-permute-start.1 = (f32[2,6656]{1,0:T(2,128)S(1)}, f32[2,6656]{1,0:T(2,128)S(1)}, u32[]{:S(2)}, u32[]{:S(2)}) collective-permute-start(f32[2,6656]{1,0:T(2,128)S(1)} %get-tuple-element.24), channel_id=1, source_target_pairs={{1,2},{3,4},{5,6},{7,8},{9,10},{11,12},{13,14},{15,0},{2,1},{4,3},... | collective-permute-start | bytes 159752 | tf_op jit(solution)/shard_map/ppermute | solution.py:380
  14.3 16.1 %all-to-all-start = ((bf16[16,96,128]{2,1,0:T(8,128)(2,1)}), bf16[16,96,128]{2,1,0:T(8,128)(2,1)S(1)}, u32[]{:S(2)}, u32[]{:S(2)}) async-start(bf16[16,96,128]{2,1,0:T(8,128)(2,1)} %bitcast.8), calls=%async_computation | async-start | bytes 786432 | tf_op jit(solution)/shard_map/all_to_all | solution.py:430
  31.9 11.5 %all-to-all-start.1 = ((bf16[16,32,128]{2,1,0:T(8,128)(2,1)}), bf16[16,32,128]{2,1,0:T(8,128)(2,1)S(1)}, u32[]{:S(2)}, u32[]{:S(2)}) async-start(bf16[16,32,128]{2,1,0:T(8,128)(2,1)} %bitcast.10), calls=%async_computation.1 | async-start | bytes 262144 | tf_op jit(solution)/shard_map/all_to_all | solution.py:444

commit v4 on v3

--- a/solution.py
+++ b/solution.py
@@ -64,31 +64,33 @@
     return copies
 
 
-def send_kernel(me_ref, atm_hbm, ocean_hbm, atm_ref, ocean_ref, even_ref, odd_ref, sems):
+def edge_rows(upper, atm_ref, ocean_ref, out_ref):
+    start = 0
+    for ref in (atm_ref, ocean_ref):
+        rows, cols = ref.shape
+        first, last = ref[0:2], ref[rows - 2 : rows]
+        out_ref[:, start : start + cols] = jnp.where(upper, last, first)
+        start += cols
+
+
+def send_kernel(me_ref, atm_hbm, ocean_hbm, atm_ref, ocean_ref, odd_ref, sems):
     copies = [
         pltpu.make_async_copy(atm_hbm, atm_ref, sems.at[0]),
         pltpu.make_async_copy(ocean_hbm, ocean_ref, sems.at[1]),
     ]
     for copy in copies:
         copy.start()
-    even = me_ref[0] % 2 == 0
-    start = 0
-    for copy, ref in zip(copies, (atm_ref, ocean_ref)):
+    for copy in copies:
         copy.wait()
-        rows, cols = ref.shape
-        first, last = ref[0:2], ref[rows - 2 : rows]
-        even_ref[:, start : start + cols] = jnp.where(even, last, first)
-        odd_ref[:, start : start + cols] = jnp.where(even, first, last)
-        start += cols
+    edge_rows(me_ref[0] % 2 == 1, atm_ref, ocean_ref, odd_ref)
 
 
 def stage_kernel(
     ntiles, main, atm_rows, atm_row_tiles, ocean_rows, row_tiles,
-    me_ref, src_hbm, own_hbm, dst_hbm, gain_hbm, coef_hbm, kappa_hbm, nu_hbm, forcing_hbm,
-    weight_hbm,
+    me_ref, atm_ref, ocean_ref, src_hbm, own_hbm, dst_hbm, gain_hbm, coef_hbm, kappa_hbm, nu_hbm, forcing_hbm,
     pick_ref, back_ref, slots_ref, sort_ref, ids_ref, field_ref, scale_ref, kappa_ref, nu_ref,
-    weight_ref,
-    ints, gains, forcing_ref, sems, weight_sems,
+    even_ref,
+    ints, gains, forcing_ref, sems,
 ):
     small = [
         (src_hbm, ints.at[0]), (own_hbm, ints.at[1]), (dst_hbm, ints.at[2]),
@@ -96,9 +98,9 @@
         (kappa_hbm, kappa_ref), (nu_hbm, nu_ref),
     ]
     copies = [pltpu.make_async_copy(a, b, sems.at[k]) for k, (a, b) in enumerate(small)]
-    copies += fetches(weight_hbm, 0, weight_ref, weight_sems)
     for copy in copies:
         copy.start()
+    edge_rows(me_ref[0] % 2 == 0, atm_ref, ocean_ref, even_ref)
     for copy in copies[:3]:
         copy.wait()
     rows = main + 2 * EDGE
@@ -139,8 +141,6 @@
     for k in range(forcing_ref.shape[0]):
         field = field + coef[:, k : k + 1] * forcing_ref[k].astype(F32)
     field_ref[...] = field
-    for copy in copies[len(small) :]:
-        copy.wait()
 
 
 def forward_kernel(
@@ -369,21 +369,20 @@
     shape = jax.ShapeDtypeStruct
     me_arr = me.astype(jnp.int32).reshape(1)
     edges = shape((2, atm_cols + ocean_cols), F32)
-    atm, ocean, to_even, to_odd = call(
+    atm, ocean, to_odd = call(
         send_kernel,
-        (shape(atm_state.shape, F32), shape(ocean_state.shape, F32), edges, edges),
+        (shape(atm_state.shape, F32), shape(ocean_state.shape, F32), edges),
         [SMEM, HBM, HBM],
-        1 << 20,
+        1 << 34,
         [pltpu.SemaphoreType.DMA((2,))],
     )(me_arr, atm_state, ocean_state)
     pairs = [(2 * k + 1, (2 * k + 2) % ntiles) for k in range(ntiles // 2)]
     from_odd = lax.ppermute(to_odd, "tiles", pairs + [(j, i) for i, j in pairs])
-    from_even = lax.ppermute(to_even, "tiles", [(i, i ^ 1) for i in range(ntiles)])
     atm_row_tiles = atm_cols // LANE
     early = min(EARLY, blocks)
     whole = blocks // PIECE
     nflux = forcing.shape[0]
-    pick, back, slots, sort, ids, field, scale, kappa, nu, weight = call(
+    pick, back, slots, sort, ids, field, scale, kappa, nu, to_even = call(
         functools.partial(
             stage_kernel, ntiles, main, atm_rows, atm_row_tiles, ocean_rows, row_tiles
         ),
@@ -397,19 +396,20 @@
             shape((1, LANE), F32),
             shape((1, atm_cols), F32),
             shape((row_tiles, LANE), F32),
-            shape(remap_weight.shape, BF16),
+            edges,
         ),
-        [SMEM] + [HBM] * 9,
-        1 << 31,
+        [SMEM, VMEM, VMEM] + [HBM] * 8,
+        1 << 20,
         [
             pltpu.VMEM((3, 1, blocks), jnp.int32),
             pltpu.VMEM((2, 1, nflux), F32),
             pltpu.VMEM(forcing.shape, BF16),
             pltpu.SemaphoreType.DMA((8,)),
-            pltpu.SemaphoreType.DMA((whole,)),
         ],
     )(
         me_arr,
+        atm,
+        ocean,
         remap_source.reshape(1, blocks),
         remap_owner.reshape(1, blocks),
         remap_dest.reshape(1, blocks),
@@ -418,15 +418,15 @@
         atm_kappa.reshape(1, atm_cols),
         ocean_nu.reshape(row_tiles, LANE),
         forcing,
-        remap_weight,
     )
+    from_even = lax.ppermute(to_even, "tiles", [(i, i ^ 1) for i in range(ntiles)])
     atm_next, outgoing = call(
         functools.partial(forward_kernel, ntiles, main),
         (shape(atm_state.shape, F32), shape((ntiles * rows, LANE), BF16)),
         [SMEM] + [VMEM] * 10,
         1 << 28,
         [pltpu.VMEM((2 * atm_rows, atm_cols), F32)],
-    )(me_arr, atm, kappa, from_even, from_odd, field, scale, pick, slots, ids, weight)
+    )(me_arr, atm, kappa, from_even, from_odd, field, scale, pick, slots, ids, remap_weight)
     arrived = lax.all_to_all(outgoing, "tiles", split_axis=0, concat_axis=0, tiled=True)
     free = call(
         functools.partial(free_ocean_kernel, ntiles, atm_cols),

time: 48.5 us -> 48 us (0.990)
  Pallas kernels: 15.8 us -> 13.8 us
  waiting for transfers between devices: 18 us -> 19.2 us
    pallas_call x7, Pallas kernels: 15.8 us -> 13.8 us  [placed(): run(*[pltpu.with_memory_space_constraint(x, pltpu.HBM) if spec is HBM els...]
    ppermute x1, waiting for transfers between devices: 0.01 us -> 1.08 us  [per_device(): lax.ppermute(to_even, 'tiles', [(i, i ^ 1) for i in range(ntiles)])]
    all_to_all x1, starting transfers between devices: 3.87 us -> 4.75 us  [per_device(): lax.all_to_all(outgoing, 'tiles', split_axis=0, concat_axis=0, tiled=True)]
  transfers between devices with their start and end apart: 4 -> 4, of which waited for: 2 -> 4; matrix products, arithmetic and copies ran while one was open for 0% -> 0% of each run, Pallas kernels for 12% -> 8%
where the time goes in v4:
time: 48 us; the launch traced here: 47.6 us
  waiting for transfers between devices  19.2 us (40%)
  starting transfers between devices  13.9 us (29%)
  Pallas kernels  13.8 us (29%)
  between operations  0.7 us (1%)
    pallas_call x7, Pallas kernels, placed(): run(*[pltpu.with_memory_space_constraint(x, pltpu.HBM) if spec is HBM els...  13.8 us
    all_to_all x1, waiting for transfers between devices, per_device(): lax.all_to_all(outgoing, 'tiles', split_axis=0, concat_axis=0, tiled=True)  11.6 us
    all_to_all x1, waiting for transfers between devices, per_device(): lax.all_to_all(returned, 'tiles', split_axis=0, concat_axis=0, tiled=True)  6.36 us
    ppermute x1, starting transfers between devices, per_device(): from_odd = lax.ppermute(to_odd, 'tiles', pairs + [(j, i) for i, j in pairs])  5.51 us
    all_to_all x1, starting transfers between devices, per_device(): lax.all_to_all(outgoing, 'tiles', split_axis=0, concat_axis=0, tiled=True)  4.75 us
    all_to_all x1, starting transfers between devices, per_device(): lax.all_to_all(returned, 'tiles', split_axis=0, concat_axis=0, tiled=True)  3.52 us
    ppermute x1, waiting for transfers between devices, per_device(): lax.ppermute(to_even, 'tiles', [(i, i ^ 1) for i in range(ntiles)])  1.08 us
  transfers between devices with their start and end apart: 4, of which 4 were waited for; matrix products, arithmetic and copies ran while one was open for 0% of the time, Pallas kernels for 8%

profile of v4, /device:TPU:0, one launch (start us, length us, event | category | flops | bytes accessed | tf_op | source)
XLA Modules:
  0.0 47.6 jit_solution(11076429676484659553)
XLA Ops:
  0.6 0.0 copy-start
  0.6 1.2 %shard_map.130 = (f32[8,3072]{1,0:T(8,128)S(1)}, f32[16,3584]{1,0:T(8,128)S(1)}, f32[2,6656]{1,0:T(2,128)S(1)}) custom-call(s32[1]{0:T(128)} %bitcast.me_ref, f32[8,3072]{1,0:T(8,128)} %atm_hbm.1, f32[16,3584]{1,0:T(8,128)} %ocean_hbm.1), custom_call_target="tpu_custom_call" | custom-call | flops 17179869184 | bytes 268435456 | tf_op jit(solution)/shard_map/pallas_call | solution.py:336
  1.8 5.5 %collective-permute-start.1 = (f32[2,6656]{1,0:T(2,128)S(1)}, f32[2,6656]{1,0:T(2,128)S(1)}, u32[]{:S(2)}, u32[]{:S(2)}) collective-permute-start(f32[2,6656]{1,0:T(2,128)S(1)} %get-tuple-element.24), channel_id=1, source_target_pairs={{1,2},{3,4},{5,6},{7,8},{9,10},{11,12},{13,14},{15,0},{2,1},{4,3},... | collective-permute-start | bytes 159752 | tf_op jit(solution)/shard_map/ppermute | solution.py:380
  7.3 1.6 %shard_map.131 = (bf16[256,192]{1,0:T(8,128)(2,1)S(1)}, bf16[192,256]{1,0:T(8,128)(2,1)S(1)}, bf16[1536,256]{1,0:T(8,128)(2,1)S(1)}, bf16[256,512]{1,0:T(8,128)(...) custom-call(s32[1]{0:T(128)} %bitcast.me_ref, ...), custom_call_target="tpu_custom_call" | custom-call | flops 1048576 | bytes 16384 | tf_op jit(solution)/shard_map/pallas_call | solution.py:336
  8.9 0.1 collective-permute-start
  9.0 0.1 collective-permute-done.1.odd_ref
  9.2 1.1 %collective-permute-done.even_ref = f32[2,6656]{1,0:T(2,128)S(1)} collective-permute-done((f32[2,6656]{1,0:T(2,128)S(1)}, f32[2,6656]{1,0:T(2,128)S(1)}, u32[]{:S(2)}, u32[]{:S(2)}) %collective-permute-start) | collective-permute-done | bytes 53280 | tf_op jit(solution)/shard_map/ppermute | solution.py:422
  10.2 0.0 copy-done
  10.2 2.7 %shard_map.132 = (f32[8,3072]{1,0:T(8,128)}, bf16[1536,128]{1,0:T(8,128)(2,1)}) custom-call(s32[1]{0:T(128)} %bitcast.me_ref, f32[8,3072]{1,0:T(8,128)S(1)} %get-tuple-element.20.atm_ref, f32[1,3072]{1,0:T(1,128)S(1)} %get-tuple-element.22.kappa_ref, f32[2,6656]{1,0:T(2,128)S(1)} %collective-permute-done.even_ref, ...), custom_call_target="tpu_custom_call" | custom-call | flops 268435456 | bytes 4194304 | tf_op jit(solution)/shard_map/pallas_call | solution.py:336
  12.9 4.7 %all-to-all-start = ((bf16[16,96,128]{2,1,0:T(8,128)(2,1)}), bf16[16,96,128]{2,1,0:T(8,128)(2,1)S(1)}, u32[]{:S(2)}, u32[]{:S(2)}) async-start(bf16[16,96,128]{2,1,0:T(8,128)(2,1)} %bitcast.8), calls=%async_computation | async-start | bytes 786432 | tf_op jit(solution)/shard_map/all_to_all | solution.py:430
  17.7 0.6 %shard_map.133.free_ref = f32[16,3584]{1,0:T(8,128)S(1)} custom-call(s32[1]{0:T(128)} %bitcast.me_ref, f32[16,3584]{1,0:T(8,128)S(1)} %get-tuple-element.21.ocean_ref, f32[28,128]{1,0:T(8,128)S(1)} %get-tuple-element.32.nu_ref, f32[2,6656]{1,0:T(2,128)S(1)} %collective-permute-done.even_ref, f32[2,6656]{1,0:T(2,128)S(1)} %collective-permute-done.1.odd_ref), custom_call_target="tpu_custom_call" | custom-call | flops 134217728 | bytes 2097152 | tf_op jit(solution)/shard_map/pallas_call | solution.py:336
  18.2 11.6 %all-to-all-done = bf16[16,96,128]{2,1,0:T(8,128)(2,1)S(1)} async-done(((bf16[16,96,128]{2,1,0:T(8,128)(2,1)}), bf16[16,96,128]{2,1,0:T(8,128)(2,1)S(1)}, u32[]{:S(2)}, u32[]{:S(2)}) %all-to-all-start) | async-done | bytes 393248 | tf_op jit(solution)/shard_map/all_to_all | solution.py:430
  29.9 1.5 %shard_map.134 = (f32[16,3584]{1,0:T(8,128)}, bf16[512,128]{1,0:T(8,128)(2,1)}) custom-call(s32[1]{0:T(128)} %bitcast.me_ref, bf16[1536,128]{1,0:T(8,128)(2,1)S(1)} %bitcast.12, f32[16,3584]{1,0:T(8,128)S(1)} %shard_map.133.free_ref, f32[28,128]{1,0:T(8,128)S(1)} %get-tuple-element.32.nu_ref), custom_call_target="tpu_custom_call" | custom-call | flops 134217728 | bytes 2097152 | tf_op jit(solution)/shard_map/pallas_call | solution.py:336
  31.4 3.5 %all-to-all-start.1 = ((bf16[16,32,128]{2,1,0:T(8,128)(2,1)}), bf16[16,32,128]{2,1,0:T(8,128)(2,1)S(1)}, u32[]{:S(2)}, u32[]{:S(2)}) async-start(bf16[16,32,128]{2,1,0:T(8,128)(2,1)} %bitcast.10), calls=%async_computation.1 | async-start | bytes 262144 | tf_op jit(solution)/shard_map/all_to_all | solution.py:444
  35.0 1.6 %shard_map.135.early_ref = bf16[64,128,128]{2,1,0:T(8,128)(2,1)S(1)} custom-call(f32[16,3584]{1,0:T(8,128)} %get-tuple-element.18.after_hbm, bf16[256,128,128]{2,1,0:T(8,128)(2,1)} %weight_hbm.3), custom_call_target="tpu_custom_call" | custom-call | flops 2147483648 | bytes 33554432 | tf_op jit(solution)/shard_map/pallas_call | solution.py:336
  36.5 6.4 %all-to-all-done.1 = bf16[16,32,128]{2,1,0:T(8,128)(2,1)S(1)} async-done(((bf16[16,32,128]{2,1,0:T(8,128)(2,1)}), bf16[16,32,128]{2,1,0:T(8,128)(2,1)S(1)}, u32[]{:S(2)}, u32[]{:S(2)}) %all-to-all-start.1) | async-done | bytes 131104 | tf_op jit(solution)/shard_map/all_to_all | solution.py:444
  42.9 4.7 %shard_map.136 = f32[8,3072]{1,0:T(8,128)} custom-call(bf16[512,128]{1,0:T(8,128)(2,1)S(1)} %bitcast.13, bf16[256,512]{1,0:T(8,128)(2,1)S(1)} %get-tuple-element.35.sort_ref, bf16[192,256]{1,0:T(8,128)(2,1)S(1)} %get-tuple-element.36.back_ref, bf16[64,128,128]{2,1,0:T(8,128)(2,1)S(1)} %shard_map.135.early_ref, bf16[256,128,128]{2,1,0:T(8,128)(2,1)} %weight_hbm.3), custom_call_target="tpu_custom_call" | custom-call | flops 268435456 | bytes 4194304 | tf_op jit(solution)/shard_map/pallas_call | solution.py:336
Async XLA Ops:
  0.6 9.6 %copy-start = (bf16[256,128,128]{2,1,0:T(8,128)(2,1)S(1)}, bf16[256,128,128]{2,1,0:T(8,128)(2,1)}, u32[]{:S(2)}) copy-start(bf16[256,128,128]{2,1,0:T(8,128)(2,1)} %weight_hbm.3) | copy-start | bytes 25165828
  1.8 7.3 %collective-permute-start.1 = (f32[2,6656]{1,0:T(2,128)S(1)}, f32[2,6656]{1,0:T(2,128)S(1)}, u32[]{:S(2)}, u32[]{:S(2)}) collective-permute-start(f32[2,6656]{1,0:T(2,128)S(1)} %get-tuple-element.24), channel_id=1, source_target_pairs={{1,2},{3,4},{5,6},{7,8},{9,10},{11,12},{13,14},{15,0},{2,1},{4,3},... | collective-permute-start | bytes 159752 | tf_op jit(solution)/shard_map/ppermute | solution.py:380
  8.9 1.3 %collective-permute-start = (f32[2,6656]{1,0:T(2,128)S(1)}, f32[2,6656]{1,0:T(2,128)S(1)}, u32[]{:S(2)}, u32[]{:S(2)}) collective-permute-start(f32[2,6656]{1,0:T(2,128)S(1)} %get-tuple-element.23), channel_id=1, source_target_pairs={{0,1},{1,0},{2,3},{3,2},{4,5},{5,4},{6,7},{7,6},{8,9},{9,8},{10,11... | collective-permute-start | bytes 159752 | tf_op jit(solution)/shard_map/ppermute | solution.py:422
  12.9 17.0 %all-to-all-start = ((bf16[16,96,128]{2,1,0:T(8,128)(2,1)}), bf16[16,96,128]{2,1,0:T(8,128)(2,1)S(1)}, u32[]{:S(2)}, u32[]{:S(2)}) async-start(bf16[16,96,128]{2,1,0:T(8,128)(2,1)} %bitcast.8), calls=%async_computation | async-start | bytes 786432 | tf_op jit(solution)/shard_map/all_to_all | solution.py:430
  31.4 11.5 %all-to-all-start.1 = ((bf16[16,32,128]{2,1,0:T(8,128)(2,1)}), bf16[16,32,128]{2,1,0:T(8,128)(2,1)S(1)}, u32[]{:S(2)}, u32[]{:S(2)}) async-start(bf16[16,32,128]{2,1,0:T(8,128)(2,1)} %bitcast.10), calls=%async_computation.1 | async-start | bytes 262144 | tf_op jit(solution)/shard_map/all_to_all | solution.py:444

commit v5 on v4

--- a/solution.py
+++ b/solution.py
@@ -88,7 +88,7 @@
 def stage_kernel(
     ntiles, main, atm_rows, atm_row_tiles, ocean_rows, row_tiles,
     me_ref, atm_ref, ocean_ref, src_hbm, own_hbm, dst_hbm, gain_hbm, coef_hbm, kappa_hbm, nu_hbm, forcing_hbm,
-    pick_ref, back_ref, slots_ref, sort_ref, ids_ref, field_ref, scale_ref, kappa_ref, nu_ref,
+    pick_ref, keys_ref, slots_ref, ids_ref, field_ref, scale_ref, kappa_ref, nu_ref,
     even_ref,
     ints, gains, forcing_ref, sems,
 ):
@@ -103,7 +103,7 @@
     edge_rows(me_ref[0] % 2 == 0, atm_ref, ocean_ref, even_ref)
     for copy in copies[:3]:
         copy.wait()
-    rows = main + 2 * EDGE
+    rows = main + EDGE
     per_lane = LANE // main
     source, owner, dest = ints[0], ints[1], ints[2]
     blocks = owner.shape[1]
@@ -115,18 +115,20 @@
         jnp.where(match, dot(onehot(match), above), 0.0), axis=0, keepdims=True
     ).astype(jnp.int32)
     pick_ref[...] = matches_lane(as_column(source), pick_ref.shape[1])
-    back_ref[...] = onehot(source == iota(back_ref.shape, 0))
-    sort_ref[...] = matches_lane(as_column(owner * main + rank), sort_ref.shape[1])
+    keys_ref[0] = source
+    keys_ref[1] = owner * main + rank
+    odd = owner % 2 == 1
     own_slot = owner * rows + rank
-    low = (row_of == ocean_rows - 1) & (owner < ntiles - 1)
-    low_slot = jnp.where(low, (owner + 1) * rows + main + col_of, -1)
-    high = (row_of == 0) & (owner > 0)
-    high_slot = jnp.where(high, (owner - 1) * rows + main + EDGE + col_of, -1)
+    beside = jnp.where(
+        odd,
+        (row_of - (ocean_rows - 1)) + jnp.where(owner < ntiles - 1, 0, 1),
+        row_of + jnp.where(owner > 0, 0, 1),
+    )
+    side_slot = jnp.where(odd, owner + 1, owner - 1) * rows + main + col_of
+    side_slot = jnp.where(beside == 0, side_slot, -1)
     for t in range(ntiles):
         slot = iota((rows, blocks), 0) + t * rows
-        slots_ref[pl.ds(t * rows, rows), :] = onehot(
-            (slot == own_slot) | (slot == low_slot) | (slot == high_slot)
-        )
+        slots_ref[pl.ds(t * rows, rows), :] = onehot((slot == own_slot) | (slot == side_slot))
     lane_of = rank + (me_ref[0] % per_lane) * main
     place = onehot(lane_of == iota((LANE, blocks), 0))
     ids_ref[0] = dot_nt(jnp.where(match, (col_of + 1).astype(F32), 0.0).astype(BF16), place)
@@ -148,7 +150,7 @@
     pick_ref, slots_ref, ids_ref, weight_ref, next_ref, out_ref, work,
 ):
     atm_rows, cols = atm_ref.shape
-    rows = main + 2 * EDGE
+    rows = main + EDGE
     even = me_ref[0] % 2 == 0
     ev, od = even_ref[:, :cols], odd_ref[:, :cols]
     size = 2 * atm_rows
@@ -185,12 +187,11 @@
     at = iota((EDGE, LANE), 0)
     for t in range(ntiles):
         sent = dot(slots_ref[pl.ds(t * rows, rows), :], contribution)
-        low = sent[main : main + EDGE]
+        low = sent[main:]
         low = jnp.where(at == EDGE - 4, ids_ref[0, t : t + 1, :], low)
         low = jnp.where(at == EDGE - 3, ids_ref[1, t : t + 1, :], low)
         out_ref[pl.ds(t * rows, main), :] = sent[:main].astype(BF16)
         out_ref[pl.ds(t * rows + main, EDGE), :] = low.astype(BF16)
-        out_ref[pl.ds(t * rows + main + EDGE, EDGE), :] = sent[main + EDGE :].astype(BF16)
 
 
 def reverse_lanes(x):
@@ -202,7 +203,11 @@
     return jnp.concatenate(parts[::-1], axis=1)
 
 
-def free_ocean_kernel(ntiles, offset, me_ref, ocean_ref, nu_ref, even_ref, odd_ref, out_ref, work):
+def free_ocean_kernel(
+    ntiles, me_ref, ocean_ref, nu_ref, even_ref, odd_ref, atm_ref, out_ref, next_ref, work
+):
+    next_ref[...] = atm_ref[...]
+    offset = atm_ref.shape[1]
     rows, cols = ocean_ref.shape
     me = me_ref[0]
     even, bottom, top = me % 2 == 0, me == 0, me == ntiles - 1
@@ -228,75 +233,98 @@
     out_ref[...] = x[:rows]
 
 
-def ocean_kernel(ntiles, main, me_ref, arrived_ref, free_ref, nu_ref, next_ref, return_ref):
-    rows, cols = free_ref.shape
-    row_tiles = cols // LANE
+def drive_kernel(ntiles, main, rows, me_ref, arrived_ref, drive_ref, side_ref, keys_ref, pair_ref):
     per_lane = LANE // main
-    step = main + 2 * EDGE
-    total = rows * row_tiles
-    top = me_ref[0] == ntiles - 1
-    groups = ntiles // per_lane
+    step = main + EDGE
+    total = drive_ref.shape[0]
+    row_tiles = total // rows
     drive = jnp.zeros((total, LANE), F32)
-    low = jnp.zeros((EDGE, LANE), F32)
-    high = jnp.zeros((EDGE, LANE), F32)
-    keys = []
-    for g in range(groups):
+    side = jnp.zeros((EDGE, LANE), F32)
+    for g in range(ntiles // per_lane):
         edge = jnp.zeros((EDGE, LANE), F32)
         values = []
         for s in range(g * per_lane, (g + 1) * per_lane):
             values.append(arrived_ref[pl.ds(s * step, main), :])
             edge = edge + arrived_ref[pl.ds(s * step + main, EDGE), :].astype(F32)
-            high = high + arrived_ref[pl.ds(s * step + main + EDGE, EDGE), :].astype(F32)
-        low = low + edge
+        side = side + edge
         key = (edge[EDGE - 4 : EDGE - 3] - 1.0) * rows + edge[EDGE - 3 : EDGE - 2]
         key = key.astype(jnp.int32)
-        keys.append(key)
+        keys_ref[g : g + 1] = key
         drive = drive + dot(
             onehot(key == iota((total, LANE), 0)), jnp.concatenate(values, axis=0)
         )
+    side_ref[...] = side
+    drive_ref[...] = drive
+    even = me_ref[0] % 2 == 0
+    pair_ref[...] = jnp.where(
+        even,
+        drive_ref[pl.ds(rows - 1, row_tiles, stride=rows), :],
+        drive_ref[pl.ds(0, row_tiles, stride=rows), :],
+    )
+
+
+def ocean_kernel(
+    ntiles, me_ref, drive_ref, side_ref, keys_ref, free_ref, nu_ref, value_ref, pick_ref
+):
+    rows, cols = free_ref.shape
+    row_tiles = cols // LANE
+    total = rows * row_tiles
+    even, top = me_ref[0] % 2 == 0, me_ref[0] == ntiles - 1
+    drive, side = drive_ref[...], side_ref[...]
     tile = lambda c: drive[c * rows : (c + 1) * rows]
     spun = [pltpu.roll(tile(c), 1, 1) for c in range(row_tiles)]
     back = [pltpu.roll(tile(c), LANE - 1, 1) for c in range(row_tiles)]
     lane, at = iota((rows, LANE), 1), iota((rows, LANE), 0)
     turned = LANE - 1 - iota((8, LANE), 1)
-    results = []
     for c in range(row_tiles):
         d = tile(c)
         left = jnp.where(lane == 0, spun[c - 1], spun[c])
         right = jnp.where(lane == LANE - 1, back[(c + 1) % row_tiles], back[c])
-        under = jnp.where(at == 0, low[c : c + 1], pltpu.roll(d, 1, 0))
+        under_row = jnp.where(even, side[c : c + 1], 0.0)
+        under = jnp.where(at == 0, under_row, pltpu.roll(d, 1, 0))
         fold = jnp.take_along_axis(tile(row_tiles - 1 - c)[rows - 8 :], turned, axis=1)[7:8]
-        over_row = jnp.where(top, fold, high[c : c + 1])
+        over_row = jnp.where(top, fold, jnp.where(even, 0.0, side[c : c + 1]))
         over = jnp.where(at == rows - 1, over_row, pltpu.roll(d, rows - 1, 0))
-        span = slice(c * LANE, (c + 1) * LANE)
         near = under + over + left + right
-        value = free_ref[:, span] + (2.0 * d + nu_ref[c : c + 1] * (near - 4.0 * d))
-        next_ref[:, span] = value
-        results.append(value.astype(BF16))
-    cells = jnp.concatenate(results, axis=0)
-    for g in range(groups):
-        column = jnp.transpose(jnp.broadcast_to(keys[g], (LANE, LANE)))
+        value_ref[c * rows : (c + 1) * rows] = free_ref[:, c * LANE : (c + 1) * LANE] + (
+            2.0 * d + nu_ref[c : c + 1] * (near - 4.0 * d)
+        )
+    for g in range(keys_ref.shape[0]):
+        column = jnp.transpose(jnp.broadcast_to(keys_ref[g : g + 1], (LANE, LANE)))
         wide = jnp.concatenate([column] * -(-total // LANE), axis=1)[:, :total]
-        picked = dot(onehot(wide == iota((LANE, total), 1)), cells)
-        return_ref[pl.ds(g * LANE, LANE), :] = picked.astype(BF16)
-
-
-def fetch_kernel(after_hbm, weight_hbm, weight_ref, sems):
+        pick_ref[pl.ds(g * LANE, LANE), :] = onehot(wide == iota((LANE, total), 1))
+
+
+def return_kernel(rows, me_ref, value_ref, pick_ref, nu_ref, pair_ref, cells_ref, return_ref):
+    row_tiles = nu_ref.shape[0]
+    even = me_ref[0] % 2 == 0
+    cells_ref[...] = value_ref[...]
+    extra = nu_ref[...] * pair_ref[...]
+    high, low = pl.ds(rows - 1, row_tiles, stride=rows), pl.ds(0, row_tiles, stride=rows)
+    cells_ref[high, :] = cells_ref[high, :] + jnp.where(even, extra, 0.0)
+    cells_ref[low, :] = cells_ref[low, :] + jnp.where(even, 0.0, extra)
+    return_ref[...] = dot(pick_ref[...], cells_ref[...].astype(BF16)).astype(BF16)
+
+
+def fetch_kernel(cells_ref, weight_hbm, next_ref, weight_ref, sems):
     copies = fetches(weight_hbm, 0, weight_ref, sems)
     for copy in copies:
         copy.start()
+    rows = next_ref.shape[0]
+    for c in range(next_ref.shape[1] // LANE):
+        next_ref[:, c * LANE : (c + 1) * LANE] = cells_ref[c * rows : (c + 1) * rows]
     for copy in copies:
         copy.wait()
 
 
 def backward_kernel(
-    came_ref, sort_ref, back_ref, early_ref, weight_hbm, out_ref, late_ref, sems
+    came_ref, keys_ref, early_ref, weight_hbm, out_ref, late_ref, sems
 ):
     early = early_ref.shape[0]
     copies = fetches(weight_hbm, early, late_ref, sems)
     for copy in copies:
         copy.start()
-    values = dot(sort_ref[...], came_ref[...])
+    values = dot(matches_lane(as_column(keys_ref[1]), came_ref.shape[0]), came_ref[...])
     blocks = values.shape[0]
     row = iota((CHUNK, LANE), 0)
     parts = []
@@ -315,8 +343,10 @@
     result = jnp.concatenate(parts, axis=0)
     coarse = result.astype(BF16)
     fine = (result - coarse.astype(F32)).astype(BF16)
-    tiles = dot(back_ref[...], coarse) + dot(back_ref[...], fine)
     rows = out_ref.shape[0]
+    total = rows * out_ref.shape[1] // LANE
+    back = onehot(keys_ref[0] == iota((total, blocks), 0))
+    tiles = dot(back, coarse) + dot(back, fine)
     for c in range(out_ref.shape[1] // LANE):
         out_ref[:, c * LANE : (c + 1) * LANE] = tiles[c * rows : (c + 1) * rows]
 
@@ -361,7 +391,7 @@
     blocks = remap_source.shape[0]
     capacity = max(2, 2 * blocks // ntiles)
     main = -(-capacity // 16) * 16
-    rows = main + 2 * EDGE
+    rows = main + EDGE
     atm_rows, atm_cols = atm_state.shape
     ocean_rows, ocean_cols = ocean_state.shape
     atm_tiles = atm_rows * atm_cols // LANE
@@ -382,15 +412,14 @@
     early = min(EARLY, blocks)
     whole = blocks // PIECE
     nflux = forcing.shape[0]
-    pick, back, slots, sort, ids, field, scale, kappa, nu, to_even = call(
+    pick, keys, slots, ids, field, scale, kappa, nu, to_even = call(
         functools.partial(
             stage_kernel, ntiles, main, atm_rows, atm_row_tiles, ocean_rows, row_tiles
         ),
         (
             shape((blocks, atm_tiles), BF16),
-            shape((atm_tiles, blocks), BF16),
+            shape((2, 1, blocks), jnp.int32),
             shape((ntiles * rows, blocks), BF16),
-            shape((blocks, ntiles * main), BF16),
             shape((2, ntiles, LANE), F32),
             shape(atm_state.shape, F32),
             shape((1, LANE), F32),
@@ -428,38 +457,57 @@
         [pltpu.VMEM((2 * atm_rows, atm_cols), F32)],
     )(me_arr, atm, kappa, from_even, from_odd, field, scale, pick, slots, ids, remap_weight)
     arrived = lax.all_to_all(outgoing, "tiles", split_axis=0, concat_axis=0, tiled=True)
-    free = call(
-        functools.partial(free_ocean_kernel, ntiles, atm_cols),
-        shape(ocean_state.shape, F32),
+    free, atm_out = call(
+        functools.partial(free_ocean_kernel, ntiles),
+        (shape(ocean_state.shape, F32), shape(atm_state.shape, F32)),
+        [SMEM] + [VMEM] * 5,
+        1 << 27,
+        [pltpu.VMEM((ocean_rows + 8, ocean_cols), F32)],
+    )(me_arr, ocean, nu, from_even, from_odd, atm_next)
+    total = ocean_rows * row_tiles
+    drive, side, slot_keys, to_pair = call(
+        functools.partial(drive_kernel, ntiles, main, ocean_rows),
+        (
+            shape((total, LANE), F32),
+            shape((EDGE, LANE), F32),
+            shape((ntiles * main // LANE, LANE), jnp.int32),
+            shape((row_tiles, LANE), F32),
+        ),
+        [SMEM, VMEM],
+        1 << 27,
+    )(me_arr, arrived)
+    from_pair = lax.ppermute(to_pair, "tiles", [(i, i ^ 1) for i in range(ntiles)])
+    value, take = call(
+        functools.partial(ocean_kernel, ntiles),
+        (shape((total, LANE), F32), shape((ntiles * main, total), BF16)),
+        [SMEM] + [VMEM] * 5,
+        1 << 31,
+    )(me_arr, drive, side, slot_keys, free, nu)
+    cells, returned = call(
+        functools.partial(return_kernel, ocean_rows),
+        (shape((total, LANE), F32), shape((ntiles * main, LANE), BF16)),
         [SMEM] + [VMEM] * 4,
         1 << 27,
-        [pltpu.VMEM((ocean_rows + 8, ocean_cols), F32)],
-    )(me_arr, ocean, nu, from_even, from_odd)
-    ocean_next, returned = call(
-        functools.partial(ocean_kernel, ntiles, main),
-        (shape(ocean_state.shape, F32), shape((ntiles * main, LANE), BF16)),
-        [SMEM] + [VMEM] * 3,
-        1 << 27,
-    )(me_arr, arrived, free, nu)
+    )(me_arr, value, take, nu, from_pair)
     came_back = lax.all_to_all(returned, "tiles", split_axis=0, concat_axis=0, tiled=True)
-    again = call(
+    ocean_next, again = call(
         fetch_kernel,
-        shape((early, LANE, LANE), BF16),
-        [HBM, HBM],
+        (shape(ocean_state.shape, F32), shape((early, LANE, LANE), BF16)),
+        [VMEM, HBM],
         1 << 31,
         [pltpu.SemaphoreType.DMA((early // PIECE,))],
-    )(ocean_next, remap_weight)
+    )(cells, remap_weight)
     feedback = call(
         backward_kernel,
         shape(atm_state.shape, F32),
-        [VMEM] * 4 + [HBM],
+        [VMEM] * 3 + [HBM],
         1 << 28,
         [
             pltpu.VMEM((blocks - early, LANE, LANE), BF16),
             pltpu.SemaphoreType.DMA(((blocks - early) // PIECE,)),
         ],
-    )(came_back, sort, back, again, remap_weight)
-    return (atm_next, ocean_next, feedback)
+    )(came_back, keys, again, remap_weight)
+    return (atm_out, ocean_next, feedback)
 
 
 def solution(mesh):

time: 48 us -> 46.7 us (0.973)
  waiting for transfers between devices: 19.2 us -> 16.6 us
  Pallas kernels: 13.8 us -> 14.8 us
    all_to_all x1, waiting for transfers between devices: 11.6 us -> 8.9 us  [per_device(): lax.all_to_all(outgoing, 'tiles', split_axis=0, concat_axis=0, tiled=True)]
    pallas_call x7 -> x9, Pallas kernels: 13.8 us -> 14.8 us  [placed(): run(*[pltpu.with_memory_space_constraint(x, pltpu.HBM) if spec is HBM els...]
    ppermute x0 -> x1, waiting for transfers between devices: none -> 0.8 us  [per_device(): lax.ppermute(to_pair, 'tiles', [(i, i ^ 1) for i in range(ntiles)])]
    all_to_all x1, waiting for transfers between devices: 6.36 us -> 5.64 us  [per_device(): lax.all_to_all(returned, 'tiles', split_axis=0, concat_axis=0, tiled=True)]
  transfers between devices with their start and end apart: 4 -> 5, of which waited for: 4 -> 5; matrix products, arithmetic and copies ran while one was open for 0% -> 0% of each run, Pallas kernels for 8% -> 11%
where the time goes in v5:
time: 46.7 us; the launch traced here: 46.3 us
  waiting for transfers between devices  16.6 us (36%)
  Pallas kernels  14.8 us (32%)
  starting transfers between devices  14.2 us (30%)
  between operations  0.72 us (2%)
    pallas_call x9, Pallas kernels, placed(): run(*[pltpu.with_memory_space_constraint(x, pltpu.HBM) if spec is HBM els...  14.8 us
    all_to_all x1, waiting for transfers between devices, per_device(): lax.all_to_all(outgoing, 'tiles', split_axis=0, concat_axis=0, tiled=True)  8.9 us
    all_to_all x1, waiting for transfers between devices, per_device(): lax.all_to_all(returned, 'tiles', split_axis=0, concat_axis=0, tiled=True)  5.64 us
    ppermute x1, starting transfers between devices, per_device(): from_odd = lax.ppermute(to_odd, 'tiles', pairs + [(j, i) for i, j in pairs])  5.51 us
    all_to_all x1, starting transfers between devices, per_device(): lax.all_to_all(outgoing, 'tiles', split_axis=0, concat_axis=0, tiled=True)  5.03 us
    all_to_all x1, starting transfers between devices, per_device(): lax.all_to_all(returned, 'tiles', split_axis=0, concat_axis=0, tiled=True)  3.51 us
  transfers between devices with their start and end apart: 5, of which 5 were waited for; matrix products, arithmetic and copies ran while one was open for 0% of the time, Pallas kernels for 11%

profile of v5, /device:TPU:0, one launch (start us, length us, event | category | flops | bytes accessed | tf_op | source)
XLA Modules:
  0.0 46.3 jit_solution(528267922621725910)
XLA Ops:
  0.6 0.0 copy-start
  0.6 1.2 %shard_map.130 = (f32[8,3072]{1,0:T(8,128)S(1)}, f32[16,3584]{1,0:T(8,128)S(1)}, f32[2,6656]{1,0:T(2,128)S(1)}) custom-call(s32[1]{0:T(128)} %bitcast.me_ref, f32[8,3072]{1,0:T(8,128)} %atm_hbm.1, f32[16,3584]{1,0:T(8,128)} %ocean_hbm.1), custom_call_target="tpu_custom_call" | custom-call | flops 17179869184 | bytes 268435456 | tf_op jit(solution)/shard_map/pallas_call | solution.py:366
  1.8 5.5 %collective-permute-start.1 = (f32[2,6656]{1,0:T(2,128)S(1)}, f32[2,6656]{1,0:T(2,128)S(1)}, u32[]{:S(2)}, u32[]{:S(2)}) collective-permute-start(f32[2,6656]{1,0:T(2,128)S(1)} %get-tuple-element.33), channel_id=1, source_target_pairs={{1,2},{3,4},{5,6},{7,8},{9,10},{11,12},{13,14},{15,0},{2,1},{4,3},... | collective-permute-start | bytes 159752 | tf_op jit(solution)/shard_map/ppermute | solution.py:410
  7.3 1.3 %shard_map.131 = (bf16[256,192]{1,0:T(8,128)(2,1)S(1)}, s32[2,1,256]{2,1,0:T(1,128)S(1)}, bf16[1024,256]{1,0:T(8,128)(2,1)S(1)}, f32[2,16,128]{2,1,0:T(8,128)S(1...) custom-call(s32[1]{0:T(128)} %bitcast.me_ref, ...), custom_call_target="tpu_custom_call" | custom-call | flops 1048576 | bytes 16384 | tf_op jit(solution)/shard_map/pallas_call | solution.py:366
  8.7 0.1 collective-permute-start
  8.7 0.4 collective-permute-done.1.odd_ref
  9.2 0.8 %collective-permute-done.even_ref = f32[2,6656]{1,0:T(2,128)S(1)} collective-permute-done((f32[2,6656]{1,0:T(2,128)S(1)}, f32[2,6656]{1,0:T(2,128)S(1)}, u32[]{:S(2)}, u32[]{:S(2)}) %collective-permute-start) | collective-permute-done | bytes 53280 | tf_op jit(solution)/shard_map/ppermute | solution.py:451
  10.0 0.0 copy-done
  10.0 2.6 %shard_map.132 = (f32[8,3072]{1,0:T(8,128)S(1)}, bf16[1024,128]{1,0:T(8,128)(2,1)}) custom-call(s32[1]{0:T(128)} %bitcast.me_ref, f32[8,3072]{1,0:T(8,128)S(1)} %get-tuple-element.30.atm_ref, f32[1,3072]{1,0:T(1,128)S(1)} %get-tuple-element.34.kappa_ref, f32[2,6656]{1,0:T(2,128)S(1)} %collective-permute-done.even_ref, ...), custom_call_target="tpu_custom_call" | custom-call | flops 268435456 | bytes 4194304 | tf_op jit(solution)/shard_map/pallas_call | solution.py:366
  12.5 5.0 %all-to-all-start = ((bf16[16,64,128]{2,1,0:T(8,128)(2,1)}), bf16[16,64,128]{2,1,0:T(8,128)(2,1)S(1)}, u32[]{:S(2)}, u32[]{:S(2)}) async-start(bf16[16,64,128]{2,1,0:T(8,128)(2,1)} %bitcast.8), calls=%async_computation | async-start | bytes 524288 | tf_op jit(solution)/shard_map/all_to_all | solution.py:459
  17.6 1.1 %shard_map.133 = (f32[16,3584]{1,0:T(8,128)S(1)}, f32[8,3072]{1,0:T(8,128)}) custom-call(s32[1]{0:T(128)} %bitcast.me_ref, f32[16,3584]{1,0:T(8,128)S(1)} %get-tuple-element.29.ocean_ref, f32[28,128]{1,0:T(8,128)S(1)} %get-tuple-element.31.nu_ref, f32[2,6656]{1,0:T(2,128)S(1)} %collective-permute-done.even_ref, ...), custom_call_target="tpu_custom_call" | custom-call | flops 134217728 | bytes 2097152 | tf_op jit(solution)/shard_map/pallas_call | solution.py:366
  18.7 8.9 %all-to-all-done = bf16[16,64,128]{2,1,0:T(8,128)(2,1)S(1)} async-done(((bf16[16,64,128]{2,1,0:T(8,128)(2,1)}), bf16[16,64,128]{2,1,0:T(8,128)(2,1)S(1)}, u32[]{:S(2)}, u32[]{:S(2)}) %all-to-all-start) | async-done | bytes 262176 | tf_op jit(solution)/shard_map/all_to_all | solution.py:459
  27.6 0.3 shard_map.134
  28.0 0.1 collective-permute-start.2
  28.0 0.4 shard_map.135
  28.4 0.8 %collective-permute-done.2.pair_ref = f32[28,128]{1,0:T(8,128)S(1)} collective-permute-done((f32[28,128]{1,0:T(8,128)S(1)}, f32[28,128]{1,0:T(8,128)S(1)}, u32[]{:S(2)}, u32[]{:S(2)}) %collective-permute-start.2) | collective-permute-done | bytes 14368 | tf_op jit(solution)/shard_map/ppermute | solution.py:479
  29.2 1.0 %shard_map.136 = (f32[448,128]{1,0:T(8,128)S(1)}, bf16[512,128]{1,0:T(8,128)(2,1)}) custom-call(s32[1]{0:T(128)} %bitcast.me_ref, f32[448,128]{1,0:T(8,128)S(1)} %get-tuple-element.47.value_ref, bf16[512,448]{1,0:T(8,128)(2,1)S(1)} %get-tuple-element.48.pick_ref, f32[28,128]{1,0:T(8,128)S(1)} %get-tuple-element.31.nu_ref, ...), custom_call_target="tpu_custom_call" | custom-call | flops 134217728 | bytes 2097152 | tf_op jit(solution)/shard_map/pallas_call | solution.py:366
  30.2 3.5 %all-to-all-start.1 = ((bf16[16,32,128]{2,1,0:T(8,128)(2,1)}), bf16[16,32,128]{2,1,0:T(8,128)(2,1)S(1)}, u32[]{:S(2)}, u32[]{:S(2)}) async-start(bf16[16,32,128]{2,1,0:T(8,128)(2,1)} %bitcast.10), calls=%async_computation.1 | async-start | bytes 262144 | tf_op jit(solution)/shard_map/all_to_all | solution.py:492
  33.7 2.2 %shard_map.137 = (f32[16,3584]{1,0:T(8,128)}, bf16[64,128,128]{2,1,0:T(8,128)(2,1)S(1)}) custom-call(f32[448,128]{1,0:T(8,128)S(1)} %get-tuple-element.50.cells_ref, bf16[256,128,128]{2,1,0:T(8,128)(2,1)} %weight_hbm.3), custom_call_target="tpu_custom_call" | custom-call | flops 2147483648 | bytes 33554432 | tf_op jit(solution)/shard_map/pallas_call | solution.py:366
  36.0 5.6 %all-to-all-done.1 = bf16[16,32,128]{2,1,0:T(8,128)(2,1)S(1)} async-done(((bf16[16,32,128]{2,1,0:T(8,128)(2,1)}), bf16[16,32,128]{2,1,0:T(8,128)(2,1)S(1)}, u32[]{:S(2)}, u32[]{:S(2)}) %all-to-all-start.1) | async-done | bytes 131104 | tf_op jit(solution)/shard_map/all_to_all | solution.py:492
  41.6 4.7 %shard_map.138 = f32[8,3072]{1,0:T(8,128)} custom-call(bf16[512,128]{1,0:T(8,128)(2,1)S(1)} %bitcast.12, s32[2,1,256]{2,1,0:T(1,128)S(1)} %get-tuple-element.53.keys_ref, bf16[64,128,128]{2,1,0:T(8,128)(2,1)S(1)} %get-tuple-element.54.early_ref, bf16[256,128,128]{2,1,0:T(8,128)(2,1)} %weight_hbm.3), custom_call_target="tpu_custom_call" | custom-call | flops 268435456 | bytes 4194304 | tf_op jit(solution)/shard_map/pallas_call | solution.py:366
Async XLA Ops:
  0.6 9.3 %copy-start = (bf16[256,128,128]{2,1,0:T(8,128)(2,1)S(1)}, bf16[256,128,128]{2,1,0:T(8,128)(2,1)}, u32[]{:S(2)}) copy-start(bf16[256,128,128]{2,1,0:T(8,128)(2,1)} %weight_hbm.3) | copy-start | bytes 25165828
  1.8 7.3 %collective-permute-start.1 = (f32[2,6656]{1,0:T(2,128)S(1)}, f32[2,6656]{1,0:T(2,128)S(1)}, u32[]{:S(2)}, u32[]{:S(2)}) collective-permute-start(f32[2,6656]{1,0:T(2,128)S(1)} %get-tuple-element.33), channel_id=1, source_target_pairs={{1,2},{3,4},{5,6},{7,8},{9,10},{11,12},{13,14},{15,0},{2,1},{4,3},... | collective-permute-start | bytes 159752 | tf_op jit(solution)/shard_map/ppermute | solution.py:410
  8.7 1.3 %collective-permute-start = (f32[2,6656]{1,0:T(2,128)S(1)}, f32[2,6656]{1,0:T(2,128)S(1)}, u32[]{:S(2)}, u32[]{:S(2)}) collective-permute-start(f32[2,6656]{1,0:T(2,128)S(1)} %get-tuple-element.32), channel_id=1, source_target_pairs={{0,1},{1,0},{2,3},{3,2},{4,5},{5,4},{6,7},{7,6},{8,9},{9,8},{10,11... | collective-permute-start | bytes 159752 | tf_op jit(solution)/shard_map/ppermute | solution.py:451
  12.5 15.1 %all-to-all-start = ((bf16[16,64,128]{2,1,0:T(8,128)(2,1)}), bf16[16,64,128]{2,1,0:T(8,128)(2,1)S(1)}, u32[]{:S(2)}, u32[]{:S(2)}) async-start(bf16[16,64,128]{2,1,0:T(8,128)(2,1)} %bitcast.8), calls=%async_computation | async-start | bytes 524288 | tf_op jit(solution)/shard_map/all_to_all | solution.py:459
  28.0 1.2 %collective-permute-start.2 = (f32[28,128]{1,0:T(8,128)S(1)}, f32[28,128]{1,0:T(8,128)S(1)}, u32[]{:S(2)}, u32[]{:S(2)}) collective-permute-start(f32[28,128]{1,0:T(8,128)S(1)} %get-tuple-element.49), channel_id=1, source_target_pairs={{0,1},{1,0},{2,3},{3,2},{4,5},{5,4},{6,7},{7,6},{8,9},{9,8},{10,11... | collective-permute-start | bytes 43016 | tf_op jit(solution)/shard_map/ppermute | solution.py:479
  30.2 11.4 %all-to-all-start.1 = ((bf16[16,32,128]{2,1,0:T(8,128)(2,1)}), bf16[16,32,128]{2,1,0:T(8,128)(2,1)S(1)}, u32[]{:S(2)}, u32[]{:S(2)}) async-start(bf16[16,32,128]{2,1,0:T(8,128)(2,1)} %bitcast.10), calls=%async_computation.1 | async-start | bytes 262144 | tf_op jit(solution)/shard_map/all_to_all | solution.py:492

commit v6 on v5

--- a/solution.py
+++ b/solution.py
@@ -11,7 +11,7 @@
 EDGE = 32
 CHUNK = 8
 PIECE = 32
-EARLY = 64
+EARLY = 96
 F32 = jnp.float32
 BF16 = jnp.bfloat16
 VMEM = pl.BlockSpec(memory_space=pltpu.VMEM)
@@ -203,13 +203,9 @@
     return jnp.concatenate(parts[::-1], axis=1)
 
 
-def free_ocean_kernel(
-    ntiles, me_ref, ocean_ref, nu_ref, even_ref, odd_ref, atm_ref, out_ref, next_ref, work
-):
-    next_ref[...] = atm_ref[...]
-    offset = atm_ref.shape[1]
+def free_ocean(ntiles, me, ocean_ref, nu_ref, even_ref, odd_ref, work):
     rows, cols = ocean_ref.shape
-    me = me_ref[0]
+    offset = even_ref.shape[1] - cols
     even, bottom, top = me % 2 == 0, me == 0, me == ntiles - 1
     ev, od = even_ref[:, offset:], odd_ref[:, offset:]
     size = rows + 8
@@ -230,7 +226,7 @@
         )
         x = x + nu * (near - 4.0 * x)
         x = jnp.where(bottom & (at >= rows + 4), 0.0, x)
-    out_ref[...] = x[:rows]
+    return x[:rows]
 
 
 def drive_kernel(ntiles, main, rows, me_ref, arrived_ref, drive_ref, side_ref, keys_ref, pair_ref):
@@ -264,9 +260,11 @@
 
 
 def ocean_kernel(
-    ntiles, me_ref, drive_ref, side_ref, keys_ref, free_ref, nu_ref, value_ref, pick_ref
+    ntiles, me_ref, drive_ref, side_ref, keys_ref, ocean_ref, nu_ref, even_ref, odd_ref,
+    value_ref, pick_ref, work,
 ):
-    rows, cols = free_ref.shape
+    rows, cols = ocean_ref.shape
+    free = free_ocean(ntiles, me_ref[0], ocean_ref, nu_ref, even_ref, odd_ref, work)
     row_tiles = cols // LANE
     total = rows * row_tiles
     even, top = me_ref[0] % 2 == 0, me_ref[0] == ntiles - 1
@@ -286,7 +284,7 @@
         over_row = jnp.where(top, fold, jnp.where(even, 0.0, side[c : c + 1]))
         over = jnp.where(at == rows - 1, over_row, pltpu.roll(d, rows - 1, 0))
         near = under + over + left + right
-        value_ref[c * rows : (c + 1) * rows] = free_ref[:, c * LANE : (c + 1) * LANE] + (
+        value_ref[c * rows : (c + 1) * rows] = free[:, c * LANE : (c + 1) * LANE] + (
             2.0 * d + nu_ref[c : c + 1] * (near - 4.0 * d)
         )
     for g in range(keys_ref.shape[0]):
@@ -306,7 +304,8 @@
     return_ref[...] = dot(pick_ref[...], cells_ref[...].astype(BF16)).astype(BF16)
 
 
-def fetch_kernel(cells_ref, weight_hbm, next_ref, weight_ref, sems):
+def fetch_kernel(cells_ref, atm_ref, weight_hbm, next_ref, atm_out, weight_ref, sems):
+    atm_out[...] = atm_ref[...]
     copies = fetches(weight_hbm, 0, weight_ref, sems)
     for copy in copies:
         copy.start()
@@ -457,13 +456,6 @@
         [pltpu.VMEM((2 * atm_rows, atm_cols), F32)],
     )(me_arr, atm, kappa, from_even, from_odd, field, scale, pick, slots, ids, remap_weight)
     arrived = lax.all_to_all(outgoing, "tiles", split_axis=0, concat_axis=0, tiled=True)
-    free, atm_out = call(
-        functools.partial(free_ocean_kernel, ntiles),
-        (shape(ocean_state.shape, F32), shape(atm_state.shape, F32)),
-        [SMEM] + [VMEM] * 5,
-        1 << 27,
-        [pltpu.VMEM((ocean_rows + 8, ocean_cols), F32)],
-    )(me_arr, ocean, nu, from_even, from_odd, atm_next)
     total = ocean_rows * row_tiles
     drive, side, slot_keys, to_pair = call(
         functools.partial(drive_kernel, ntiles, main, ocean_rows),
@@ -480,9 +472,10 @@
     value, take = call(
         functools.partial(ocean_kernel, ntiles),
         (shape((total, LANE), F32), shape((ntiles * main, total), BF16)),
-        [SMEM] + [VMEM] * 5,
+        [SMEM] + [VMEM] * 7,
         1 << 31,
-    )(me_arr, drive, side, slot_keys, free, nu)
+        [pltpu.VMEM((ocean_rows + 8, ocean_cols), F32)],
+    )(me_arr, drive, side, slot_keys, ocean, nu, from_even, from_odd)
     cells, returned = call(
         functools.partial(return_kernel, ocean_rows),
         (shape((total, LANE), F32), shape((ntiles * main, LANE), BF16)),
@@ -490,13 +483,17 @@
         1 << 27,
     )(me_arr, value, take, nu, from_pair)
     came_back = lax.all_to_all(returned, "tiles", split_axis=0, concat_axis=0, tiled=True)
-    ocean_next, again = call(
+    ocean_next, atm_out, again = call(
         fetch_kernel,
-        (shape(ocean_state.shape, F32), shape((early, LANE, LANE), BF16)),
-        [VMEM, HBM],
+        (
+            shape(ocean_state.shape, F32),
+            shape(atm_state.shape, F32),
+            shape((early, LANE, LANE), BF16),
+        ),
+        [VMEM, VMEM, HBM],
         1 << 31,
         [pltpu.SemaphoreType.DMA((early // PIECE,))],
-    )(cells, remap_weight)
+    )(cells, atm_next, remap_weight)
     feedback = call(
         backward_kernel,
         shape(atm_state.shape, F32),

time: 46.7 us -> 45.4 us (0.972)
  blocking collectives: 0 us -> 14.9 us
  waiting for transfers between devices: 16.6 us -> 5.91 us
  starting transfers between devices: 14.2 us -> 9.16 us
  Pallas kernels: 14.8 us -> 13.5 us
  local copies, waits for them, and re-layouts: 0.01 us -> 0.9 us
    all_to_all x0 -> x1, blocking collectives: none -> 14.9 us  [per_device(): lax.all_to_all(outgoing, 'tiles', split_axis=0, concat_axis=0, tiled=True)]
    all_to_all x1 -> x0, waiting for transfers between devices: 8.9 us -> none  [per_device(): lax.all_to_all(outgoing, 'tiles', split_axis=0, concat_axis=0, tiled=True)]
    all_to_all x1 -> x0, starting transfers between devices: 5.03 us -> none  [per_device(): lax.all_to_all(outgoing, 'tiles', split_axis=0, concat_axis=0, tiled=True)]
    pallas_call x9 -> x8, Pallas kernels: 14.8 us -> 13.5 us  [placed(): run(*[pltpu.with_memory_space_constraint(x, pltpu.HBM) if spec is HBM els...]
    all_to_all x1, waiting for transfers between devices: 5.64 us -> 4.4 us  [per_device(): lax.all_to_all(returned, 'tiles', split_axis=0, concat_axis=0, tiled=True)]
    unnamed x2 -> x6, local copies, waits for them, and re-layouts: 0.01 us -> 0.9 us
    ppermute x1, waiting for transfers between devices: 0.8 us -> 0.3 us  [per_device(): lax.ppermute(to_pair, 'tiles', [(i, i ^ 1) for i in range(ntiles)])]
  transfers between devices with their start and end apart: 5 -> 4, of which waited for: 5 -> 4; matrix products, arithmetic and copies ran while one was open for 0% -> 0% of each run, Pallas kernels for 11% -> 11%
where the time goes in v6:
time: 45.4 us; the launch traced here: 45.1 us
  blocking collectives  14.9 us (33%)
  Pallas kernels  13.5 us (30%)
  starting transfers between devices  9.16 us (20%)
  waiting for transfers between devices  5.91 us (13%)
  local copies, waits for them, and re-layouts  0.9 us (2%)
  between operations  0.73 us (2%)
    all_to_all x1, blocking collectives, per_device(): lax.all_to_all(outgoing, 'tiles', split_axis=0, concat_axis=0, tiled=True)  14.9 us
    pallas_call x8, Pallas kernels, placed(): run(*[pltpu.with_memory_space_constraint(x, pltpu.HBM) if spec is HBM els...  13.5 us
    ppermute x1, starting transfers between devices, per_device(): from_odd = lax.ppermute(to_odd, 'tiles', pairs + [(j, i) for i, j in pairs])  5.51 us
    all_to_all x1, waiting for transfers between devices, per_device(): lax.all_to_all(returned, 'tiles', split_axis=0, concat_axis=0, tiled=True)  4.4 us
    all_to_all x1, starting transfers between devices, per_device(): lax.all_to_all(returned, 'tiles', split_axis=0, concat_axis=0, tiled=True)  3.51 us
  transfers between devices with their start and end apart: 4, of which 4 were waited for; matrix products, arithmetic and copies ran while one was open for 0% of the time, Pallas kernels for 11%

profile of v6, /device:TPU:0, one launch (start us, length us, event | category | flops | bytes accessed | tf_op | source)
XLA Modules:
  0.0 45.1 jit_solution(16390963668478541293)
XLA Ops:
  0.6 0.0 copy-start
  0.6 1.2 %shard_map.130 = (f32[8,3072]{1,0:T(8,128)S(1)}, f32[16,3584]{1,0:T(8,128)S(1)}, f32[2,6656]{1,0:T(2,128)S(1)}) custom-call(s32[1]{0:T(128)} %bitcast.me_ref, f32[8,3072]{1,0:T(8,128)} %atm_hbm.1, f32[16,3584]{1,0:T(8,128)} %ocean_hbm.1), custom_call_target="tpu_custom_call" | custom-call | flops 17179869184 | bytes 268435456 | tf_op jit(solution)/shard_map/pallas_call | solution.py:365
  1.8 5.5 %collective-permute-start.1 = (f32[2,6656]{1,0:T(2,128)S(1)}, f32[2,6656]{1,0:T(2,128)S(1)}, u32[]{:S(2)}, u32[]{:S(2)}) collective-permute-start(f32[2,6656]{1,0:T(2,128)S(1)} %get-tuple-element.32), channel_id=1, source_target_pairs={{1,2},{3,4},{5,6},{7,8},{9,10},{11,12},{13,14},{15,0},{2,1},{4,3},... | collective-permute-start | bytes 159752 | tf_op jit(solution)/shard_map/ppermute | solution.py:409
  7.3 1.3 %shard_map.131 = (bf16[256,192]{1,0:T(8,128)(2,1)S(1)}, s32[2,1,256]{2,1,0:T(1,128)S(1)}, bf16[1024,256]{1,0:T(8,128)(2,1)S(1)}, f32[2,16,128]{2,1,0:T(8,128)S(1...) custom-call(s32[1]{0:T(128)} %bitcast.me_ref, ...), custom_call_target="tpu_custom_call" | custom-call | flops 1048576 | bytes 16384 | tf_op jit(solution)/shard_map/pallas_call | solution.py:365
  8.7 0.1 collective-permute-start
  8.7 0.4 collective-permute-done.1.odd_ref
  9.2 0.8 %collective-permute-done.even_ref = f32[2,6656]{1,0:T(2,128)S(1)} collective-permute-done((f32[2,6656]{1,0:T(2,128)S(1)}, f32[2,6656]{1,0:T(2,128)S(1)}, u32[]{:S(2)}, u32[]{:S(2)}) %collective-permute-start) | collective-permute-done | bytes 53280 | tf_op jit(solution)/shard_map/ppermute | solution.py:450
  10.0 0.0 copy-done
  10.0 1.9 %shard_map.132 = (f32[8,3072]{1,0:T(8,128)S(1)}, bf16[1024,128]{1,0:T(8,128)(2,1)S(1)}) custom-call(s32[1]{0:T(128)} %bitcast.me_ref, f32[8,3072]{1,0:T(8,128)S(1)} %get-tuple-element.28.atm_ref, f32[1,3072]{1,0:T(1,128)S(1)} %get-tuple-element.30.kappa_ref, f32[2,6656]{1,0:T(2,128)S(1)} %collective-permute-done.even_ref, ...), custom_call_target="tpu_custom_call" | custom-call | flops 268435456 | bytes 4194304 | tf_op jit(solution)/shard_map/pallas_call | solution.py:365
  11.8 0.0 copy-start.1
  11.9 14.9 %all_to_all.22 = bf16[16,64,128]{2,1,0:T(8,128)(2,1)S(1)} all-to-all(bf16[16,64,128]{2,1,0:T(8,128)(2,1)S(1)} %bitcast.13), channel_id=1, replica_groups=mesh['members'=2,'tiles'=16] {'tiles'}, dimensions={0} | all-to-all | bytes 524288 | tf_op jit(solution)/shard_map/all_to_all | solution.py:458
  26.7 0.3 shard_map.133
  27.1 0.1 collective-permute-start.2
  27.1 0.9 %shard_map.134 = (f32[448,128]{1,0:T(8,128)S(1)}, bf16[512,448]{1,0:T(8,128)(2,1)S(1)}) custom-call(s32[1]{0:T(128)} %bitcast.me_ref, f32[448,128]{1,0:T(8,128)S(1)} %get-tuple-element.39.drive_ref, f32[32,128]{1,0:T(8,128)S(1)} %get-tuple-element.40.side_ref, s32[4,128]{1,0:T(4,128)S(1)} %get-tuple-element.41.keys_ref, ...), custom_call_target="tpu_custom_call" | custom-call | flops 2147483648 | bytes 33554432 | tf_op jit(solution)/shard_map/pallas_call | solution.py:365
  28.0 0.3 collective-permute-done.2.pair_ref
  28.3 0.0 copy-done.1
  28.3 1.0 %shard_map.135 = (f32[448,128]{1,0:T(8,128)S(1)}, bf16[512,128]{1,0:T(8,128)(2,1)}) custom-call(s32[1]{0:T(128)} %bitcast.me_ref, f32[448,128]{1,0:T(8,128)S(1)} %get-tuple-element.43.value_ref, bf16[512,448]{1,0:T(8,128)(2,1)S(1)} %get-tuple-element.44.pick_ref, f32[28,128]{1,0:T(8,128)S(1)} %get-tuple-element.42.nu_ref, ...), custom_call_target="tpu_custom_call" | custom-call | flops 134217728 | bytes 2097152 | tf_op jit(solution)/shard_map/pallas_call | solution.py:365
  29.3 3.5 %all-to-all-start.1 = ((bf16[16,32,128]{2,1,0:T(8,128)(2,1)}), bf16[16,32,128]{2,1,0:T(8,128)(2,1)S(1)}, u32[]{:S(2)}, u32[]{:S(2)}) async-start(bf16[16,32,128]{2,1,0:T(8,128)(2,1)} %bitcast.10), calls=%async_computation.1 | async-start | bytes 262144 | tf_op jit(solution)/shard_map/all_to_all | solution.py:485
  32.8 0.0 copy-start.2
  32.8 0.9 %copy-done.2 = f32[8,3072]{1,0:T(8,128)S(1)} copy-done((f32[8,3072]{1,0:T(8,128)S(1)}, f32[8,3072]{1,0:T(8,128)}, u32[]{:S(2)}) %copy-start.2) | copy-done | bytes 98328
  33.7 2.6 %shard_map.136 = (f32[16,3584]{1,0:T(8,128)}, f32[8,3072]{1,0:T(8,128)}, bf16[96,128,128]{2,1,0:T(8,128)(2,1)S(1)}) custom-call(f32[448,128]{1,0:T(8,128)S(1)} %get-tuple-element.46.cells_ref, f32[8,3072]{1,0:T(8,128)S(1)} %copy-done.2, bf16[256,128,128]{2,1,0:T(8,128)(2,1)} %weight_hbm.3), custom_call_target="tpu_custom_call" | custom-call | flops 2147483648 | bytes 33554432 | tf_op jit(solution)/shard_map/pallas_call | solution.py:365
  36.3 4.4 %all-to-all-done.1 = bf16[16,32,128]{2,1,0:T(8,128)(2,1)S(1)} async-done(((bf16[16,32,128]{2,1,0:T(8,128)(2,1)}), bf16[16,32,128]{2,1,0:T(8,128)(2,1)S(1)}, u32[]{:S(2)}, u32[]{:S(2)}) %all-to-all-start.1) | async-done | bytes 131104 | tf_op jit(solution)/shard_map/all_to_all | solution.py:485
  40.7 4.4 %shard_map.137 = f32[8,3072]{1,0:T(8,128)} custom-call(bf16[512,128]{1,0:T(8,128)(2,1)S(1)} %bitcast.12, s32[2,1,256]{2,1,0:T(1,128)S(1)} %get-tuple-element.51.keys_ref, bf16[96,128,128]{2,1,0:T(8,128)(2,1)S(1)} %get-tuple-element.52.early_ref, bf16[256,128,128]{2,1,0:T(8,128)(2,1)} %weight_hbm.3), custom_call_target="tpu_custom_call" | custom-call | flops 268435456 | bytes 4194304 | tf_op jit(solution)/shard_map/pallas_call | solution.py:365
Async XLA Ops:
  0.6 9.3 %copy-start = (bf16[256,128,128]{2,1,0:T(8,128)(2,1)S(1)}, bf16[256,128,128]{2,1,0:T(8,128)(2,1)}, u32[]{:S(2)}) copy-start(bf16[256,128,128]{2,1,0:T(8,128)(2,1)} %weight_hbm.3) | copy-start | bytes 25165828
  1.8 7.3 %collective-permute-start.1 = (f32[2,6656]{1,0:T(2,128)S(1)}, f32[2,6656]{1,0:T(2,128)S(1)}, u32[]{:S(2)}, u32[]{:S(2)}) collective-permute-start(f32[2,6656]{1,0:T(2,128)S(1)} %get-tuple-element.32), channel_id=1, source_target_pairs={{1,2},{3,4},{5,6},{7,8},{9,10},{11,12},{13,14},{15,0},{2,1},{4,3},... | collective-permute-start | bytes 159752 | tf_op jit(solution)/shard_map/ppermute | solution.py:409
  8.7 1.3 %collective-permute-start = (f32[2,6656]{1,0:T(2,128)S(1)}, f32[2,6656]{1,0:T(2,128)S(1)}, u32[]{:S(2)}, u32[]{:S(2)}) collective-permute-start(f32[2,6656]{1,0:T(2,128)S(1)} %get-tuple-element.31), channel_id=1, source_target_pairs={{0,1},{1,0},{2,3},{3,2},{4,5},{5,4},{6,7},{7,6},{8,9},{9,8},{10,11... | collective-permute-start | bytes 159752 | tf_op jit(solution)/shard_map/ppermute | solution.py:450
  11.8 16.5 %copy-start.1 = (f32[8,3072]{1,0:T(8,128)}, f32[8,3072]{1,0:T(8,128)S(1)}, u32[]{:S(2)}) copy-start(f32[8,3072]{1,0:T(8,128)S(1)} %get-tuple-element.47.atm_ref) | copy-start | bytes 294916
  27.1 1.2 %collective-permute-start.2 = (f32[28,128]{1,0:T(8,128)S(1)}, f32[28,128]{1,0:T(8,128)S(1)}, u32[]{:S(2)}, u32[]{:S(2)}) collective-permute-start(f32[28,128]{1,0:T(8,128)S(1)} %get-tuple-element.45), channel_id=1, source_target_pairs={{0,1},{1,0},{2,3},{3,2},{4,5},{5,4},{6,7},{7,6},{8,9},{9,8},{10,11... | collective-permute-start | bytes 43016 | tf_op jit(solution)/shard_map/ppermute | solution.py:471
  29.3 11.4 %all-to-all-start.1 = ((bf16[16,32,128]{2,1,0:T(8,128)(2,1)}), bf16[16,32,128]{2,1,0:T(8,128)(2,1)S(1)}, u32[]{:S(2)}, u32[]{:S(2)}) async-start(bf16[16,32,128]{2,1,0:T(8,128)(2,1)} %bitcast.10), calls=%async_computation.1 | async-start | bytes 262144 | tf_op jit(solution)/shard_map/all_to_all | solution.py:485
  32.8 0.9 %copy-start.2 = (f32[8,3072]{1,0:T(8,128)S(1)}, f32[8,3072]{1,0:T(8,128)}, u32[]{:S(2)}) copy-start(f32[8,3072]{1,0:T(8,128)} %copy-done.1) | copy-start | bytes 294916

commit v7 on v6

--- a/solution.py
+++ b/solution.py
@@ -11,7 +11,7 @@
 EDGE = 32
 CHUNK = 8
 PIECE = 32
-EARLY = 96
+EARLY = 64
 F32 = jnp.float32
 BF16 = jnp.bfloat16
 VMEM = pl.BlockSpec(memory_space=pltpu.VMEM)
@@ -88,9 +88,9 @@
 def stage_kernel(
     ntiles, main, atm_rows, atm_row_tiles, ocean_rows, row_tiles,
     me_ref, atm_ref, ocean_ref, src_hbm, own_hbm, dst_hbm, gain_hbm, coef_hbm, kappa_hbm, nu_hbm, forcing_hbm,
-    pick_ref, keys_ref, slots_ref, ids_ref, field_ref, scale_ref, kappa_ref, nu_ref,
-    even_ref,
-    ints, gains, forcing_ref, sems,
+    weight_hbm, pick_ref, keys_ref, slots_ref, ids_ref, field_ref, scale_ref, kappa_ref, nu_ref,
+    even_ref, early_ref,
+    ints, gains, forcing_ref, sems, early_sems,
 ):
     small = [
         (src_hbm, ints.at[0]), (own_hbm, ints.at[1]), (dst_hbm, ints.at[2]),
@@ -98,7 +98,8 @@
         (kappa_hbm, kappa_ref), (nu_hbm, nu_ref),
     ]
     copies = [pltpu.make_async_copy(a, b, sems.at[k]) for k, (a, b) in enumerate(small)]
-    for copy in copies:
+    weights = fetches(weight_hbm, 0, early_ref, early_sems)
+    for copy in copies + weights:
         copy.start()
     edge_rows(me_ref[0] % 2 == 0, atm_ref, ocean_ref, even_ref)
     for copy in copies[:3]:
@@ -143,11 +144,13 @@
     for k in range(forcing_ref.shape[0]):
         field = field + coef[:, k : k + 1] * forcing_ref[k].astype(F32)
     field_ref[...] = field
+    for copy in weights:
+        copy.wait()
 
 
 def forward_kernel(
     ntiles, main, me_ref, atm_ref, kappa_ref, even_ref, odd_ref, field_ref, scale_ref,
-    pick_ref, slots_ref, ids_ref, weight_ref, next_ref, out_ref, work,
+    pick_ref, slots_ref, ids_ref, early_ref, weight_ref, next_ref, out_ref, work,
 ):
     atm_rows, cols = atm_ref.shape
     rows = main + EDGE
@@ -181,7 +184,8 @@
         spread = jnp.concatenate(
             [jnp.where(row == q, piece, 0.0) for q in range(CHUNK)], axis=1
         ).astype(BF16)
-        weight = weight_ref[pl.ds(n * CHUNK, CHUNK)].reshape(CHUNK * LANE, LANE)
+        held = early_ref if n * CHUNK < early_ref.shape[0] else weight_ref
+        weight = held[pl.ds(n * CHUNK, CHUNK)].reshape(CHUNK * LANE, LANE)
         parts.append(dot(spread, weight))
     contribution = jnp.concatenate(parts, axis=0).astype(BF16)
     at = iota((EDGE, LANE), 0)
@@ -304,24 +308,22 @@
     return_ref[...] = dot(pick_ref[...], cells_ref[...].astype(BF16)).astype(BF16)
 
 
-def fetch_kernel(cells_ref, atm_ref, weight_hbm, next_ref, atm_out, weight_ref, sems):
-    atm_out[...] = atm_ref[...]
-    copies = fetches(weight_hbm, 0, weight_ref, sems)
+def backward_kernel(
+    came_ref, keys_ref, early_ref, cells_ref, atm_ref, weight_hbm,
+    out_ref, next_hbm, atm_hbm, late_ref, next_ref, sems, out_sems,
+):
+    early = early_ref.shape[0]
+    copies = fetches(weight_hbm, early, late_ref, sems)
     for copy in copies:
         copy.start()
     rows = next_ref.shape[0]
     for c in range(next_ref.shape[1] // LANE):
         next_ref[:, c * LANE : (c + 1) * LANE] = cells_ref[c * rows : (c + 1) * rows]
-    for copy in copies:
-        copy.wait()
-
-
-def backward_kernel(
-    came_ref, keys_ref, early_ref, weight_hbm, out_ref, late_ref, sems
-):
-    early = early_ref.shape[0]
-    copies = fetches(weight_hbm, early, late_ref, sems)
-    for copy in copies:
+    written = [
+        pltpu.make_async_copy(atm_ref, atm_hbm, out_sems.at[0]),
+        pltpu.make_async_copy(next_ref, next_hbm, out_sems.at[1]),
+    ]
+    for copy in written:
         copy.start()
     values = dot(matches_lane(as_column(keys_ref[1]), came_ref.shape[0]), came_ref[...])
     blocks = values.shape[0]
@@ -348,14 +350,16 @@
     tiles = dot(back, coarse) + dot(back, fine)
     for c in range(out_ref.shape[1] // LANE):
         out_ref[:, c * LANE : (c + 1) * LANE] = tiles[c * rows : (c + 1) * rows]
-
-
-def call(kernel, outs, specs, cost, scratch=(), limit=24 << 20):
+    for copy in written:
+        copy.wait()
+
+
+def call(kernel, outs, specs, cost, scratch=(), limit=24 << 20, out_specs=None):
     run = pl.pallas_call(
         kernel,
         out_shape=outs,
         in_specs=specs,
-        out_specs=jax.tree.map(lambda _: VMEM, outs),
+        out_specs=out_specs or jax.tree.map(lambda _: VMEM, outs),
         scratch_shapes=scratch,
         compiler_params=pltpu.CompilerParams(vmem_limit_bytes=limit),
         cost_estimate=pl.CostEstimate(flops=cost, bytes_accessed=cost // 64, transcendentals=0),
@@ -411,7 +415,7 @@
     early = min(EARLY, blocks)
     whole = blocks // PIECE
     nflux = forcing.shape[0]
-    pick, keys, slots, ids, field, scale, kappa, nu, to_even = call(
+    pick, keys, slots, ids, field, scale, kappa, nu, to_even, again = call(
         functools.partial(
             stage_kernel, ntiles, main, atm_rows, atm_row_tiles, ocean_rows, row_tiles
         ),
@@ -425,14 +429,16 @@
             shape((1, atm_cols), F32),
             shape((row_tiles, LANE), F32),
             edges,
+            shape((early, LANE, LANE), BF16),
         ),
-        [SMEM, VMEM, VMEM] + [HBM] * 8,
+        [SMEM, VMEM, VMEM] + [HBM] * 9,
         1 << 20,
         [
             pltpu.VMEM((3, 1, blocks), jnp.int32),
             pltpu.VMEM((2, 1, nflux), F32),
             pltpu.VMEM(forcing.shape, BF16),
             pltpu.SemaphoreType.DMA((8,)),
+            pltpu.SemaphoreType.DMA((early // PIECE,)),
         ],
     )(
         me_arr,
@@ -446,15 +452,17 @@
         atm_kappa.reshape(1, atm_cols),
         ocean_nu.reshape(row_tiles, LANE),
         forcing,
+        remap_weight,
     )
     from_even = lax.ppermute(to_even, "tiles", [(i, i ^ 1) for i in range(ntiles)])
     atm_next, outgoing = call(
         functools.partial(forward_kernel, ntiles, main),
         (shape(atm_state.shape, F32), shape((ntiles * rows, LANE), BF16)),
-        [SMEM] + [VMEM] * 10,
+        [SMEM] + [VMEM] * 11,
         1 << 28,
         [pltpu.VMEM((2 * atm_rows, atm_cols), F32)],
-    )(me_arr, atm, kappa, from_even, from_odd, field, scale, pick, slots, ids, remap_weight)
+    )(me_arr, atm, kappa, from_even, from_odd, field, scale, pick, slots, ids, again,
+      remap_weight)
     arrived = lax.all_to_all(outgoing, "tiles", split_axis=0, concat_axis=0, tiled=True)
     total = ocean_rows * row_tiles
     drive, side, slot_keys, to_pair = call(
@@ -483,27 +491,23 @@
         1 << 27,
     )(me_arr, value, take, nu, from_pair)
     came_back = lax.all_to_all(returned, "tiles", split_axis=0, concat_axis=0, tiled=True)
-    ocean_next, atm_out, again = call(
-        fetch_kernel,
+    feedback, ocean_next, atm_out = call(
+        backward_kernel,
         (
+            shape(atm_state.shape, F32),
             shape(ocean_state.shape, F32),
             shape(atm_state.shape, F32),
-            shape((early, LANE, LANE), BF16),
         ),
-        [VMEM, VMEM, HBM],
-        1 << 31,
-        [pltpu.SemaphoreType.DMA((early // PIECE,))],
-    )(cells, atm_next, remap_weight)
-    feedback = call(
-        backward_kernel,
-        shape(atm_state.shape, F32),
-        [VMEM] * 3 + [HBM],
+        [VMEM] * 5 + [HBM],
         1 << 28,
         [
             pltpu.VMEM((blocks - early, LANE, LANE), BF16),
+            pltpu.VMEM(ocean_state.shape, F32),
             pltpu.SemaphoreType.DMA(((blocks - early) // PIECE,)),
+            pltpu.SemaphoreType.DMA((2,)),
         ],
-    )(came_back, keys, again, remap_weight)
+        out_specs=(VMEM, HBM, HBM),
+    )(came_back, keys, again, cells, atm_next, remap_weight)
     return (atm_out, ocean_next, feedback)
 
 

time: 45.4 us -> 44.4 us (0.978)
  blocking collectives: 14.9 us -> 25.1 us
  waiting for transfers between devices: 5.91 us -> 1.51 us
  starting transfers between devices: 9.16 us -> 5.65 us
  Pallas kernels: 13.5 us -> 11.2 us
  local copies, waits for them, and re-layouts: 0.9 us -> 0.01 us
    all_to_all x0 -> x1, blocking collectives: none -> 10.7 us  [per_device(): lax.all_to_all(returned, 'tiles', split_axis=0, concat_axis=0, tiled=True)]
    all_to_all x1 -> x0, waiting for transfers between devices: 4.4 us -> none  [per_device(): lax.all_to_all(returned, 'tiles', split_axis=0, concat_axis=0, tiled=True)]
    all_to_all x1 -> x0, starting transfers between devices: 3.51 us -> none  [per_device(): lax.all_to_all(returned, 'tiles', split_axis=0, concat_axis=0, tiled=True)]
    pallas_call x8 -> x7, Pallas kernels: 13.5 us -> 11.2 us  [placed(): run(*[pltpu.with_memory_space_constraint(x, pltpu.HBM) if spec is HBM els...]
    unnamed x6 -> x4, local copies, waits for them, and re-layouts: 0.9 us -> 0.01 us
    all_to_all x1, blocking collectives: 14.9 us -> 14.4 us  [per_device(): lax.all_to_all(outgoing, 'tiles', split_axis=0, concat_axis=0, tiled=True)]
  transfers between devices with their start and end apart: 4 -> 3, of which waited for: 4 -> 2; matrix products, arithmetic and copies ran while one was open for 0% -> 0% of each run, Pallas kernels for 11% -> 6%
where the time goes in v7:
time: 44.4 us; the launch traced here: 44.2 us
  blocking collectives  25.1 us (57%)
  Pallas kernels  11.2 us (25%)
  starting transfers between devices  5.65 us (13%)
  waiting for transfers between devices  1.51 us (3%)
  between operations  0.72 us (2%)
    all_to_all x1, blocking collectives, per_device(): lax.all_to_all(outgoing, 'tiles', split_axis=0, concat_axis=0, tiled=True)  14.4 us
    pallas_call x7, Pallas kernels, placed(): run(*[pltpu.with_memory_space_constraint(x, pltpu.HBM) if spec is HBM els...  11.2 us
    all_to_all x1, blocking collectives, per_device(): lax.all_to_all(returned, 'tiles', split_axis=0, concat_axis=0, tiled=True)  10.7 us
    ppermute x1, starting transfers between devices, per_device(): from_odd = lax.ppermute(to_odd, 'tiles', pairs + [(j, i) for i, j in pairs])  5.51 us
    ppermute x1, waiting for transfers between devices, per_device(): lax.ppermute(to_even, 'tiles', [(i, i ^ 1) for i in range(ntiles)])  1.21 us
  transfers between devices with their start and end apart: 3, of which 2 were waited for; matrix products, arithmetic and copies ran while one was open for 0% of the time, Pallas kernels for 6%

profile of v7, /device:TPU:0, one launch (start us, length us, event | category | flops | bytes accessed | tf_op | source)
XLA Modules:
  0.0 44.2 jit_solution(14547959545363276151)
XLA Ops:
  0.6 0.0 slice-start
  0.6 0.0 slice-start.1
  0.7 1.2 %shard_map.130 = (f32[8,3072]{1,0:T(8,128)S(1)}, f32[16,3584]{1,0:T(8,128)S(1)}, f32[2,6656]{1,0:T(2,128)S(1)}) custom-call(s32[1]{0:T(128)} %bitcast.me_ref, f32[8,3072]{1,0:T(8,128)} %atm_hbm.1, f32[16,3584]{1,0:T(8,128)} %ocean_hbm.1), custom_call_target="tpu_custom_call" | custom-call | flops 17179869184 | bytes 268435456 | tf_op jit(solution)/shard_map/pallas_call | solution.py:369
  1.9 5.5 %collective-permute-start.1 = (f32[2,6656]{1,0:T(2,128)S(1)}, f32[2,6656]{1,0:T(2,128)S(1)}, u32[]{:S(2)}, u32[]{:S(2)}) collective-permute-start(f32[2,6656]{1,0:T(2,128)S(1)} %get-tuple-element.33), channel_id=1, source_target_pairs={{1,2},{3,4},{5,6},{7,8},{9,10},{11,12},{13,14},{15,0},{2,1},{4,3},... | collective-permute-start | bytes 159752 | tf_op jit(solution)/shard_map/ppermute | solution.py:413
  7.4 1.8 %shard_map.131 = (bf16[256,192]{1,0:T(8,128)(2,1)S(1)}, s32[2,1,256]{2,1,0:T(1,128)S(1)}, bf16[1024,256]{1,0:T(8,128)(2,1)S(1)}, f32[2,16,128]{2,1,0:T(8,128)S(1...) custom-call(s32[1]{0:T(128)} %bitcast.me_ref, ...), custom_call_target="tpu_custom_call" | custom-call | flops 1048576 | bytes 16384 | tf_op jit(solution)/shard_map/pallas_call | solution.py:369
  9.2 0.1 collective-permute-start
  9.3 0.0 collective-permute-done.1.odd_ref
  9.3 1.2 %collective-permute-done.even_ref = f32[2,6656]{1,0:T(2,128)S(1)} collective-permute-done((f32[2,6656]{1,0:T(2,128)S(1)}, f32[2,6656]{1,0:T(2,128)S(1)}, u32[]{:S(2)}, u32[]{:S(2)}) %collective-permute-start) | collective-permute-done | bytes 53280 | tf_op jit(solution)/shard_map/ppermute | solution.py:457
  10.5 0.0 slice-done
  10.5 0.0 slice-done.1
  10.5 1.9 %shard_map.132 = (f32[8,3072]{1,0:T(8,128)S(1)}, bf16[1024,128]{1,0:T(8,128)(2,1)S(1)}) custom-call(s32[1]{0:T(128)} %bitcast.me_ref, f32[8,3072]{1,0:T(8,128)S(1)} %get-tuple-element.29.atm_ref, f32[1,3072]{1,0:T(1,128)S(1)} %get-tuple-element.31.kappa_ref, f32[2,6656]{1,0:T(2,128)S(1)} %collective-permute-done.even_ref, ...), custom_call_target="tpu_custom_call" | custom-call | flops 268435456 | bytes 4194304 | tf_op jit(solution)/shard_map/pallas_call | solution.py:369
  12.4 14.4 %all_to_all.22 = bf16[16,64,128]{2,1,0:T(8,128)(2,1)S(1)} all-to-all(bf16[16,64,128]{2,1,0:T(8,128)(2,1)S(1)} %bitcast.15), channel_id=1, replica_groups=mesh['members'=2,'tiles'=16] {'tiles'}, dimensions={0} | all-to-all | bytes 524288 | tf_op jit(solution)/shard_map/all_to_all | solution.py:466
  26.8 0.3 shard_map.133
  27.1 0.1 collective-permute-start.2
  27.2 0.9 %shard_map.134 = (f32[448,128]{1,0:T(8,128)S(1)}, bf16[512,448]{1,0:T(8,128)(2,1)S(1)}) custom-call(s32[1]{0:T(128)} %bitcast.me_ref, f32[448,128]{1,0:T(8,128)S(1)} %get-tuple-element.41.drive_ref, f32[32,128]{1,0:T(8,128)S(1)} %get-tuple-element.42.side_ref, s32[4,128]{1,0:T(4,128)S(1)} %get-tuple-element.43.keys_ref, ...), custom_call_target="tpu_custom_call" | custom-call | flops 2147483648 | bytes 33554432 | tf_op jit(solution)/shard_map/pallas_call | solution.py:369
  28.1 0.3 collective-permute-done.2.pair_ref
  28.3 0.3 shard_map.135
  28.7 10.7 %all_to_all.23 = bf16[16,32,128]{2,1,0:T(8,128)(2,1)S(1)} all-to-all(bf16[16,32,128]{2,1,0:T(8,128)(2,1)S(1)} %bitcast.17), channel_id=1, replica_groups=mesh['members'=2,'tiles'=16] {'tiles'}, dimensions={0} | all-to-all | bytes 262144 | tf_op jit(solution)/shard_map/all_to_all | solution.py:493
  39.4 4.8 %shard_map.136 = (f32[8,3072]{1,0:T(8,128)}, f32[16,3584]{1,0:T(8,128)}, f32[8,3072]{1,0:T(8,128)}) custom-call(bf16[512,128]{1,0:T(8,128)(2,1)S(1)} %bitcast.14, s32[2,1,256]{2,1,0:T(1,128)S(1)} %get-tuple-element.49.keys_ref, bf16[64,128,128]{2,1,0:T(8,128)(2,1)S(1)} %get-tuple-element.39.early_ref, f32[448,128]{1,0:T(8,128)S(1)} %get-tuple-element.50.cells_ref, ...), custom_call_target="tpu_custom_call" | custom-call | flops 268435456 | bytes 4194304 | tf_op jit(solution)/shard_map/pallas_call | solution.py:369
  (1 shorter events, 0.0 us)
Async XLA Ops:
  0.6 9.9 %slice-start = ((s8[8388608]{0:T(1024)(128)(4,1)}), s8[4194304]{0:T(1024)(128)(4,1)S(1)}, s32[]{:S(2)}) async-start(s8[8388608]{0:T(1024)(128)(4,1)} %bitcast.12), calls=%async_computation.2 | async-start | bytes 8388608
  0.6 9.9 %slice-start.1 = ((s8[8388608]{0:T(1024)(128)(4,1)}), s8[4194304]{0:T(1024)(128)(4,1)S(1)}, s32[]{:S(2)}) async-start(s8[8388608]{0:T(1024)(128)(4,1)} %bitcast.12), calls=%async_computation.3 | async-start | bytes 8388608
  1.9 7.4 %collective-permute-start.1 = (f32[2,6656]{1,0:T(2,128)S(1)}, f32[2,6656]{1,0:T(2,128)S(1)}, u32[]{:S(2)}, u32[]{:S(2)}) collective-permute-start(f32[2,6656]{1,0:T(2,128)S(1)} %get-tuple-element.33), channel_id=1, source_target_pairs={{1,2},{3,4},{5,6},{7,8},{9,10},{11,12},{13,14},{15,0},{2,1},{4,3},... | collective-permute-start | bytes 159752 | tf_op jit(solution)/shard_map/ppermute | solution.py:413
  9.2 1.3 %collective-permute-start = (f32[2,6656]{1,0:T(2,128)S(1)}, f32[2,6656]{1,0:T(2,128)S(1)}, u32[]{:S(2)}, u32[]{:S(2)}) collective-permute-start(f32[2,6656]{1,0:T(2,128)S(1)} %get-tuple-element.32), channel_id=1, source_target_pairs={{0,1},{1,0},{2,3},{3,2},{4,5},{5,4},{6,7},{7,6},{8,9},{9,8},{10,11... | collective-permute-start | bytes 159752 | tf_op jit(solution)/shard_map/ppermute | solution.py:457
  27.1 1.2 %collective-permute-start.2 = (f32[28,128]{1,0:T(8,128)S(1)}, f32[28,128]{1,0:T(8,128)S(1)}, u32[]{:S(2)}, u32[]{:S(2)}) collective-permute-start(f32[28,128]{1,0:T(8,128)S(1)} %get-tuple-element.47), channel_id=1, source_target_pairs={{0,1},{1,0},{2,3},{3,2},{4,5},{5,4},{6,7},{7,6},{8,9},{9,8},{10,11... | collective-permute-start | bytes 43016 | tf_op jit(solution)/shard_map/ppermute | solution.py:479

commit v8 on v7

--- a/solution.py
+++ b/solution.py
@@ -11,7 +11,7 @@
 EDGE = 32
 CHUNK = 8
 PIECE = 32
-EARLY = 64
+EARLY = 96
 F32 = jnp.float32
 BF16 = jnp.bfloat16
 VMEM = pl.BlockSpec(memory_space=pltpu.VMEM)

time: 44.4 us -> 44.1 us (level)
  transfers between devices with their start and end apart: 3 -> 3, of which waited for: 2 -> 2; matrix products, arithmetic and copies ran while one was open for 0% -> 0% of each run, Pallas kernels for 6% -> 7%
where the time goes in v8:
time: 44.1 us; the launch traced here: 43.9 us
  blocking collectives  24.7 us (56%)
  Pallas kernels  11.2 us (25%)
  starting transfers between devices  5.65 us (13%)
  waiting for transfers between devices  1.51 us (3%)
  between operations  0.72 us (2%)
    all_to_all x1, blocking collectives, per_device(): lax.all_to_all(outgoing, 'tiles', split_axis=0, concat_axis=0, tiled=True)  14 us
    pallas_call x7, Pallas kernels, placed(): run(*[pltpu.with_memory_space_constraint(x, pltpu.HBM) if spec is HBM els...  11.2 us
    all_to_all x1, blocking collectives, per_device(): lax.all_to_all(returned, 'tiles', split_axis=0, concat_axis=0, tiled=True)  10.7 us
    ppermute x1, starting transfers between devices, per_device(): from_odd = lax.ppermute(to_odd, 'tiles', pairs + [(j, i) for i, j in pairs])  5.51 us
    ppermute x1, waiting for transfers between devices, per_device(): lax.ppermute(to_even, 'tiles', [(i, i ^ 1) for i in range(ntiles)])  1.21 us
  transfers between devices with their start and end apart: 3, of which 2 were waited for; matrix products, arithmetic and copies ran while one was open for 0% of the time, Pallas kernels for 7%

profile of v8, /device:TPU:0, one launch (start us, length us, event | category | flops | bytes accessed | tf_op | source)
XLA Modules:
  0.0 43.9 jit_solution(16626565035380284569)
XLA Ops:
  0.6 0.0 slice-start
  0.6 0.0 slice-start.1
  0.7 1.2 %shard_map.130 = (f32[8,3072]{1,0:T(8,128)S(1)}, f32[16,3584]{1,0:T(8,128)S(1)}, f32[2,6656]{1,0:T(2,128)S(1)}) custom-call(s32[1]{0:T(128)} %bitcast.me_ref, f32[8,3072]{1,0:T(8,128)} %atm_hbm.1, f32[16,3584]{1,0:T(8,128)} %ocean_hbm.1), custom_call_target="tpu_custom_call" | custom-call | flops 17179869184 | bytes 268435456 | tf_op jit(solution)/shard_map/pallas_call | solution.py:369
  1.9 5.5 %collective-permute-start.1 = (f32[2,6656]{1,0:T(2,128)S(1)}, f32[2,6656]{1,0:T(2,128)S(1)}, u32[]{:S(2)}, u32[]{:S(2)}) collective-permute-start(f32[2,6656]{1,0:T(2,128)S(1)} %get-tuple-element.33), channel_id=1, source_target_pairs={{1,2},{3,4},{5,6},{7,8},{9,10},{11,12},{13,14},{15,0},{2,1},{4,3},... | collective-permute-start | bytes 159752 | tf_op jit(solution)/shard_map/ppermute | solution.py:413
  7.4 2.2 %shard_map.131 = (bf16[256,192]{1,0:T(8,128)(2,1)S(1)}, s32[2,1,256]{2,1,0:T(1,128)S(1)}, bf16[1024,256]{1,0:T(8,128)(2,1)S(1)}, f32[2,16,128]{2,1,0:T(8,128)S(1...) custom-call(s32[1]{0:T(128)} %bitcast.me_ref, ...), custom_call_target="tpu_custom_call" | custom-call | flops 1048576 | bytes 16384 | tf_op jit(solution)/shard_map/pallas_call | solution.py:369
  9.5 0.1 collective-permute-start
  9.6 0.0 collective-permute-done.1.odd_ref
  9.6 1.2 %collective-permute-done.even_ref = f32[2,6656]{1,0:T(2,128)S(1)} collective-permute-done((f32[2,6656]{1,0:T(2,128)S(1)}, f32[2,6656]{1,0:T(2,128)S(1)}, u32[]{:S(2)}, u32[]{:S(2)}) %collective-permute-start) | collective-permute-done | bytes 53280 | tf_op jit(solution)/shard_map/ppermute | solution.py:457
  10.8 0.0 slice-done
  10.8 0.0 slice-done.1
  10.9 1.9 %shard_map.132 = (f32[8,3072]{1,0:T(8,128)S(1)}, bf16[1024,128]{1,0:T(8,128)(2,1)S(1)}) custom-call(s32[1]{0:T(128)} %bitcast.me_ref, f32[8,3072]{1,0:T(8,128)S(1)} %get-tuple-element.29.atm_ref, f32[1,3072]{1,0:T(1,128)S(1)} %get-tuple-element.31.kappa_ref, f32[2,6656]{1,0:T(2,128)S(1)} %collective-permute-done.even_ref, ...), custom_call_target="tpu_custom_call" | custom-call | flops 268435456 | bytes 4194304 | tf_op jit(solution)/shard_map/pallas_call | solution.py:369
  12.7 14.0 %all_to_all.22 = bf16[16,64,128]{2,1,0:T(8,128)(2,1)S(1)} all-to-all(bf16[16,64,128]{2,1,0:T(8,128)(2,1)S(1)} %bitcast.15), channel_id=1, replica_groups=mesh['members'=2,'tiles'=16] {'tiles'}, dimensions={0} | all-to-all | bytes 524288 | tf_op jit(solution)/shard_map/all_to_all | solution.py:466
  26.8 0.3 shard_map.133
  27.1 0.1 collective-permute-start.2
  27.2 0.9 %shard_map.134 = (f32[448,128]{1,0:T(8,128)S(1)}, bf16[512,448]{1,0:T(8,128)(2,1)S(1)}) custom-call(s32[1]{0:T(128)} %bitcast.me_ref, f32[448,128]{1,0:T(8,128)S(1)} %get-tuple-element.41.drive_ref, f32[32,128]{1,0:T(8,128)S(1)} %get-tuple-element.42.side_ref, s32[4,128]{1,0:T(4,128)S(1)} %get-tuple-element.43.keys_ref, ...), custom_call_target="tpu_custom_call" | custom-call | flops 2147483648 | bytes 33554432 | tf_op jit(solution)/shard_map/pallas_call | solution.py:369
  28.0 0.3 collective-permute-done.2.pair_ref
  28.3 0.3 shard_map.135
  28.7 10.7 %all_to_all.23 = bf16[16,32,128]{2,1,0:T(8,128)(2,1)S(1)} all-to-all(bf16[16,32,128]{2,1,0:T(8,128)(2,1)S(1)} %bitcast.17), channel_id=1, replica_groups=mesh['members'=2,'tiles'=16] {'tiles'}, dimensions={0} | all-to-all | bytes 262144 | tf_op jit(solution)/shard_map/all_to_all | solution.py:493
  39.4 4.5 %shard_map.136 = (f32[8,3072]{1,0:T(8,128)}, f32[16,3584]{1,0:T(8,128)}, f32[8,3072]{1,0:T(8,128)}) custom-call(bf16[512,128]{1,0:T(8,128)(2,1)S(1)} %bitcast.14, s32[2,1,256]{2,1,0:T(1,128)S(1)} %get-tuple-element.49.keys_ref, bf16[96,128,128]{2,1,0:T(8,128)(2,1)S(1)} %get-tuple-element.39.early_ref, f32[448,128]{1,0:T(8,128)S(1)} %get-tuple-element.50.cells_ref, ...), custom_call_target="tpu_custom_call" | custom-call | flops 268435456 | bytes 4194304 | tf_op jit(solution)/shard_map/pallas_call | solution.py:369
  (1 shorter events, 0.0 us)
Async XLA Ops:
  0.6 10.2 %slice-start = ((s8[8388608]{0:T(1024)(128)(4,1)}), s8[4194304]{0:T(1024)(128)(4,1)S(1)}, s32[]{:S(2)}) async-start(s8[8388608]{0:T(1024)(128)(4,1)} %bitcast.12), calls=%async_computation.2 | async-start | bytes 8388608
  0.6 10.2 %slice-start.1 = ((s8[8388608]{0:T(1024)(128)(4,1)}), s8[4194304]{0:T(1024)(128)(4,1)S(1)}, s32[]{:S(2)}) async-start(s8[8388608]{0:T(1024)(128)(4,1)} %bitcast.12), calls=%async_computation.3 | async-start | bytes 8388608
  1.9 7.8 %collective-permute-start.1 = (f32[2,6656]{1,0:T(2,128)S(1)}, f32[2,6656]{1,0:T(2,128)S(1)}, u32[]{:S(2)}, u32[]{:S(2)}) collective-permute-start(f32[2,6656]{1,0:T(2,128)S(1)} %get-tuple-element.33), channel_id=1, source_target_pairs={{1,2},{3,4},{5,6},{7,8},{9,10},{11,12},{13,14},{15,0},{2,1},{4,3},... | collective-permute-start | bytes 159752 | tf_op jit(solution)/shard_map/ppermute | solution.py:413
  9.5 1.3 %collective-permute-start = (f32[2,6656]{1,0:T(2,128)S(1)}, f32[2,6656]{1,0:T(2,128)S(1)}, u32[]{:S(2)}, u32[]{:S(2)}) collective-permute-start(f32[2,6656]{1,0:T(2,128)S(1)} %get-tuple-element.32), channel_id=1, source_target_pairs={{0,1},{1,0},{2,3},{3,2},{4,5},{5,4},{6,7},{7,6},{8,9},{9,8},{10,11... | collective-permute-start | bytes 159752 | tf_op jit(solution)/shard_map/ppermute | solution.py:457
  27.1 1.2 %collective-permute-start.2 = (f32[28,128]{1,0:T(8,128)S(1)}, f32[28,128]{1,0:T(8,128)S(1)}, u32[]{:S(2)}, u32[]{:S(2)}) collective-permute-start(f32[28,128]{1,0:T(8,128)S(1)} %get-tuple-element.47), channel_id=1, source_target_pairs={{0,1},{1,0},{2,3},{3,2},{4,5},{5,4},{6,7},{7,6},{8,9},{9,8},{10,11... | collective-permute-start | bytes 43016 | tf_op jit(solution)/shard_map/ppermute | solution.py:479

commit v9 on v8

--- a/solution.py
+++ b/solution.py
@@ -10,8 +10,6 @@
 LANE = 128
 EDGE = 32
 CHUNK = 8
-PIECE = 32
-EARLY = 96
 F32 = jnp.float32
 BF16 = jnp.bfloat16
 VMEM = pl.BlockSpec(memory_space=pltpu.VMEM)
@@ -49,19 +47,6 @@
         for k in range(0, width, LANE)
     ]
     return jnp.concatenate(parts, axis=1)
-
-
-def fetches(weight_hbm, first, held, sems):
-    copies = []
-    for n in range(held.shape[0] // PIECE):
-        copies.append(
-            pltpu.make_async_copy(
-                weight_hbm.at[pl.ds(first + n * PIECE, PIECE)],
-                held.at[pl.ds(n * PIECE, PIECE)],
-                sems.at[n],
-            )
-        )
-    return copies
 
 
 def edge_rows(upper, atm_ref, ocean_ref, out_ref):
@@ -88,9 +73,9 @@
 def stage_kernel(
     ntiles, main, atm_rows, atm_row_tiles, ocean_rows, row_tiles,
     me_ref, atm_ref, ocean_ref, src_hbm, own_hbm, dst_hbm, gain_hbm, coef_hbm, kappa_hbm, nu_hbm, forcing_hbm,
-    weight_hbm, pick_ref, keys_ref, slots_ref, ids_ref, field_ref, scale_ref, kappa_ref, nu_ref,
-    even_ref, early_ref,
-    ints, gains, forcing_ref, sems, early_sems,
+    pick_ref, keys_ref, slots_ref, ids_ref, field_ref, scale_ref, kappa_ref, nu_ref,
+    even_ref,
+    ints, gains, forcing_ref, sems,
 ):
     small = [
         (src_hbm, ints.at[0]), (own_hbm, ints.at[1]), (dst_hbm, ints.at[2]),
@@ -98,8 +83,7 @@
         (kappa_hbm, kappa_ref), (nu_hbm, nu_ref),
     ]
     copies = [pltpu.make_async_copy(a, b, sems.at[k]) for k, (a, b) in enumerate(small)]
-    weights = fetches(weight_hbm, 0, early_ref, early_sems)
-    for copy in copies + weights:
+    for copy in copies:
         copy.start()
     edge_rows(me_ref[0] % 2 == 0, atm_ref, ocean_ref, even_ref)
     for copy in copies[:3]:
@@ -144,13 +128,11 @@
     for k in range(forcing_ref.shape[0]):
         field = field + coef[:, k : k + 1] * forcing_ref[k].astype(F32)
     field_ref[...] = field
-    for copy in weights:
-        copy.wait()
 
 
 def forward_kernel(
     ntiles, main, me_ref, atm_ref, kappa_ref, even_ref, odd_ref, field_ref, scale_ref,
-    pick_ref, slots_ref, ids_ref, early_ref, weight_ref, next_ref, out_ref, work,
+    pick_ref, slots_ref, ids_ref, weight_ref, next_ref, out_ref, work,
 ):
     atm_rows, cols = atm_ref.shape
     rows = main + EDGE
@@ -184,8 +166,7 @@
         spread = jnp.concatenate(
             [jnp.where(row == q, piece, 0.0) for q in range(CHUNK)], axis=1
         ).astype(BF16)
-        held = early_ref if n * CHUNK < early_ref.shape[0] else weight_ref
-        weight = held[pl.ds(n * CHUNK, CHUNK)].reshape(CHUNK * LANE, LANE)
+        weight = weight_ref[pl.ds(n * CHUNK, CHUNK)].reshape(CHUNK * LANE, LANE)
         parts.append(dot(spread, weight))
     contribution = jnp.concatenate(parts, axis=0).astype(BF16)
     at = iota((EDGE, LANE), 0)
@@ -309,13 +290,9 @@
 
 
 def backward_kernel(
-    came_ref, keys_ref, early_ref, cells_ref, atm_ref, weight_hbm,
-    out_ref, next_hbm, atm_hbm, late_ref, next_ref, sems, out_sems,
+    came_ref, keys_ref, cells_ref, atm_ref, weight_ref,
+    out_ref, next_hbm, atm_hbm, next_ref, out_sems,
 ):
-    early = early_ref.shape[0]
-    copies = fetches(weight_hbm, early, late_ref, sems)
-    for copy in copies:
-        copy.start()
     rows = next_ref.shape[0]
     for c in range(next_ref.shape[1] // LANE):
         next_ref[:, c * LANE : (c + 1) * LANE] = cells_ref[c * rows : (c + 1) * rows]
@@ -331,11 +308,7 @@
     parts = []
     for n in range(blocks // CHUNK):
         value = values[n * CHUNK : (n + 1) * CHUNK].astype(BF16)
-        at = n * CHUNK - early
-        if at >= 0 and at % PIECE == 0:
-            copies[at // PIECE].wait()
-        held = early_ref[pl.ds(n * CHUNK, CHUNK)] if at < 0 else late_ref[pl.ds(at, CHUNK)]
-        weight = held.reshape(CHUNK * LANE, LANE)
+        weight = weight_ref[pl.ds(n * CHUNK, CHUNK)].reshape(CHUNK * LANE, LANE)
         full = dot_nt(value, weight)
         part = full[:, :LANE]
         for q in range(1, CHUNK):
@@ -412,10 +385,8 @@
     pairs = [(2 * k + 1, (2 * k + 2) % ntiles) for k in range(ntiles // 2)]
     from_odd = lax.ppermute(to_odd, "tiles", pairs + [(j, i) for i, j in pairs])
     atm_row_tiles = atm_cols // LANE
-    early = min(EARLY, blocks)
-    whole = blocks // PIECE
     nflux = forcing.shape[0]
-    pick, keys, slots, ids, field, scale, kappa, nu, to_even, again = call(
+    pick, keys, slots, ids, field, scale, kappa, nu, to_even = call(
         functools.partial(
             stage_kernel, ntiles, main, atm_rows, atm_row_tiles, ocean_rows, row_tiles
         ),
@@ -429,16 +400,14 @@
             shape((1, atm_cols), F32),
             shape((row_tiles, LANE), F32),
             edges,
-            shape((early, LANE, LANE), BF16),
-        ),
-        [SMEM, VMEM, VMEM] + [HBM] * 9,
+        ),
+        [SMEM, VMEM, VMEM] + [HBM] * 8,
         1 << 20,
         [
             pltpu.VMEM((3, 1, blocks), jnp.int32),
             pltpu.VMEM((2, 1, nflux), F32),
             pltpu.VMEM(forcing.shape, BF16),
             pltpu.SemaphoreType.DMA((8,)),
-            pltpu.SemaphoreType.DMA((early // PIECE,)),
         ],
     )(
         me_arr,
@@ -452,17 +421,15 @@
         atm_kappa.reshape(1, atm_cols),
         ocean_nu.reshape(row_tiles, LANE),
         forcing,
-        remap_weight,
     )
     from_even = lax.ppermute(to_even, "tiles", [(i, i ^ 1) for i in range(ntiles)])
     atm_next, outgoing = call(
         functools.partial(forward_kernel, ntiles, main),
         (shape(atm_state.shape, F32), shape((ntiles * rows, LANE), BF16)),
-        [SMEM] + [VMEM] * 11,
+        [SMEM] + [VMEM] * 10,
         1 << 28,
         [pltpu.VMEM((2 * atm_rows, atm_cols), F32)],
-    )(me_arr, atm, kappa, from_even, from_odd, field, scale, pick, slots, ids, again,
-      remap_weight)
+    )(me_arr, atm, kappa, from_even, from_odd, field, scale, pick, slots, ids, remap_weight)
     arrived = lax.all_to_all(outgoing, "tiles", split_axis=0, concat_axis=0, tiled=True)
     total = ocean_rows * row_tiles
     drive, side, slot_keys, to_pair = call(
@@ -498,16 +465,11 @@
             shape(ocean_state.shape, F32),
             shape(atm_state.shape, F32),
         ),
-        [VMEM] * 5 + [HBM],
+        [VMEM] * 5,
         1 << 28,
-        [
-            pltpu.VMEM((blocks - early, LANE, LANE), BF16),
-            pltpu.VMEM(ocean_state.shape, F32),
-            pltpu.SemaphoreType.DMA(((blocks - early) // PIECE,)),
-            pltpu.SemaphoreType.DMA((2,)),
-        ],
+        [pltpu.VMEM(ocean_state.shape, F32), pltpu.SemaphoreType.DMA((2,))],
         out_specs=(VMEM, HBM, HBM),
-    )(came_back, keys, again, cells, atm_next, remap_weight)
+    )(came_back, keys, cells, atm_next, remap_weight)
     return (atm_out, ocean_next, feedback)
 
 

time: 44.1 us -> 43.5 us (0.986)
  Pallas kernels: 11.2 us -> 9.76 us
  blocking collectives: 24.7 us -> 25.6 us
    pallas_call x7, Pallas kernels: 11.2 us -> 9.76 us  [placed(): run(*[pltpu.with_memory_space_constraint(x, pltpu.HBM) if spec is HBM els...]
    all_to_all x1, blocking collectives: 14 us -> 14.9 us  [per_device(): lax.all_to_all(outgoing, 'tiles', split_axis=0, concat_axis=0, tiled=True)]
  transfers between devices with their start and end apart: 3 -> 3, of which waited for: 2 -> 3; matrix products, arithmetic and copies ran while one was open for 0% -> 0% of each run, Pallas kernels for 7% -> 5%
where the time goes in v9:
time: 43.5 us; the launch traced here: 43.2 us
  blocking collectives  25.6 us (59%)
  Pallas kernels  9.76 us (22%)
  starting transfers between devices  5.65 us (13%)
  waiting for transfers between devices  1.52 us (3%)
  between operations  0.7 us (2%)
    all_to_all x1, blocking collectives, per_device(): lax.all_to_all(outgoing, 'tiles', split_axis=0, concat_axis=0, tiled=True)  14.9 us
    all_to_all x1, blocking collectives, per_device(): lax.all_to_all(returned, 'tiles', split_axis=0, concat_axis=0, tiled=True)  10.7 us
    pallas_call x7, Pallas kernels, placed(): run(*[pltpu.with_memory_space_constraint(x, pltpu.HBM) if spec is HBM els...  9.76 us
    ppermute x1, starting transfers between devices, per_device(): from_odd = lax.ppermute(to_odd, 'tiles', pairs + [(j, i) for i, j in pairs])  5.51 us
  transfers between devices with their start and end apart: 3, of which 3 were waited for; matrix products, arithmetic and copies ran while one was open for 0% of the time, Pallas kernels for 5%

profile of v9, /device:TPU:0, one launch (start us, length us, event | category | flops | bytes accessed | tf_op | source)
XLA Modules:
  0.0 43.2 jit_solution(14147772051136709439)
XLA Ops:
  0.6 0.0 copy-start
  0.6 1.2 %shard_map.130 = (f32[8,3072]{1,0:T(8,128)S(1)}, f32[16,3584]{1,0:T(8,128)S(1)}, f32[2,6656]{1,0:T(2,128)S(1)}) custom-call(s32[1]{0:T(128)} %bitcast.me_ref, f32[8,3072]{1,0:T(8,128)} %atm_hbm.1, f32[16,3584]{1,0:T(8,128)} %ocean_hbm.1), custom_call_target="tpu_custom_call" | custom-call | flops 17179869184 | bytes 268435456 | tf_op jit(solution)/shard_map/pallas_call | solution.py:342
  1.8 5.5 %collective-permute-start.1 = (f32[2,6656]{1,0:T(2,128)S(1)}, f32[2,6656]{1,0:T(2,128)S(1)}, u32[]{:S(2)}, u32[]{:S(2)}) collective-permute-start(f32[2,6656]{1,0:T(2,128)S(1)} %get-tuple-element.32), channel_id=1, source_target_pairs={{1,2},{3,4},{5,6},{7,8},{9,10},{11,12},{13,14},{15,0},{2,1},{4,3},... | collective-permute-start | bytes 159752 | tf_op jit(solution)/shard_map/ppermute | solution.py:386
  7.3 1.3 %shard_map.131 = (bf16[256,192]{1,0:T(8,128)(2,1)S(1)}, s32[2,1,256]{2,1,0:T(1,128)S(1)}, bf16[1024,256]{1,0:T(8,128)(2,1)S(1)}, f32[2,16,128]{2,1,0:T(8,128)S(1...) custom-call(s32[1]{0:T(128)} %bitcast.me_ref, ...), custom_call_target="tpu_custom_call" | custom-call | flops 1048576 | bytes 16384 | tf_op jit(solution)/shard_map/pallas_call | solution.py:342
  8.7 0.1 collective-permute-start
  8.7 0.4 %collective-permute-done.1.odd_ref = f32[2,6656]{1,0:T(2,128)S(1)} collective-permute-done((f32[2,6656]{1,0:T(2,128)S(1)}, f32[2,6656]{1,0:T(2,128)S(1)}, u32[]{:S(2)}, u32[]{:S(2)}) %collective-permute-start.1) | collective-permute-done | bytes 53280 | tf_op jit(solution)/shard_map/ppermute | solution.py:386
  9.2 0.8 %collective-permute-done.even_ref = f32[2,6656]{1,0:T(2,128)S(1)} collective-permute-done((f32[2,6656]{1,0:T(2,128)S(1)}, f32[2,6656]{1,0:T(2,128)S(1)}, u32[]{:S(2)}, u32[]{:S(2)}) %collective-permute-start) | collective-permute-done | bytes 53280 | tf_op jit(solution)/shard_map/ppermute | solution.py:425
  10.0 0.0 copy-done
  10.0 1.9 %shard_map.132 = (f32[8,3072]{1,0:T(8,128)S(1)}, bf16[1024,128]{1,0:T(8,128)(2,1)S(1)}) custom-call(s32[1]{0:T(128)} %bitcast.me_ref, f32[8,3072]{1,0:T(8,128)S(1)} %get-tuple-element.28.atm_ref, f32[1,3072]{1,0:T(1,128)S(1)} %get-tuple-element.30.kappa_ref, f32[2,6656]{1,0:T(2,128)S(1)} %collective-permute-done.even_ref, ...), custom_call_target="tpu_custom_call" | custom-call | flops 268435456 | bytes 4194304 | tf_op jit(solution)/shard_map/pallas_call | solution.py:342
  11.8 14.9 %all_to_all.22 = bf16[16,64,128]{2,1,0:T(8,128)(2,1)S(1)} all-to-all(bf16[16,64,128]{2,1,0:T(8,128)(2,1)S(1)} %bitcast.13), channel_id=1, replica_groups=mesh['members'=2,'tiles'=16] {'tiles'}, dimensions={0} | all-to-all | bytes 524288 | tf_op jit(solution)/shard_map/all_to_all | solution.py:433
  26.7 0.3 shard_map.133
  27.1 0.1 collective-permute-start.2
  27.1 0.9 %shard_map.134 = (f32[448,128]{1,0:T(8,128)S(1)}, bf16[512,448]{1,0:T(8,128)(2,1)S(1)}) custom-call(s32[1]{0:T(128)} %bitcast.me_ref, f32[448,128]{1,0:T(8,128)S(1)} %get-tuple-element.39.drive_ref, f32[32,128]{1,0:T(8,128)S(1)} %get-tuple-element.40.side_ref, s32[4,128]{1,0:T(4,128)S(1)} %get-tuple-element.41.keys_ref, ...), custom_call_target="tpu_custom_call" | custom-call | flops 2147483648 | bytes 33554432 | tf_op jit(solution)/shard_map/pallas_call | solution.py:342
  28.0 0.3 collective-permute-done.2.pair_ref
  28.3 0.3 shard_map.135
  28.6 10.7 %all_to_all.23 = bf16[16,32,128]{2,1,0:T(8,128)(2,1)S(1)} all-to-all(bf16[16,32,128]{2,1,0:T(8,128)(2,1)S(1)} %bitcast.15), channel_id=1, replica_groups=mesh['members'=2,'tiles'=16] {'tiles'}, dimensions={0} | all-to-all | bytes 262144 | tf_op jit(solution)/shard_map/all_to_all | solution.py:460
  39.3 3.9 %shard_map.136 = (f32[8,3072]{1,0:T(8,128)}, f32[16,3584]{1,0:T(8,128)}, f32[8,3072]{1,0:T(8,128)}) custom-call(bf16[512,128]{1,0:T(8,128)(2,1)S(1)} %bitcast.12, s32[2,1,256]{2,1,0:T(1,128)S(1)} %get-tuple-element.47.keys_ref, f32[448,128]{1,0:T(8,128)S(1)} %get-tuple-element.48.cells_ref, f32[8,3072]{1,0:T(8,128)S(1)} %get-tuple-element.49.atm_ref, ...), custom_call_target="tpu_custom_call" | custom-call | flops 268435456 | bytes 4194304 | tf_op jit(solution)/shard_map/pallas_call | solution.py:342
Async XLA Ops:
  0.6 9.3 %copy-start = (bf16[256,128,128]{2,1,0:T(8,128)(2,1)S(1)}, bf16[256,128,128]{2,1,0:T(8,128)(2,1)}, u32[]{:S(2)}) copy-start(bf16[256,128,128]{2,1,0:T(8,128)(2,1)} %weight_ref.3) | copy-start | bytes 25165828
  1.8 7.3 %collective-permute-start.1 = (f32[2,6656]{1,0:T(2,128)S(1)}, f32[2,6656]{1,0:T(2,128)S(1)}, u32[]{:S(2)}, u32[]{:S(2)}) collective-permute-start(f32[2,6656]{1,0:T(2,128)S(1)} %get-tuple-element.32), channel_id=1, source_target_pairs={{1,2},{3,4},{5,6},{7,8},{9,10},{11,12},{13,14},{15,0},{2,1},{4,3},... | collective-permute-start | bytes 159752 | tf_op jit(solution)/shard_map/ppermute | solution.py:386
  8.7 1.3 %collective-permute-start = (f32[2,6656]{1,0:T(2,128)S(1)}, f32[2,6656]{1,0:T(2,128)S(1)}, u32[]{:S(2)}, u32[]{:S(2)}) collective-permute-start(f32[2,6656]{1,0:T(2,128)S(1)} %get-tuple-element.31), channel_id=1, source_target_pairs={{0,1},{1,0},{2,3},{3,2},{4,5},{5,4},{6,7},{7,6},{8,9},{9,8},{10,11... | collective-permute-start | bytes 159752 | tf_op jit(solution)/shard_map/ppermute | solution.py:425
  27.1 1.2 %collective-permute-start.2 = (f32[28,128]{1,0:T(8,128)S(1)}, f32[28,128]{1,0:T(8,128)S(1)}, u32[]{:S(2)}, u32[]{:S(2)}) collective-permute-start(f32[28,128]{1,0:T(8,128)S(1)} %get-tuple-element.45), channel_id=1, source_target_pairs={{0,1},{1,0},{2,3},{3,2},{4,5},{5,4},{6,7},{7,6},{8,9},{9,8},{10,11... | collective-permute-start | bytes 43016 | tf_op jit(solution)/shard_map/ppermute | solution.py:446

commit v10 on v9

--- a/solution.py
+++ b/solution.py
@@ -10,6 +10,7 @@
 LANE = 128
 EDGE = 32
 CHUNK = 8
+TURNED = 4
 F32 = jnp.float32
 BF16 = jnp.bfloat16
 VMEM = pl.BlockSpec(memory_space=pltpu.VMEM)
@@ -130,6 +131,13 @@
     field_ref[...] = field
 
 
+def spread(rows, count):
+    row = iota((CHUNK, LANE), 0)
+    return jnp.concatenate(
+        [jnp.where(row == q, rows, 0.0) for q in range(count)], axis=1
+    ).astype(BF16)
+
+
 def forward_kernel(
     ntiles, main, me_ref, atm_ref, kappa_ref, even_ref, odd_ref, field_ref, scale_ref,
     pick_ref, slots_ref, ids_ref, weight_ref, next_ref, out_ref, work,
@@ -159,15 +167,12 @@
     ).astype(BF16)
     pieces = dot(pick_ref[...], tiles)
     blocks = pieces.shape[0]
-    row = iota((CHUNK, LANE), 0)
     parts = []
     for n in range(blocks // CHUNK):
         piece = pieces[n * CHUNK : (n + 1) * CHUNK]
-        spread = jnp.concatenate(
-            [jnp.where(row == q, piece, 0.0) for q in range(CHUNK)], axis=1
-        ).astype(BF16)
+        rows_of = spread(piece, CHUNK)
         weight = weight_ref[pl.ds(n * CHUNK, CHUNK)].reshape(CHUNK * LANE, LANE)
-        parts.append(dot(spread, weight))
+        parts.append(dot(rows_of, weight))
     contribution = jnp.concatenate(parts, axis=0).astype(BF16)
     at = iota((EDGE, LANE), 0)
     for t in range(ntiles):
@@ -307,12 +312,16 @@
     row = iota((CHUNK, LANE), 0)
     parts = []
     for n in range(blocks // CHUNK):
-        value = values[n * CHUNK : (n + 1) * CHUNK].astype(BF16)
-        weight = weight_ref[pl.ds(n * CHUNK, CHUNK)].reshape(CHUNK * LANE, LANE)
-        full = dot_nt(value, weight)
-        part = full[:, :LANE]
-        for q in range(1, CHUNK):
-            part = jnp.where(row == q, full[:, q * LANE : (q + 1) * LANE], part)
+        value = values[n * CHUNK : (n + 1) * CHUNK]
+        turned = jnp.concatenate(
+            [jnp.transpose(weight_ref[n * CHUNK + q]) for q in range(TURNED)], axis=0
+        )
+        part = dot(spread(value, TURNED), turned)
+        weight = weight_ref[pl.ds(n * CHUNK + TURNED, CHUNK - TURNED)]
+        full = dot_nt(value.astype(BF16), weight.reshape((CHUNK - TURNED) * LANE, LANE))
+        for q in range(TURNED, CHUNK):
+            k = (q - TURNED) * LANE
+            part = jnp.where(row == q, full[:, k : k + LANE], part)
         parts.append(part)
     result = jnp.concatenate(parts, axis=0)
     coarse = result.astype(BF16)

time: 43.5 us -> 43 us (0.989)
  Pallas kernels: 9.76 us -> 9.32 us
    pallas_call x7, Pallas kernels: 9.76 us -> 9.32 us  [placed(): run(*[pltpu.with_memory_space_constraint(x, pltpu.HBM) if spec is HBM els...]
where the time goes in v10:
time: 43 us; the launch traced here: 42.8 us
  blocking collectives  25.6 us (60%)
  Pallas kernels  9.32 us (22%)
  starting transfers between devices  5.65 us (13%)
  waiting for transfers between devices  1.52 us (4%)
  between operations  0.7 us (2%)
    all_to_all x1, blocking collectives, per_device(): lax.all_to_all(outgoing, 'tiles', split_axis=0, concat_axis=0, tiled=True)  14.9 us
    all_to_all x1, blocking collectives, per_device(): lax.all_to_all(returned, 'tiles', split_axis=0, concat_axis=0, tiled=True)  10.7 us
    pallas_call x7, Pallas kernels, placed(): run(*[pltpu.with_memory_space_constraint(x, pltpu.HBM) if spec is HBM els...  9.32 us
    ppermute x1, starting transfers between devices, per_device(): from_odd = lax.ppermute(to_odd, 'tiles', pairs + [(j, i) for i, j in pairs])  5.51 us
  transfers between devices with their start and end apart: 3, of which 3 were waited for; matrix products, arithmetic and copies ran while one was open for 0% of the time, Pallas kernels for 5%

profile of v10, /device:TPU:0, one launch (start us, length us, event | category | flops | bytes accessed | tf_op | source)
XLA Modules:
  0.0 42.8 jit_solution(16277527678549690853)
XLA Ops:
  0.6 0.0 copy-start
  0.6 1.2 %shard_map.130 = (f32[8,3072]{1,0:T(8,128)S(1)}, f32[16,3584]{1,0:T(8,128)S(1)}, f32[2,6656]{1,0:T(2,128)S(1)}) custom-call(s32[1]{0:T(128)} %bitcast.me_ref, f32[8,3072]{1,0:T(8,128)} %atm_hbm.1, f32[16,3584]{1,0:T(8,128)} %ocean_hbm.1), custom_call_target="tpu_custom_call" | custom-call | flops 17179869184 | bytes 268435456 | tf_op jit(solution)/shard_map/pallas_call | solution.py:351
  1.8 5.5 %collective-permute-start.1 = (f32[2,6656]{1,0:T(2,128)S(1)}, f32[2,6656]{1,0:T(2,128)S(1)}, u32[]{:S(2)}, u32[]{:S(2)}) collective-permute-start(f32[2,6656]{1,0:T(2,128)S(1)} %get-tuple-element.32), channel_id=1, source_target_pairs={{1,2},{3,4},{5,6},{7,8},{9,10},{11,12},{13,14},{15,0},{2,1},{4,3},... | collective-permute-start | bytes 159752 | tf_op jit(solution)/shard_map/ppermute | solution.py:395
  7.3 1.3 %shard_map.131 = (bf16[256,192]{1,0:T(8,128)(2,1)S(1)}, s32[2,1,256]{2,1,0:T(1,128)S(1)}, bf16[1024,256]{1,0:T(8,128)(2,1)S(1)}, f32[2,16,128]{2,1,0:T(8,128)S(1...) custom-call(s32[1]{0:T(128)} %bitcast.me_ref, ...), custom_call_target="tpu_custom_call" | custom-call | flops 1048576 | bytes 16384 | tf_op jit(solution)/shard_map/pallas_call | solution.py:351
  8.7 0.1 collective-permute-start
  8.7 0.4 %collective-permute-done.1.odd_ref = f32[2,6656]{1,0:T(2,128)S(1)} collective-permute-done((f32[2,6656]{1,0:T(2,128)S(1)}, f32[2,6656]{1,0:T(2,128)S(1)}, u32[]{:S(2)}, u32[]{:S(2)}) %collective-permute-start.1) | collective-permute-done | bytes 53280 | tf_op jit(solution)/shard_map/ppermute | solution.py:395
  9.2 0.8 %collective-permute-done.even_ref = f32[2,6656]{1,0:T(2,128)S(1)} collective-permute-done((f32[2,6656]{1,0:T(2,128)S(1)}, f32[2,6656]{1,0:T(2,128)S(1)}, u32[]{:S(2)}, u32[]{:S(2)}) %collective-permute-start) | collective-permute-done | bytes 53280 | tf_op jit(solution)/shard_map/ppermute | solution.py:434
  10.0 0.0 copy-done
  10.0 1.9 %shard_map.132 = (f32[8,3072]{1,0:T(8,128)S(1)}, bf16[1024,128]{1,0:T(8,128)(2,1)S(1)}) custom-call(s32[1]{0:T(128)} %bitcast.me_ref, f32[8,3072]{1,0:T(8,128)S(1)} %get-tuple-element.28.atm_ref, f32[1,3072]{1,0:T(1,128)S(1)} %get-tuple-element.30.kappa_ref, f32[2,6656]{1,0:T(2,128)S(1)} %collective-permute-done.even_ref, ...), custom_call_target="tpu_custom_call" | custom-call | flops 268435456 | bytes 4194304 | tf_op jit(solution)/shard_map/pallas_call | solution.py:351
  11.8 14.9 %all_to_all.22 = bf16[16,64,128]{2,1,0:T(8,128)(2,1)S(1)} all-to-all(bf16[16,64,128]{2,1,0:T(8,128)(2,1)S(1)} %bitcast.13), channel_id=1, replica_groups=mesh['members'=2,'tiles'=16] {'tiles'}, dimensions={0} | all-to-all | bytes 524288 | tf_op jit(solution)/shard_map/all_to_all | solution.py:442
  26.7 0.3 shard_map.133
  27.1 0.1 collective-permute-start.2
  27.1 0.9 %shard_map.134 = (f32[448,128]{1,0:T(8,128)S(1)}, bf16[512,448]{1,0:T(8,128)(2,1)S(1)}) custom-call(s32[1]{0:T(128)} %bitcast.me_ref, f32[448,128]{1,0:T(8,128)S(1)} %get-tuple-element.39.drive_ref, f32[32,128]{1,0:T(8,128)S(1)} %get-tuple-element.40.side_ref, s32[4,128]{1,0:T(4,128)S(1)} %get-tuple-element.41.keys_ref, ...), custom_call_target="tpu_custom_call" | custom-call | flops 2147483648 | bytes 33554432 | tf_op jit(solution)/shard_map/pallas_call | solution.py:351
  28.0 0.3 collective-permute-done.2.pair_ref
  28.3 0.3 shard_map.135
  28.6 10.7 %all_to_all.23 = bf16[16,32,128]{2,1,0:T(8,128)(2,1)S(1)} all-to-all(bf16[16,32,128]{2,1,0:T(8,128)(2,1)S(1)} %bitcast.15), channel_id=1, replica_groups=mesh['members'=2,'tiles'=16] {'tiles'}, dimensions={0} | all-to-all | bytes 262144 | tf_op jit(solution)/shard_map/all_to_all | solution.py:469
  39.3 3.4 %shard_map.136 = (f32[8,3072]{1,0:T(8,128)}, f32[16,3584]{1,0:T(8,128)}, f32[8,3072]{1,0:T(8,128)}) custom-call(bf16[512,128]{1,0:T(8,128)(2,1)S(1)} %bitcast.12, s32[2,1,256]{2,1,0:T(1,128)S(1)} %get-tuple-element.47.keys_ref, f32[448,128]{1,0:T(8,128)S(1)} %get-tuple-element.48.cells_ref, f32[8,3072]{1,0:T(8,128)S(1)} %get-tuple-element.49.atm_ref, ...), custom_call_target="tpu_custom_call" | custom-call | flops 268435456 | bytes 4194304 | tf_op jit(solution)/shard_map/pallas_call | solution.py:351
Async XLA Ops:
  0.6 9.3 %copy-start = (bf16[256,128,128]{2,1,0:T(8,128)(2,1)S(1)}, bf16[256,128,128]{2,1,0:T(8,128)(2,1)}, u32[]{:S(2)}) copy-start(bf16[256,128,128]{2,1,0:T(8,128)(2,1)} %weight_ref.3) | copy-start | bytes 25165828
  1.8 7.3 %collective-permute-start.1 = (f32[2,6656]{1,0:T(2,128)S(1)}, f32[2,6656]{1,0:T(2,128)S(1)}, u32[]{:S(2)}, u32[]{:S(2)}) collective-permute-start(f32[2,6656]{1,0:T(2,128)S(1)} %get-tuple-element.32), channel_id=1, source_target_pairs={{1,2},{3,4},{5,6},{7,8},{9,10},{11,12},{13,14},{15,0},{2,1},{4,3},... | collective-permute-start | bytes 159752 | tf_op jit(solution)/shard_map/ppermute | solution.py:395
  8.7 1.3 %collective-permute-start = (f32[2,6656]{1,0:T(2,128)S(1)}, f32[2,6656]{1,0:T(2,128)S(1)}, u32[]{:S(2)}, u32[]{:S(2)}) collective-permute-start(f32[2,6656]{1,0:T(2,128)S(1)} %get-tuple-element.31), channel_id=1, source_target_pairs={{0,1},{1,0},{2,3},{3,2},{4,5},{5,4},{6,7},{7,6},{8,9},{9,8},{10,11... | collective-permute-start | bytes 159752 | tf_op jit(solution)/shard_map/ppermute | solution.py:434
  27.1 1.2 %collective-permute-start.2 = (f32[28,128]{1,0:T(8,128)S(1)}, f32[28,128]{1,0:T(8,128)S(1)}, u32[]{:S(2)}, u32[]{:S(2)}) collective-permute-start(f32[28,128]{1,0:T(8,128)S(1)} %get-tuple-element.45), channel_id=1, source_target_pairs={{0,1},{1,0},{2,3},{3,2},{4,5},{5,4},{6,7},{7,6},{8,9},{9,8},{10,11... | collective-permute-start | bytes 43016 | tf_op jit(solution)/shard_map/ppermute | solution.py:455

commit v11 on v10

--- a/solution.py
+++ b/solution.py
@@ -10,7 +10,7 @@
 LANE = 128
 EDGE = 32
 CHUNK = 8
-TURNED = 4
+TURNED = 6
 F32 = jnp.float32
 BF16 = jnp.bfloat16
 VMEM = pl.BlockSpec(memory_space=pltpu.VMEM)

time: 43 us -> 42.9 us (level)
  no operation moved by 1% of the time
where the time goes in v11:
time: 42.9 us; the launch traced here: 42.7 us
  blocking collectives  25.6 us (60%)
  Pallas kernels  9.2 us (21%)
  starting transfers between devices  5.65 us (13%)
  waiting for transfers between devices  1.52 us (4%)
  between operations  0.7 us (2%)
    all_to_all x1, blocking collectives, per_device(): lax.all_to_all(outgoing, 'tiles', split_axis=0, concat_axis=0, tiled=True)  14.9 us
    all_to_all x1, blocking collectives, per_device(): lax.all_to_all(returned, 'tiles', split_axis=0, concat_axis=0, tiled=True)  10.7 us
    pallas_call x7, Pallas kernels, placed(): run(*[pltpu.with_memory_space_constraint(x, pltpu.HBM) if spec is HBM els...  9.2 us
    ppermute x1, starting transfers between devices, per_device(): from_odd = lax.ppermute(to_odd, 'tiles', pairs + [(j, i) for i, j in pairs])  5.51 us
  transfers between devices with their start and end apart: 3, of which 3 were waited for; matrix products, arithmetic and copies ran while one was open for 0% of the time, Pallas kernels for 5%

profile of v11, /device:TPU:0, one launch (start us, length us, event | category | flops | bytes accessed | tf_op | source)
XLA Modules:
  0.0 42.7 jit_solution(7574369008099245630)
XLA Ops:
  0.6 0.0 copy-start
  0.6 1.2 %shard_map.130 = (f32[8,3072]{1,0:T(8,128)S(1)}, f32[16,3584]{1,0:T(8,128)S(1)}, f32[2,6656]{1,0:T(2,128)S(1)}) custom-call(s32[1]{0:T(128)} %bitcast.me_ref, f32[8,3072]{1,0:T(8,128)} %atm_hbm.1, f32[16,3584]{1,0:T(8,128)} %ocean_hbm.1), custom_call_target="tpu_custom_call" | custom-call | flops 17179869184 | bytes 268435456 | tf_op jit(solution)/shard_map/pallas_call | solution.py:351
  1.8 5.5 %collective-permute-start.1 = (f32[2,6656]{1,0:T(2,128)S(1)}, f32[2,6656]{1,0:T(2,128)S(1)}, u32[]{:S(2)}, u32[]{:S(2)}) collective-permute-start(f32[2,6656]{1,0:T(2,128)S(1)} %get-tuple-element.32), channel_id=1, source_target_pairs={{1,2},{3,4},{5,6},{7,8},{9,10},{11,12},{13,14},{15,0},{2,1},{4,3},... | collective-permute-start | bytes 159752 | tf_op jit(solution)/shard_map/ppermute | solution.py:395
  7.3 1.3 %shard_map.131 = (bf16[256,192]{1,0:T(8,128)(2,1)S(1)}, s32[2,1,256]{2,1,0:T(1,128)S(1)}, bf16[1024,256]{1,0:T(8,128)(2,1)S(1)}, f32[2,16,128]{2,1,0:T(8,128)S(1...) custom-call(s32[1]{0:T(128)} %bitcast.me_ref, ...), custom_call_target="tpu_custom_call" | custom-call | flops 1048576 | bytes 16384 | tf_op jit(solution)/shard_map/pallas_call | solution.py:351
  8.7 0.1 collective-permute-start
  8.7 0.4 %collective-permute-done.1.odd_ref = f32[2,6656]{1,0:T(2,128)S(1)} collective-permute-done((f32[2,6656]{1,0:T(2,128)S(1)}, f32[2,6656]{1,0:T(2,128)S(1)}, u32[]{:S(2)}, u32[]{:S(2)}) %collective-permute-start.1) | collective-permute-done | bytes 53280 | tf_op jit(solution)/shard_map/ppermute | solution.py:395
  9.2 0.8 %collective-permute-done.even_ref = f32[2,6656]{1,0:T(2,128)S(1)} collective-permute-done((f32[2,6656]{1,0:T(2,128)S(1)}, f32[2,6656]{1,0:T(2,128)S(1)}, u32[]{:S(2)}, u32[]{:S(2)}) %collective-permute-start) | collective-permute-done | bytes 53280 | tf_op jit(solution)/shard_map/ppermute | solution.py:434
  10.0 0.0 copy-done
  10.0 1.9 %shard_map.132 = (f32[8,3072]{1,0:T(8,128)S(1)}, bf16[1024,128]{1,0:T(8,128)(2,1)S(1)}) custom-call(s32[1]{0:T(128)} %bitcast.me_ref, f32[8,3072]{1,0:T(8,128)S(1)} %get-tuple-element.28.atm_ref, f32[1,3072]{1,0:T(1,128)S(1)} %get-tuple-element.30.kappa_ref, f32[2,6656]{1,0:T(2,128)S(1)} %collective-permute-done.even_ref, ...), custom_call_target="tpu_custom_call" | custom-call | flops 268435456 | bytes 4194304 | tf_op jit(solution)/shard_map/pallas_call | solution.py:351
  11.8 14.9 %all_to_all.22 = bf16[16,64,128]{2,1,0:T(8,128)(2,1)S(1)} all-to-all(bf16[16,64,128]{2,1,0:T(8,128)(2,1)S(1)} %bitcast.13), channel_id=1, replica_groups=mesh['members'=2,'tiles'=16] {'tiles'}, dimensions={0} | all-to-all | bytes 524288 | tf_op jit(solution)/shard_map/all_to_all | solution.py:442
  26.7 0.3 shard_map.133
  27.1 0.1 collective-permute-start.2
  27.1 0.9 %shard_map.134 = (f32[448,128]{1,0:T(8,128)S(1)}, bf16[512,448]{1,0:T(8,128)(2,1)S(1)}) custom-call(s32[1]{0:T(128)} %bitcast.me_ref, f32[448,128]{1,0:T(8,128)S(1)} %get-tuple-element.39.drive_ref, f32[32,128]{1,0:T(8,128)S(1)} %get-tuple-element.40.side_ref, s32[4,128]{1,0:T(4,128)S(1)} %get-tuple-element.41.keys_ref, ...), custom_call_target="tpu_custom_call" | custom-call | flops 2147483648 | bytes 33554432 | tf_op jit(solution)/shard_map/pallas_call | solution.py:351
  28.0 0.3 collective-permute-done.2.pair_ref
  28.3 0.3 shard_map.135
  28.6 10.7 %all_to_all.23 = bf16[16,32,128]{2,1,0:T(8,128)(2,1)S(1)} all-to-all(bf16[16,32,128]{2,1,0:T(8,128)(2,1)S(1)} %bitcast.15), channel_id=1, replica_groups=mesh['members'=2,'tiles'=16] {'tiles'}, dimensions={0} | all-to-all | bytes 262144 | tf_op jit(solution)/shard_map/all_to_all | solution.py:469
  39.3 3.3 %shard_map.136 = (f32[8,3072]{1,0:T(8,128)}, f32[16,3584]{1,0:T(8,128)}, f32[8,3072]{1,0:T(8,128)}) custom-call(bf16[512,128]{1,0:T(8,128)(2,1)S(1)} %bitcast.12, s32[2,1,256]{2,1,0:T(1,128)S(1)} %get-tuple-element.47.keys_ref, f32[448,128]{1,0:T(8,128)S(1)} %get-tuple-element.48.cells_ref, f32[8,3072]{1,0:T(8,128)S(1)} %get-tuple-element.49.atm_ref, ...), custom_call_target="tpu_custom_call" | custom-call | flops 268435456 | bytes 4194304 | tf_op jit(solution)/shard_map/pallas_call | solution.py:351
Async XLA Ops:
  0.6 9.3 %copy-start = (bf16[256,128,128]{2,1,0:T(8,128)(2,1)S(1)}, bf16[256,128,128]{2,1,0:T(8,128)(2,1)}, u32[]{:S(2)}) copy-start(bf16[256,128,128]{2,1,0:T(8,128)(2,1)} %weight_ref.3) | copy-start | bytes 25165828
  1.8 7.3 %collective-permute-start.1 = (f32[2,6656]{1,0:T(2,128)S(1)}, f32[2,6656]{1,0:T(2,128)S(1)}, u32[]{:S(2)}, u32[]{:S(2)}) collective-permute-start(f32[2,6656]{1,0:T(2,128)S(1)} %get-tuple-element.32), channel_id=1, source_target_pairs={{1,2},{3,4},{5,6},{7,8},{9,10},{11,12},{13,14},{15,0},{2,1},{4,3},... | collective-permute-start | bytes 159752 | tf_op jit(solution)/shard_map/ppermute | solution.py:395
  8.7 1.3 %collective-permute-start = (f32[2,6656]{1,0:T(2,128)S(1)}, f32[2,6656]{1,0:T(2,128)S(1)}, u32[]{:S(2)}, u32[]{:S(2)}) collective-permute-start(f32[2,6656]{1,0:T(2,128)S(1)} %get-tuple-element.31), channel_id=1, source_target_pairs={{0,1},{1,0},{2,3},{3,2},{4,5},{5,4},{6,7},{7,6},{8,9},{9,8},{10,11... | collective-permute-start | bytes 159752 | tf_op jit(solution)/shard_map/ppermute | solution.py:434
  27.1 1.2 %collective-permute-start.2 = (f32[28,128]{1,0:T(8,128)S(1)}, f32[28,128]{1,0:T(8,128)S(1)}, u32[]{:S(2)}, u32[]{:S(2)}) collective-permute-start(f32[28,128]{1,0:T(8,128)S(1)} %get-tuple-element.45), channel_id=1, source_target_pairs={{0,1},{1,0},{2,3},{3,2},{4,5},{5,4},{6,7},{7,6},{8,9},{9,8},{10,11... | collective-permute-start | bytes 43016 | tf_op jit(solution)/shard_map/ppermute | solution.py:455

commit v12 on v11

--- a/solution.py
+++ b/solution.py
@@ -9,8 +9,8 @@
 
 LANE = 128
 EDGE = 32
-CHUNK = 8
-TURNED = 6
+CHUNK = 16
+TURNED = 12
 F32 = jnp.float32
 BF16 = jnp.bfloat16
 VMEM = pl.BlockSpec(memory_space=pltpu.VMEM)

time: 42.9 us -> 42.9 us (level)
  no operation moved by 1% of the time
where the time goes in v12:
time: 42.9 us; the launch traced here: 42.7 us
  blocking collectives  25.6 us (60%)
  Pallas kernels  9.22 us (21%)
  starting transfers between devices  5.65 us (13%)
  waiting for transfers between devices  1.52 us (4%)
  between operations  0.7 us (2%)
    all_to_all x1, blocking collectives, per_device(): lax.all_to_all(outgoing, 'tiles', split_axis=0, concat_axis=0, tiled=True)  14.9 us
    all_to_all x1, blocking collectives, per_device(): lax.all_to_all(returned, 'tiles', split_axis=0, concat_axis=0, tiled=True)  10.7 us
    pallas_call x7, Pallas kernels, placed(): run(*[pltpu.with_memory_space_constraint(x, pltpu.HBM) if spec is HBM els...  9.22 us
    ppermute x1, starting transfers between devices, per_device(): from_odd = lax.ppermute(to_odd, 'tiles', pairs + [(j, i) for i, j in pairs])  5.51 us
  transfers between devices with their start and end apart: 3, of which 3 were waited for; matrix products, arithmetic and copies ran while one was open for 0% of the time, Pallas kernels for 5%

profile of v12, /device:TPU:0, one launch (start us, length us, event | category | flops | bytes accessed | tf_op | source)
XLA Modules:
  0.0 42.7 jit_solution(7456468079828951598)
XLA Ops:
  0.6 0.0 copy-start
  0.6 1.2 %shard_map.130 = (f32[8,3072]{1,0:T(8,128)S(1)}, f32[16,3584]{1,0:T(8,128)S(1)}, f32[2,6656]{1,0:T(2,128)S(1)}) custom-call(s32[1]{0:T(128)} %bitcast.me_ref, f32[8,3072]{1,0:T(8,128)} %atm_hbm.1, f32[16,3584]{1,0:T(8,128)} %ocean_hbm.1), custom_call_target="tpu_custom_call" | custom-call | flops 17179869184 | bytes 268435456 | tf_op jit(solution)/shard_map/pallas_call | solution.py:351
  1.8 5.5 %collective-permute-start.1 = (f32[2,6656]{1,0:T(2,128)S(1)}, f32[2,6656]{1,0:T(2,128)S(1)}, u32[]{:S(2)}, u32[]{:S(2)}) collective-permute-start(f32[2,6656]{1,0:T(2,128)S(1)} %get-tuple-element.32), channel_id=1, source_target_pairs={{1,2},{3,4},{5,6},{7,8},{9,10},{11,12},{13,14},{15,0},{2,1},{4,3},... | collective-permute-start | bytes 159752 | tf_op jit(solution)/shard_map/ppermute | solution.py:395
  7.3 1.3 %shard_map.131 = (bf16[256,192]{1,0:T(8,128)(2,1)S(1)}, s32[2,1,256]{2,1,0:T(1,128)S(1)}, bf16[1024,256]{1,0:T(8,128)(2,1)S(1)}, f32[2,16,128]{2,1,0:T(8,128)S(1...) custom-call(s32[1]{0:T(128)} %bitcast.me_ref, ...), custom_call_target="tpu_custom_call" | custom-call | flops 1048576 | bytes 16384 | tf_op jit(solution)/shard_map/pallas_call | solution.py:351
  8.7 0.1 collective-permute-start
  8.7 0.4 %collective-permute-done.1.odd_ref = f32[2,6656]{1,0:T(2,128)S(1)} collective-permute-done((f32[2,6656]{1,0:T(2,128)S(1)}, f32[2,6656]{1,0:T(2,128)S(1)}, u32[]{:S(2)}, u32[]{:S(2)}) %collective-permute-start.1) | collective-permute-done | bytes 53280 | tf_op jit(solution)/shard_map/ppermute | solution.py:395
  9.2 0.8 %collective-permute-done.even_ref = f32[2,6656]{1,0:T(2,128)S(1)} collective-permute-done((f32[2,6656]{1,0:T(2,128)S(1)}, f32[2,6656]{1,0:T(2,128)S(1)}, u32[]{:S(2)}, u32[]{:S(2)}) %collective-permute-start) | collective-permute-done | bytes 53280 | tf_op jit(solution)/shard_map/ppermute | solution.py:434
  10.0 0.0 copy-done
  10.0 1.9 %shard_map.132 = (f32[8,3072]{1,0:T(8,128)S(1)}, bf16[1024,128]{1,0:T(8,128)(2,1)S(1)}) custom-call(s32[1]{0:T(128)} %bitcast.me_ref, f32[8,3072]{1,0:T(8,128)S(1)} %get-tuple-element.28.atm_ref, f32[1,3072]{1,0:T(1,128)S(1)} %get-tuple-element.30.kappa_ref, f32[2,6656]{1,0:T(2,128)S(1)} %collective-permute-done.even_ref, ...), custom_call_target="tpu_custom_call" | custom-call | flops 268435456 | bytes 4194304 | tf_op jit(solution)/shard_map/pallas_call | solution.py:351
  11.8 14.9 %all_to_all.22 = bf16[16,64,128]{2,1,0:T(8,128)(2,1)S(1)} all-to-all(bf16[16,64,128]{2,1,0:T(8,128)(2,1)S(1)} %bitcast.13), channel_id=1, replica_groups=mesh['members'=2,'tiles'=16] {'tiles'}, dimensions={0} | all-to-all | bytes 524288 | tf_op jit(solution)/shard_map/all_to_all | solution.py:442
  26.7 0.3 shard_map.133
  27.1 0.1 collective-permute-start.2
  27.1 0.9 %shard_map.134 = (f32[448,128]{1,0:T(8,128)S(1)}, bf16[512,448]{1,0:T(8,128)(2,1)S(1)}) custom-call(s32[1]{0:T(128)} %bitcast.me_ref, f32[448,128]{1,0:T(8,128)S(1)} %get-tuple-element.39.drive_ref, f32[32,128]{1,0:T(8,128)S(1)} %get-tuple-element.40.side_ref, s32[4,128]{1,0:T(4,128)S(1)} %get-tuple-element.41.keys_ref, ...), custom_call_target="tpu_custom_call" | custom-call | flops 2147483648 | bytes 33554432 | tf_op jit(solution)/shard_map/pallas_call | solution.py:351
  28.0 0.3 collective-permute-done.2.pair_ref
  28.3 0.3 shard_map.135
  28.6 10.7 %all_to_all.23 = bf16[16,32,128]{2,1,0:T(8,128)(2,1)S(1)} all-to-all(bf16[16,32,128]{2,1,0:T(8,128)(2,1)S(1)} %bitcast.15), channel_id=1, replica_groups=mesh['members'=2,'tiles'=16] {'tiles'}, dimensions={0} | all-to-all | bytes 262144 | tf_op jit(solution)/shard_map/all_to_all | solution.py:469
  39.4 3.3 %shard_map.136 = (f32[8,3072]{1,0:T(8,128)}, f32[16,3584]{1,0:T(8,128)}, f32[8,3072]{1,0:T(8,128)}) custom-call(bf16[512,128]{1,0:T(8,128)(2,1)S(1)} %bitcast.12, s32[2,1,256]{2,1,0:T(1,128)S(1)} %get-tuple-element.47.keys_ref, f32[448,128]{1,0:T(8,128)S(1)} %get-tuple-element.48.cells_ref, f32[8,3072]{1,0:T(8,128)S(1)} %get-tuple-element.49.atm_ref, ...), custom_call_target="tpu_custom_call" | custom-call | flops 268435456 | bytes 4194304 | tf_op jit(solution)/shard_map/pallas_call | solution.py:351
Async XLA Ops:
  0.6 9.3 %copy-start = (bf16[256,128,128]{2,1,0:T(8,128)(2,1)S(1)}, bf16[256,128,128]{2,1,0:T(8,128)(2,1)}, u32[]{:S(2)}) copy-start(bf16[256,128,128]{2,1,0:T(8,128)(2,1)} %weight_ref.3) | copy-start | bytes 25165828
  1.8 7.3 %collective-permute-start.1 = (f32[2,6656]{1,0:T(2,128)S(1)}, f32[2,6656]{1,0:T(2,128)S(1)}, u32[]{:S(2)}, u32[]{:S(2)}) collective-permute-start(f32[2,6656]{1,0:T(2,128)S(1)} %get-tuple-element.32), channel_id=1, source_target_pairs={{1,2},{3,4},{5,6},{7,8},{9,10},{11,12},{13,14},{15,0},{2,1},{4,3},... | collective-permute-start | bytes 159752 | tf_op jit(solution)/shard_map/ppermute | solution.py:395
  8.7 1.3 %collective-permute-start = (f32[2,6656]{1,0:T(2,128)S(1)}, f32[2,6656]{1,0:T(2,128)S(1)}, u32[]{:S(2)}, u32[]{:S(2)}) collective-permute-start(f32[2,6656]{1,0:T(2,128)S(1)} %get-tuple-element.31), channel_id=1, source_target_pairs={{0,1},{1,0},{2,3},{3,2},{4,5},{5,4},{6,7},{7,6},{8,9},{9,8},{10,11... | collective-permute-start | bytes 159752 | tf_op jit(solution)/shard_map/ppermute | solution.py:434
  27.1 1.2 %collective-permute-start.2 = (f32[28,128]{1,0:T(8,128)S(1)}, f32[28,128]{1,0:T(8,128)S(1)}, u32[]{:S(2)}, u32[]{:S(2)}) collective-permute-start(f32[28,128]{1,0:T(8,128)S(1)} %get-tuple-element.45), channel_id=1, source_target_pairs={{0,1},{1,0},{2,3},{3,2},{4,5},{5,4},{6,7},{7,6},{8,9},{9,8},{10,11... | collective-permute-start | bytes 43016 | tf_op jit(solution)/shard_map/ppermute | solution.py:455
